TPU v7x, 512 devices: a whole 4x8x8 slice. The times are simulated.
512 devices in a mesh: slab: 32 (over x_lo, z, core), plane: 16 (over y, x_hi).
Axes of the slice: x: 4 (x_hi: 2, x_lo: 2; x = x_hi * 2 + x_lo), y: 8, z: 8, core: 2. Of those that a mesh axis runs over, the one named last changes fastest.
Arguments:
- positions: float32 [32, 16, 3, 64], P('slab', 'plane'), as said below
- species: int32 [32, 16, 64], P('slab', 'plane'), may hold values from 0 to 88
- slab_sends: int32 [32, 16, 2, 32], P('slab', 'plane'), may hold values from 0 to 63, as said below
- plane_sends: int32 [32, 16, 2, 64], P('slab', 'plane'), may hold values from 0 to 127, as said below
- edges: int32 [32, 16, 2, 1536], P('slab', 'plane'), may hold values from 0 to 255, as said below
- edge_count: int32 [32, 16], P('slab', 'plane'), may hold values from 384 to 1536, as said below
- embed_table: float32 [89, 128], replicated, may hold values from -6 to 6
- atom_ref: float32 [89], replicated, may hold values from -8 to -1
- radial_one: float32 [2, 8, 64], replicated, may hold values from -2 to 2
- radial_two: float32 [2, 64, 64], replicated, may hold values from -0.75 to 0.75
- radial_three: float32 [2, 64, 64], replicated, may hold values from -0.75 to 0.75
- radial_four: float32 [2, 64, 384], replicated, may hold values from -0.75 to 0.75
- up_weight: float32 [2, 128, 128], replicated, may hold values from -0.5 to 0.5
- skip_weight: float32 [2, 128, 128], replicated, may hold values from -0.5 to 0.5
- out_weight: float32 [2, 128, 128], replicated, may hold values from -0.5 to 0.5
- prod_weight: float32 [2, 4, 128], replicated, may hold values from -4 to 4
- read_one: float32 [128], replicated, may hold values from -0.5 to 0.5
- read_hidden: float32 [128, 16], replicated, may hold values from -0.5 to 0.5
- read_out: float32 [16], replicated, may hold values from -1.5 to 1.5
Outputs:
- atom_energy: float32 [32, 16, 64], P('slab', 'plane')
- forces: float32 [32, 16, 3, 64], P('slab', 'plane')
Inputs may be any that keep to these rules, and one draw needn't show every extreme that they name: `positions`: each domain is a box of 4 x 2 x 2 cells of side 3 in its own frame, with 4 atoms in every cell, and no two atoms closer than 0.9; the owned slots hold the atoms in a random order. `slab_sends`: row 0 lists the owned slots of the atoms in the cells of the highest z layer, row 1 those of the lowest z layer, both in the same order of cells and atoms. `plane_sends`: row 0 lists the atoms of the cells of the highest y layer, row 1 those of the lowest y layer, over the z layers of the owned cells and of the slab ghosts on both sides, as slots of the first 128 extended rows. Senders are extended slots and receivers owned slots. Live edges join atoms of the same or adjacent cells (never across the x ends of a box, never to slab ghost rows that a boundary domain lacks), are grouped by receiver in order of owned slot, with equally many per owned atom in one domain; slots past edge_count hold zeros. `edge_count`: A multiple of 64; the domains of the lowest eighth of the slab (at least one) are full.
All inputs are finite; a program needn't handle non-finite values.
Results may differ from a plain program's by a relative error of at most 0.0003.
Values sent between devices are 32-bit elements; how exact they have to be, the bound alone decides.
No kernel may reach another device: no remote copies, remote signals or barrier semaphores. Data moves between devices by JAX's collectives and lax.ppermute only.
A program may use at most 64 MiB of HBM per device.

v0:
```python
import functools

import jax
import jax.numpy as jnp
from jax import lax
from jax.experimental import pallas as pl
from jax.experimental.pallas import tpu as pltpu
from jax.sharding import PartitionSpec as P

CELLS_Y = 2
CELLS_Z = 2

cutoff_radius = 5.0
cell_side = 3.0
inverse_neighbours = 0.2
highest = lax.Precision.HIGHEST
f32 = jnp.float32
bf16 = jnp.bfloat16

C = 128
OWN = 64
EXT = 256
EDGES = 1536
BLOCKS = 4
GROUP = 16
SPAN = EDGES // BLOCKS
KINDS = 96
LMS = (1, 3, 5)
FIRST_LM = (0, 1, 4)
STACK_AT = (0, 48, 192)
STACK = 432
R3, R5, R15 = 3.0**0.5, 5.0**0.5, 15.0**0.5

NN = (((1,), (0,)), ((), ()))
TN = (((0,), (0,)), ((), ()))
NT = (((1,), (1,)), ((), ()))


def dot(a, b, dims=NN):
    return lax.dot_general(a, b, dims, preferred_element_type=f32)


def dot3(a, b, dims=NN):
    return lax.dot_general(a, b, dims, precision=lax.Precision.HIGH, preferred_element_type=f32)


def split(x):
    hi = x.astype(bf16)
    return hi, (x - hi.astype(f32)).astype(bf16)


def pair_lanes(x):
    hi, lo = split(x)
    return jnp.concatenate([hi, lo], axis=1)


def halves(o):
    return o[:, :C] + o[:, C:]


def stack_rows(x):
    hi, lo = split(x)
    return jnp.concatenate([hi, lo, hi], axis=0)


def three(x):
    hi = x.astype(bf16).astype(f32)
    rest = x - hi
    mid = rest.astype(bf16).astype(f32)
    return hi, mid, rest - mid


def pick_lanes(values, chooser, dims=NN):
    hi, mid, lo = three(values)
    o = dot(jnp.concatenate([hi, mid, lo, jnp.zeros_like(lo)], axis=0).astype(bf16), chooser, dims)
    return (o[0:8] + o[8:16]) + o[16:24]


def pick_rows(chooser, values):
    hi, mid, lo = three(values)
    o = dot(chooser, jnp.concatenate([hi, mid, lo], axis=1).astype(bf16))
    return (o[:, :C] + o[:, C : 2 * C]) + o[:, 2 * C :]


def silu(x):
    return x * (1.0 / (1.0 + jnp.exp(-x)))


def silu_pair(x):
    s = 1.0 / (1.0 + jnp.exp(-x))
    return x * s, s * (1.0 + x * (1.0 - s))


def span(b):
    return pl.ds(b * SPAN, SPAN)


def call(kernel, outs, args, scratch=(), flops=0, name=None):
    spec = pl.BlockSpec(memory_space=pltpu.VMEM)
    out_shape = tuple(jax.ShapeDtypeStruct(shape, dtype) for shape, dtype in outs)
    moved = sum(a.size * a.dtype.itemsize for a in args)
    return pl.pallas_call(
        kernel,
        out_shape=out_shape,
        in_specs=[spec] * len(args),
        out_specs=tuple(spec for _ in out_shape),
        scratch_shapes=list(scratch),
        compiler_params=pltpu.CompilerParams(vmem_limit_bytes=56 * 1024 * 1024),
        cost_estimate=pl.CostEstimate(flops=flops, bytes_accessed=moved, transcendentals=0),
        name=name,
    )(*args)


def pick_kernel(v_ref, s_ref, a_ref, b_ref):
    o = pick_lanes(v_ref[...], s_ref[...])
    half = a_ref.shape[1]
    a_ref[...] = o[:, :half]
    b_ref[...] = o[:, half:]


def geometry(v, valid, b_ref, db_ref, geo_ref):
    vx = jnp.where(valid, v[0:1], 2.0 * cutoff_radius)
    vy = jnp.where(valid, v[1:2], 0.0)
    vz = jnp.where(valid, v[2:3], 0.0)
    d = jnp.sqrt(vx * vx + vy * vy + vz * vz)
    inv = 1.0 / d
    geo_ref[0:1, :] = vx * inv
    geo_ref[1:2, :] = vy * inv
    geo_ref[2:3, :] = vz * inv
    geo_ref[3:4, :] = inv
    s = d / cutoff_radius
    s2 = s * s
    s4 = s2 * s2
    s5 = s4 * s
    s6 = s4 * s2
    s7 = s6 * s
    inside = (s < 1.0) & valid
    u = 1.0 - 28.0 * s6 + 48.0 * s7 - 21.0 * s4 * s4
    du = (-168.0 * s5 + 336.0 * s6 - 168.0 * s7) / cutoff_radius
    geo_ref[4:5, :] = jnp.where(inside, u * inverse_neighbours, 0.0)
    geo_ref[5:6, :] = jnp.where(inside, du * inverse_neighbours, 0.0)
    geo_ref[6:8, :] = jnp.zeros_like(geo_ref[6:8, :])
    t = (jnp.minimum(s, 1.0) - 0.5) * jnp.pi
    z = t * t
    cs = 1.0 - z * (1 / 2 - z * (1 / 24 - z * (1 / 720 - z * (1 / 40320 - z * (1 / 3628800 - z * (1 / 479001600 - z * (1 / 87178291200)))))))
    sn = 1.0 - z * (1 / 6 - z * (1 / 120 - z * (1 / 5040 - z * (1 / 362880 - z * (1 / 39916800 - z * (1 / 6227020800))))))
    s1, c1 = cs, -t * sn

    def plus(a, b):
        return a[0] * b[1] + a[1] * b[0], a[1] * b[1] - a[0] * b[0]

    w1 = (s1, c1)
    w2 = plus(w1, w1)
    w3 = plus(w2, w1)
    w4 = plus(w2, w2)
    waves = (w1, w2, w3, w4, plus(w4, w1), plus(w4, w2), plus(w4, w3), plus(w4, w4))
    gain = (2.0 / cutoff_radius) ** 0.5 * inv
    for n, (sine, cosine) in enumerate(waves):
        b_ref[n : n + 1, :] = gain * sine
        db_ref[n : n + 1, :] = gain * (cosine * ((n + 1) * jnp.pi / cutoff_radius) - sine * inv)


def basis_stack(x):
    hi, mid, _ = three(x)
    lo = x - hi
    return jnp.concatenate([hi, lo, hi, jnp.zeros_like(hi)], axis=0).astype(bf16)


def radial_block(b, w1, w2, w3, w4, gate):
    h = silu(dot(w1, basis_stack(b)))
    h = silu(dot(w2, stack_rows(h)))
    h = silu(dot(w3, stack_rows(h)))
    return dot(stack_rows(h * gate), w4, TN)


def radial_tangent_block(b, db, w1, w2, w3, w4, gate, dgate):
    h, g = silu_pair(dot(w1, basis_stack(b)))
    t = g * dot(w1, basis_stack(db))
    h, g = silu_pair(dot(w2, stack_rows(h)))
    t = g * dot(w2, stack_rows(t))
    h, g = silu_pair(dot(w3, stack_rows(h)))
    t = g * dot(w3, stack_rows(t))
    return dot(stack_rows(t * gate + h * dgate), w4, TN)


def angular_rows(geo):
    x, y, z = geo[0:1], geo[1:2], geo[2:3]
    return (
        jnp.ones_like(x),
        R3 * x,
        R3 * y,
        R3 * z,
        R15 * x * y,
        R15 * y * z,
        0.5 * R5 * (3.0 * z * z - 1.0),
        R15 * x * z,
        0.5 * R15 * (x * x - y * y),
    )


def gather_messages(b, g_ref, lifted, radial, ast_ref, l_ref, m_ref, amp_ref):
    lift = halves(dot(g_ref[span(b), :], lifted))
    l_ref[span(b), :] = lift
    for l in range(3):
        n = LMS[l]
        m = pair_lanes(radial[:, l * C : (l + 1) * C] * lift)
        m_ref[l, span(b), :] = m
        o = dot(ast_ref[pl.ds(b * STACK + STACK_AT[l], 32 * n), :], m)
        amp = halves(o[: 16 * n]) + o[16 * n :, :C]
        for k in range(n):
            amp_ref[FIRST_LM[l] + k, pl.ds(b * GROUP, GROUP), :] = amp[16 * k : 16 * (k + 1)]


def invariants(amp_ref, gain):
    b0 = amp_ref[0]
    b1 = sum(amp_ref[k] * amp_ref[k] for k in range(1, 4))
    b2 = sum(amp_ref[k] * amp_ref[k] for k in range(4, 9))
    return gain[0:1] * b0 + gain[1:2] * b1 + gain[2:3] * b2 + gain[3:4] * b0 * b0


def amp_grads(amp_ref, gain, gm, ga_ref):
    ga_ref[0] = gm * (gain[0:1] + 2.0 * gain[3:4] * amp_ref[0])
    one = gm * (2.0 * gain[1:2])
    two = gm * (2.0 * gain[2:3])
    for k in range(1, 4):
        ga_ref[k] = one * amp_ref[k]
    for k in range(4, 9):
        ga_ref[k] = two * amp_ref[k]


def group_grads(ga_ref, b, l):
    return jnp.concatenate(
        [ga_ref[FIRST_LM[l] + k, pl.ds(b * GROUP, GROUP), :] for k in range(LMS[l])], axis=0
    )


def spread(ast_ref, ga_ref, b, l):
    n = LMS[l]
    hi, lo = split(group_grads(ga_ref, b, l))
    return dot(
        ast_ref[pl.ds(b * STACK + STACK_AT[l], 48 * n), :], jnp.concatenate([hi, hi, lo], axis=0), TN
    )


def edge_forces(b, x, m_ref, ga_ref, geo, mask, gv_ref):
    gd = dot(jnp.ones((16, 2 * C), bf16), pair_lanes(x), NT)[0:1]
    gy = [None]
    for l in (1, 2):
        n = LMS[l]
        hi, lo = split(group_grads(ga_ref, b, l))
        left = jnp.concatenate(
            [jnp.concatenate([hi, hi], axis=1), jnp.concatenate([lo, jnp.zeros_like(lo)], axis=1)],
            axis=0,
        )
        w = dot(left, m_ref[l, span(b), :], NT)
        w = w[: 16 * n] + w[16 * n :]
        for k in range(n):
            gy.append(jnp.sum(mask * w[16 * k : 16 * (k + 1)], axis=0, keepdims=True))
    x, y, z, inv = geo[0:1], geo[1:2], geo[2:3], geo[3:4]
    gx = R3 * gy[1] + R15 * (y * gy[4] + z * gy[7] + x * gy[8])
    gyy = R3 * gy[2] + R15 * (x * gy[4] + z * gy[5] - y * gy[8])
    gz = R3 * gy[3] + R15 * (y * gy[5] + x * gy[7]) + (3.0 * R5) * z * gy[6]
    along = x * gx + y * gyy + z * gz
    core = gd - along * inv
    gv_ref[0:1, span(b)] = core * x + gx * inv
    gv_ref[1:2, span(b)] = core * y + gyy * inv
    gv_ref[2:3, span(b)] = core * z + gz * inv
    gv_ref[3:8, span(b)] = jnp.zeros((5, SPAN), f32)


def first_kernel(
    vext_ref, dd_ref, g_ref, mask_ref, table_ref, skip_ref, w1_ref, w2_ref, w3_ref, w4_ref,
    gain_ref, out_ref, sn_ref,
    f_ref, sl_ref, si_ref, amp_ref, l_ref, m_ref, ast_ref, b_ref, db_ref, geo_ref,
):
    valid = jnp.sum(mask_ref[...], axis=0, keepdims=True) > 0.5
    geometry(pick_lanes(vext_ref[...], dd_ref[...]), valid, b_ref, db_ref, geo_ref)
    kinds = vext_ref[3:4, :]
    onehot = (
        lax.broadcasted_iota(jnp.int32, (KINDS, EXT), 0).astype(f32) == kinds
    ).astype(f32).astype(bf16)
    lifted = dot(onehot, table_ref[...], TN).astype(bf16)
    w1, w2, w3, w4 = w1_ref[...], w2_ref[...], w3_ref[...], w4_ref[...]
    for b in range(BLOCKS):
        geo = geo_ref[:, span(b)]
        mask = mask_ref[:, span(b)]
        rows = angular_rows(geo)
        for l in range(3):
            a = jnp.concatenate(
                [mask * rows[FIRST_LM[l] + k] for k in range(LMS[l])], axis=0
            )
            ast_ref[pl.ds(b * STACK + STACK_AT[l], 48 * LMS[l]), :] = stack_rows(a)
        radial = radial_block(b_ref[:, span(b)], w1, w2, w3, w4, geo[4:5])
        gather_messages(b, g_ref, lifted, radial, ast_ref, l_ref, m_ref, amp_ref)
    o = dot(onehot, skip_ref[...], TN)[:OWN]
    skipped = (o[:, :C] + o[:, C : 2 * C]) + o[:, 2 * C :]
    first = skipped + dot3(invariants(amp_ref, gain_ref[...]), out_ref[...])
    f_ref[...] = first
    sends = pick_rows(sn_ref[...], first)
    sl_ref[...] = sends[:32]
    si_ref[...] = sends[32:]


def middle_kernel(f_ref, rl_ref, ri_ref, pn_ref, a_ref, b_ref):
    o = pick_rows(pn_ref[...], jnp.concatenate([f_ref[...], rl_ref[...], ri_ref[...]], axis=0))
    a_ref[...] = o[:64]
    b_ref[...] = o[64:]


def radial_kernel(b_ref, geo_ref, w1_ref, w2_ref, w3_ref, w4_ref, r_ref):
    w1, w2, w3, w4 = w1_ref[...], w2_ref[...], w3_ref[...], w4_ref[...]
    for b in range(BLOCKS):
        r_ref[span(b), :] = radial_block(b_ref[:, span(b)], w1, w2, w3, w4, geo_ref[4:5, span(b)])


def tangent_kernel(b_ref, db_ref, geo_ref, w1_ref, w2_ref, w3_ref, w4_ref, r_ref):
    w1, w2, w3, w4 = w1_ref[...], w2_ref[...], w3_ref[...], w4_ref[...]
    for b in range(BLOCKS):
        r_ref[span(b), :] = radial_tangent_block(
            b_ref[:, span(b)], db_ref[:, span(b)], w1, w2, w3, w4, geo_ref[4:5, span(b)], geo_ref[5:6, span(b)]
        )


def second_kernel(
    f_ref, rl_ref, ri_ref, pl_ref, ps_ref, g_ref, gt_ref, ast_ref, r_ref, up_ref, skip_ref, out_ref, gain_ref,
    kinds_ref, ref_ref, one_ref, hid_ref, ro_ref,
    e_ref, gmid_ref, gl_ref, gs_ref, z_ref, l_ref, m_ref, ga_ref,
    amp_ref, glift_ref,
):
    first = f_ref[...]
    ext = jnp.concatenate([first, rl_ref[...], ri_ref[...], pl_ref[...], ps_ref[...]], axis=0)
    lifted = pair_lanes(dot3(ext, up_ref[...]))
    for b in range(BLOCKS):
        gather_messages(b, g_ref, lifted, r_ref[span(b), :], ast_ref, l_ref, m_ref, amp_ref)
    gain = gain_ref[...]
    second = dot3(first, skip_ref[...]) + dot3(invariants(amp_ref, gain), out_ref[...])
    hidden = lax.dot_general(hid_ref[...], second, NT, precision=highest, preferred_element_type=f32)
    act, slope = silu_pair(hidden)
    ro = ro_ref[...]
    grad_second = dot3(slope * ro, hid_ref[...], TN)
    gm = dot3(grad_second, out_ref[...], NT)
    amp_grads(amp_ref, gain, gm, ga_ref)
    for b in range(BLOCKS):
        grad = None
        for l in range(3):
            z = spread(ast_ref, ga_ref, b, l)
            z_ref[span(b), l * C : (l + 1) * C] = z
            term = r_ref[span(b), l * C : (l + 1) * C] * z
            grad = term if grad is None else grad + term
        glift_ref[span(b), :] = pair_lanes(grad)
    glift = halves(dot(gt_ref[...], glift_ref[...]))
    gext = dot3(glift, up_ref[...], NT)
    gl_ref[...] = gext[128:192]
    gs_ref[...] = gext[192:256]
    gmid_ref[64:128, :] = gext[64:128]
    gmid_ref[0:64, :] = gext[0:64] + dot3(grad_second, skip_ref[...], NT) + one_ref[0:1]
    onehot = (lax.broadcasted_iota(jnp.int32, (KINDS, OWN), 0).astype(f32) == kinds_ref[3:4, :]).astype(f32)
    energy = lax.dot_general(ref_ref[...], onehot, NN, precision=highest, preferred_element_type=f32)
    energy = energy + lax.dot_general(one_ref[...], first, NT, precision=highest, preferred_element_type=f32)
    e_ref[...] = energy + jnp.sum(act * ro, axis=0, keepdims=True)


def early_kernel(z_ref, dr_ref, l_ref, m_ref, ga_ref, geo_ref, mask_ref, dd_ref, gp_ref, gv_ref):
    for b in range(BLOCKS):
        x = sum(
            z_ref[span(b), l * C : (l + 1) * C] * dr_ref[span(b), l * C : (l + 1) * C] for l in range(3)
        )
        edge_forces(b, x * l_ref[span(b), :], m_ref, ga_ref, geo_ref[:, span(b)], mask_ref[:, span(b)], gv_ref)
    gp_ref[...] = pick_lanes(gv_ref[...], dd_ref[...], NT)


def back_middle_kernel(gmid_ref, al_ref, as_ref, pt_ref, own_ref, l_ref, i_ref):
    mid = gmid_ref[...] + pick_rows(pt_ref[...], jnp.concatenate([al_ref[...], as_ref[...]], axis=0))
    own_ref[...] = mid[:64]
    l_ref[...] = mid[64:96]
    i_ref[...] = mid[96:128]


def late_kernel(
    own_ref, rl_ref, ri_ref, st_ref, out_ref, gain_ref, amp_ref, ast_ref, dr_ref, l_ref, m_ref, geo_ref,
    mask_ref, dd_ref, early_ref, gp_ref, ga_ref, gv_ref,
):
    grad = own_ref[...] + pick_rows(st_ref[...], jnp.concatenate([rl_ref[...], ri_ref[...]], axis=0))
    amp_grads(amp_ref, gain_ref[...], dot3(grad, out_ref[...], NT), ga_ref)
    for b in range(BLOCKS):
        x = None
        for l in range(3):
            term = spread(ast_ref, ga_ref, b, l) * dr_ref[span(b), l * C : (l + 1) * C]
            x = term if x is None else x + term
        edge_forces(b, x * l_ref[span(b), :], m_ref, ga_ref, geo_ref[:, span(b)], mask_ref[:, span(b)], gv_ref)
    gp_ref[...] = early_ref[...] + pick_lanes(gv_ref[...], dd_ref[...], NT)


def collect_kernel(v_ref, r_ref, s_ref, o_ref, *, sign):
    o_ref[...] = sign * (v_ref[...] + pick_lanes(r_ref[...], s_ref[...]))


def swap_slab_far(value):
    count = lax.axis_size("slab")
    pairs = [(i, i + 1) for i in range(1, count - 1, 2)]
    return lax.ppermute(value, "slab", pairs + [(b, a) for a, b in pairs])


def swap_slab_near(value):
    count = lax.axis_size("slab")
    return lax.ppermute(value, "slab", [(i, i ^ 1) for i in range(count)])


def swap_plane_far(value):
    count = lax.axis_size("plane")
    pairs = [(i, (i + 1) % count) for i in range(1, count, 2)]
    return lax.ppermute(value, "plane", pairs + [(b, a) for a, b in pairs])


def swap_plane_near(value):
    count = lax.axis_size("plane")
    return lax.ppermute(value, "plane", [(i, i ^ 1) for i in range(count)])


def both(swap_far, swap_near, far, near):
    far_in = swap_far(far)
    near, far_held = lax.optimization_barrier((near, far))
    return far_in, swap_near(near)


def high_low(x):
    hi = lax.reduce_precision(x, 8, 7)
    return hi.astype(bf16), (x - hi).astype(bf16)


def high_mid_low(x):
    hi = lax.reduce_precision(x, 8, 7)
    mid = lax.reduce_precision(x - hi, 8, 7)
    return hi.astype(bf16), mid.astype(bf16), (x - hi - mid).astype(bf16)


def weights_of(one, two, three_, four):
    hi, lo = high_low(jnp.transpose(one))
    w1 = jnp.concatenate([hi, hi, lo, jnp.zeros_like(lo)], axis=1)

    def inner(w):
        hi, lo = high_low(jnp.transpose(w))
        return jnp.concatenate([hi, hi, lo], axis=1)

    hi, lo = high_low(four)
    return w1, inner(two), inner(three_), jnp.concatenate([hi, hi, lo], axis=0)


def body(
    positions,
    species,
    slab_sends,
    plane_sends,
    edges,
    edge_count,
    embed_table,
    atom_ref,
    radial_one,
    radial_two,
    radial_three,
    radial_four,
    up_weight,
    skip_weight,
    out_weight,
    prod_weight,
    read_one,
    read_hidden,
    read_out,
):
    slab_odd = lax.axis_index("slab") % 2 == 1
    plane_odd = lax.axis_index("plane") % 2 == 1
    slab_list = slab_sends[0, 0]
    slab_list = jnp.where(slab_odd, slab_list, slab_list[::-1]).reshape(-1)

    def moved_slab(slot):
        return jnp.where(slab_odd & (slot >= 64) & (slot < 128), slot ^ 32, slot)

    plane_list = plane_sends[0, 0]
    plane_list = moved_slab(jnp.where(plane_odd, plane_list, plane_list[::-1])).reshape(-1)
    slab_t = (jnp.arange(64)[:, None] == slab_list[None, :]).astype(bf16)
    slab_n = (slab_list[:, None] == jnp.arange(64)[None, :]).astype(bf16)
    plane_t = (jnp.arange(128)[:, None] == plane_list[None, :]).astype(bf16)
    plane_n = (plane_list[:, None] == jnp.arange(128)[None, :]).astype(bf16)

    values = jnp.concatenate(
        [positions[0, 0], species[0, 0].astype(f32)[None, :], jnp.zeros((4, OWN), f32)], axis=0
    )
    slab_step = jnp.where(slab_odd, 1.0, -1.0) * (CELLS_Z * cell_side)
    plane_step = jnp.where(plane_odd, 1.0, -1.0) * (CELLS_Y * cell_side)
    z_row = (jnp.arange(8) == 2).astype(f32)[:, None] * slab_step
    y_row = (jnp.arange(8) == 1).astype(f32)[:, None] * plane_step

    with jax.named_scope("atoms_slab"):
        far, near = call(pick_kernel, [((8, 32), f32)] * 2, (values, slab_t), name="pick_slab")
        far, near = both(swap_slab_far, swap_slab_near, far, near)
        values_mid = jnp.concatenate([values, far + z_row, near - z_row], axis=1)
    with jax.named_scope("atoms_plane"):
        far, near = call(pick_kernel, [((8, 64), f32)] * 2, (values_mid, plane_t), name="pick_plane")
        far, near = both(swap_plane_far, swap_plane_near, far, near)
        values_ext = jnp.concatenate([values_mid, far + y_row, near - y_row], axis=1)

    with jax.named_scope("edge_lists"):
        per_atom = edge_count[0, 0] // OWN
        padded = jnp.concatenate([edges[0, 0, 0], jnp.zeros((SPAN,), jnp.int32)])
        senders = jnp.stack(
            [lax.dynamic_slice_in_dim(padded, b * GROUP * per_atom, SPAN) for b in range(BLOCKS)]
        )
        place = jnp.arange(SPAN)
        senders = jnp.where(place[None, :] < GROUP * per_atom, senders, -1).reshape(-1)
        senders = moved_slab(senders)
        senders = jnp.where(plane_odd & (senders >= 128), senders ^ 64, senders)
        place = jnp.tile(place, BLOCKS)[None, :]
        inside = jnp.arange(GROUP)[:, None]
        mask = (place >= inside * per_atom) & (place < (inside + 1) * per_atom)
        sender_t = jnp.arange(EXT)[:, None] == senders[None, :]
        sender_n = (senders[:, None] == jnp.arange(EXT)[None, :]).astype(bf16)
        block_of = jnp.arange(EDGES) // SPAN
        atom = jnp.arange(EXT)[:, None] - GROUP * block_of[None, :]
        received = (atom >= 0) & (atom < GROUP) & (place >= atom * per_atom) & (place < (atom + 1) * per_atom)
        edge_t = sender_t.astype(bf16) - received.astype(bf16)
        sender_t = sender_t.astype(bf16)
        mask = mask.astype(f32)

    with jax.named_scope("weights"):
        weights = [
            weights_of(radial_one[t], radial_two[t], radial_three[t], radial_four[t]) for t in range(2)
        ]
        tables = jnp.dot(
            jnp.pad(embed_table, ((0, KINDS - embed_table.shape[0]), (0, 0))),
            jnp.concatenate([up_weight[0], skip_weight[0]], axis=1),
            precision=highest,
            preferred_element_type=f32,
        )
        table = jnp.concatenate(high_low(tables[:, :C]), axis=1)
        skip_table = jnp.concatenate(high_mid_low(tables[:, C:]), axis=1)
        gains = jnp.pad(prod_weight, ((0, 0), (0, 4), (0, 0)))
        ref_row = jnp.broadcast_to(jnp.pad(atom_ref, (0, KINDS - atom_ref.shape[0]))[None, :], (8, KINDS))
        one_row = jnp.broadcast_to(read_one[None, :], (8, C))
        hid = jnp.transpose(read_hidden)
        ro = jnp.broadcast_to(read_out[:, None], (read_out.shape[0], OWN))

    edge_mat = ((EDGES, C), f32)
    message_mat = ((3, EDGES, 2 * C), bf16)
    by_degree = ((EDGES, 3 * C), f32)
    rows = (((8, EDGES), f32),) * 3
    amp_mat = ((9, OWN, C), f32)
    slab_rows = ((32, C), f32)
    plane_rows = ((64, C), f32)
    with jax.named_scope("first_layer"):
        (first, far, near, amp_first, lift_first, message_first, angular, basis, basis_slope, geo) = call(
            first_kernel,
            [plane_rows, slab_rows, slab_rows, amp_mat, edge_mat, message_mat,
             ((BLOCKS * STACK, SPAN), bf16), *rows],
            (values_ext, edge_t, sender_n, mask, table, skip_table, *weights[0], gains[0], out_weight[0], slab_n),
            name="first_layer",
        )
    with jax.named_scope("features_slab"):
        far, near = both(swap_slab_far, swap_slab_near, far, near)
        slab_far, slab_near = far, near
    radial_second, = call(
        radial_kernel, [by_degree], (basis, geo, *weights[1]), flops=1_000_000_000, name="radial_second"
    )
    with jax.named_scope("features_plane"):
        far, near = call(
            middle_kernel, [plane_rows] * 2, (first, slab_far, slab_near, plane_n), name="middle"
        )
        far, near = both(swap_plane_far, swap_plane_near, far, near)
    slope_second, = call(
        tangent_kernel, [by_degree], (basis, basis_slope, geo, *weights[1]), flops=2_000_000_000, name="slope_second"
    )
    slope_first, = call(
        tangent_kernel, [by_degree], (basis, basis_slope, geo, *weights[0]), flops=2_000_000_000, name="slope_first"
    )
    with jax.named_scope("second_layer"):
        energies, gmid, far, near, z, lift_second, message_second, ga = call(
            second_kernel,
            [((8, OWN), f32), ((128, C), f32), plane_rows, plane_rows, by_degree, edge_mat, message_mat, amp_mat],
            (first, slab_far, slab_near, far, near, sender_n, sender_t, angular, radial_second,
             up_weight[1], skip_weight[1], out_weight[1], gains[1], values, ref_row, one_row, hid, ro),
            scratch=[pltpu.VMEM((9, OWN, C), f32), pltpu.VMEM((EDGES, 2 * C), bf16)],
            name="second_layer",
        )
    with jax.named_scope("feature_grads_plane"):
        far, near = both(swap_plane_far, swap_plane_near, far, near)
    early, = call(
        early_kernel,
        [((8, EXT), f32)],
        (z, slope_second, lift_second, message_second, ga, geo, mask, edge_t),
        scratch=[pltpu.VMEM((8, EDGES), f32)],
        flops=1_000_000_000,
        name="early_forces",
    )
    with jax.named_scope("feature_grads_slab"):
        own, far, near = call(
            back_middle_kernel, [plane_rows, slab_rows, slab_rows], (gmid, far, near, plane_t), name="back_middle"
        )
        far, near = both(swap_slab_far, swap_slab_near, far, near)
    with jax.named_scope("late_forces"):
        grads, = call(
            late_kernel,
            [((8, EXT), f32)],
            (own, far, near, slab_t, out_weight[0], gains[0], amp_first, angular, slope_first, lift_first,
             message_first, geo, mask, edge_t, early),
            scratch=[pltpu.VMEM((9, OWN, C), f32), pltpu.VMEM((8, EDGES), f32)],
            name="late_forces",
        )
    with jax.named_scope("position_grads_plane"):
        far, near = both(swap_plane_far, swap_plane_near, grads[:, 128:192], grads[:, 192:256])
        mid, = call(
            functools.partial(collect_kernel, sign=1.0),
            [((8, 128), f32)],
            (grads[:, :128], jnp.concatenate([far, near], axis=1), plane_n),
            name="collect_plane",
        )
    with jax.named_scope("position_grads_slab"):
        far, near = both(swap_slab_far, swap_slab_near, mid[:, 64:96], mid[:, 96:128])
        total, = call(
            functools.partial(collect_kernel, sign=-1.0),
            [((8, OWN), f32)],
            (mid[:, :64], jnp.concatenate([far, near], axis=1), slab_n),
            name="collect_slab",
        )
    return (energies[None, None, 0, :], total[None, None, :3, :])


def solution(mesh):
    in_specs = (
        P("slab", "plane", None, None),
        P("slab", "plane", None),
        P("slab", "plane", None, None),
        P("slab", "plane", None, None),
        P("slab", "plane", None, None),
        P("slab", "plane"),
    ) + (P(),) * 13
    out_specs = (P("slab", "plane", None), P("slab", "plane", None, None))
    return jax.shard_map(body, mesh=mesh, in_specs=in_specs, out_specs=out_specs, check_vma=False)
```

profile of v0, /device:TPU:2, one launch (start us, length us, event | category | flops | bytes accessed | tf_op | source)
XLA Modules:
  0.0 156.2 jit_solution(13628160582268037454)
XLA Ops:
  4.9 1.5 pick_slab.1
  6.4 10.3 %collective-permute-start = (f32[8,32]{1,0:T(8,128)}, f32[8,32]{1,0:T(8,128)S(1)}, u32[]{:S(2)}, u32[]{:S(2)}) collective-permute-start(f32[8,32]{1,0:T(8,128)} %get-tuple-element.37), channel_id=1, source_target_pairs={{16,32},{48,64},{80,96},{112,128},{144,160},{176,192},{208,224},{2... | collective-permute-start | bytes 3080 | tf_op jit(solution)/shard_map/atoms_slab/ppermute | solution.py:401
  16.7 1.9 %collective-permute-start.1 = (f32[8,32]{1,0:T(8,128)}, f32[8,32]{1,0:T(8,128)S(1)}, u32[]{:S(2)}, u32[]{:S(2)}) collective-permute-start(f32[8,32]{1,0:T(8,128)} %get-tuple-element.39), channel_id=1, source_target_pairs={{0,16},{16,0},{32,48},{48,32},{64,80},{80,64},{96,112},{112,96},{1... | collective-permute-start | bytes 3080 | tf_op jit(solution)/shard_map/atoms_slab/ppermute | solution.py:406
  27.0 1.8 %fusion.8.dd_ref = bf16[256,1536]{1,0:T(8,128)(2,1)} fusion(s32[]{:T(128)S(6)} %select_n.111, s32[1536]{0:T(1024)S(1)} %ge.73, s32[1536]{0:T(1024)S(1)} %fusion.28, s32[1536]{0:T(1024)S(1)} %xor_select_fusion), kind=kLoop, calls=%fused_computation.13 | loop fusion | flops 7077888 | bytes 804868 | tf_op jit(solution)/shard_map/edge_lists/sub | solution.py:520
  35.1 1.6 pick_plane.1
  36.6 7.2 %collective-permute-start.2 = (f32[8,64]{1,0:T(8,128)}, f32[8,64]{1,0:T(8,128)S(1)}, u32[]{:S(2)}, u32[]{:S(2)}) collective-permute-start(f32[8,64]{1,0:T(8,128)} %get-tuple-element.40), channel_id=1, source_target_pairs={{1,2},{3,4},{5,6},{7,8},{9,10},{11,12},{13,14},{15,0},{2,1},{4,3},... | collective-permute-start | bytes 6152 | tf_op jit(solution)/shard_map/atoms_plane/ppermute | solution.py:412
  43.8 1.9 %collective-permute-start.3 = (f32[8,64]{1,0:T(8,128)}, f32[8,64]{1,0:T(8,128)S(1)}, u32[]{:S(2)}, u32[]{:S(2)}) collective-permute-start(f32[8,64]{1,0:T(8,128)} %get-tuple-element.42), channel_id=1, source_target_pairs={{0,1},{1,0},{2,3},{3,2},{4,5},{5,4},{6,7},{7,6},{8,9},{9,8},{10,11... | collective-permute-start | bytes 6152 | tf_op jit(solution)/shard_map/atoms_plane/ppermute | solution.py:417
  45.8 5.3 %collective-permute-done.3 = f32[8,64]{1,0:T(8,128)S(1)} collective-permute-done((f32[8,64]{1,0:T(8,128)}, f32[8,64]{1,0:T(8,128)S(1)}, u32[]{:S(2)}, u32[]{:S(2)}) %collective-permute-start.3) | collective-permute-done | bytes 2080 | tf_op jit(solution)/shard_map/atoms_plane/ppermute | solution.py:417
  51.8 8.1 %first_layer.1 = (f32[64,128]{1,0:T(8,128)}, f32[32,128]{1,0:T(8,128)}, f32[32,128]{1,0:T(8,128)}, f32[9,64,128]{2,1,0:T(8,128)}, f32[1536,128]{1,0:T(8,128)}, /...) custom-call(f32[8,256]{1,0:T(8,128)} %concatenate.54.vext_ref, ...), custom_call_target="tpu_custom_call" | custom-call | bytes 2080768 | tf_op jit(solution)/shard_map/first_layer/first_layer/pallas_call | solution.py:102
  59.9 1.9 %collective-permute-start.4 = (f32[32,128]{1,0:T(8,128)}, f32[32,128]{1,0:T(8,128)S(1)}, u32[]{:S(2)}, u32[]{:S(2)}) collective-permute-start(f32[32,128]{1,0:T(8,128)} %get-tuple-element.44), channel_id=1, source_target_pairs={{16,32},{48,64},{80,96},{112,128},{144,160},{176,192},{208,224},{2... | collective-permute-start | bytes 49160 | tf_op jit(solution)/shard_map/features_slab/ppermute | solution.py:401
  61.8 1.9 %collective-permute-start.5 = (f32[32,128]{1,0:T(8,128)}, f32[32,128]{1,0:T(8,128)S(1)}, u32[]{:S(2)}, u32[]{:S(2)}) collective-permute-start(f32[32,128]{1,0:T(8,128)} %get-tuple-element.46), channel_id=1, source_target_pairs={{0,16},{16,0},{32,48},{48,32},{64,80},{80,64},{96,112},{112,96},{1... | collective-permute-start | bytes 49160 | tf_op jit(solution)/shard_map/features_slab/ppermute | solution.py:406
  63.8 5.5 %slope_first.1.dr_ref = f32[1536,384]{1,0:T(8,128)} custom-call(f32[8,1536]{1,0:T(8,128)} %get-tuple-element.51.b_ref, f32[8,1536]{1,0:T(8,128)} %get-tuple-element.63.db_ref, f32[8,1536]{1,0:T(8,128)} %get-tuple-element.52.geo_ref, bf16[64,32]{1,0:T(8,128)(2,1)} %get-tuple-element.119.w1_ref, bf16[64,192]{1,0:T(8,128)(2,1)} %get-tuple-element.134.w2_ref, ...), custom_call_target="tpu_custom_call" | custom-call | flops 2000000000 | bytes 348160 | tf_op jit(solution)/shard_map/slope_first/pallas_call | solution.py:102
  69.9 1.6 %middle.1 = (f32[64,128]{1,0:T(8,128)}, f32[64,128]{1,0:T(8,128)}) custom-call(f32[64,128]{1,0:T(8,128)} %get-tuple-element.43.f_ref, f32[32,128]{1,0:T(8,128)} %copy-done.4, f32[32,128]{1,0:T(8,128)} %copy-done.5, bf16[128,128]{1,0:T(8,128)(2,1)} %get-tuple-element.120.pn_ref.s_ref), custom_call_target="tpu_custom_call" | custom-call | bytes 98304 | tf_op jit(solution)/shard_map/features_plane/middle/pallas_call | solution.py:102
  71.5 2.7 %collective-permute-start.6 = (f32[64,128]{1,0:T(8,128)}, f32[64,128]{1,0:T(8,128)S(1)}, u32[]{:S(2)}, u32[]{:S(2)}) collective-permute-start(f32[64,128]{1,0:T(8,128)} %get-tuple-element.47), channel_id=1, source_target_pairs={{1,2},{3,4},{5,6},{7,8},{9,10},{11,12},{13,14},{15,0},{2,1},{4,3},... | collective-permute-start | bytes 98312 | tf_op jit(solution)/shard_map/features_plane/ppermute | solution.py:412
  74.2 2.8 %collective-permute-start.7 = (f32[64,128]{1,0:T(8,128)}, f32[64,128]{1,0:T(8,128)S(1)}, u32[]{:S(2)}, u32[]{:S(2)}) collective-permute-start(f32[64,128]{1,0:T(8,128)} %get-tuple-element.49), channel_id=1, source_target_pairs={{0,1},{1,0},{2,3},{3,2},{4,5},{5,4},{6,7},{7,6},{8,9},{9,8},{10,11... | collective-permute-start | bytes 98312 | tf_op jit(solution)/shard_map/features_plane/ppermute | solution.py:417
  77.0 5.2 %radial_second.1.r_ref = f32[1536,384]{1,0:T(8,128)} custom-call(f32[8,1536]{1,0:T(8,128)} %get-tuple-element.51.b_ref, f32[8,1536]{1,0:T(8,128)} %get-tuple-element.52.geo_ref, bf16[64,32]{1,0:T(8,128)(2,1)} %get-tuple-element.118.w1_ref, bf16[64,192]{1,0:T(8,128)(2,1)} %get-tuple-element.136.w2_ref, bf16[64,192]{1,0:T(8,128)(2,1)} %get-tuple-element.137.w3_ref, ...), custom_call_target="tpu_custom_call" | custom-call | flops 1000000000 | bytes 299008 | tf_op jit(solution)/shard_map/radial_second/pallas_call | solution.py:102
  84.2 8.7 %second_layer.1 = (f32[8,64]{1,0:T(8,128)}, f32[128,128]{1,0:T(8,128)}, f32[64,128]{1,0:T(8,128)}, f32[64,128]{1,0:T(8,128)}, f32[1536,384]{1,0:T(8,128)}, /*ind...) custom-call(f32[64,128]{1,0:T(8,128)} %get-tuple-element.43.f_ref, f32[32,128]{1,0:T(8,128)} %copy-done.4, ...), custom_call_target="tpu_custom_call" | custom-call | bytes 5612544 | tf_op jit(solution)/shard_map/second_layer/second_layer/pallas_call | solution.py:102
  92.9 6.2 %collective-permute-start.8 = (f32[64,128]{1,0:T(8,128)}, f32[64,128]{1,0:T(8,128)S(1)}, u32[]{:S(2)}, u32[]{:S(2)}) collective-permute-start(f32[64,128]{1,0:T(8,128)} %get-tuple-element.55), channel_id=1, source_target_pairs={{1,2},{3,4},{5,6},{7,8},{9,10},{11,12},{13,14},{15,0},{2,1},{4,3},... | collective-permute-start | bytes 98312 | tf_op jit(solution)/shard_map/feature_grads_plane/ppermute | solution.py:412
  99.0 2.2 %collective-permute-start.9 = (f32[64,128]{1,0:T(8,128)}, f32[64,128]{1,0:T(8,128)S(1)}, u32[]{:S(2)}, u32[]{:S(2)}) collective-permute-start(f32[64,128]{1,0:T(8,128)} %get-tuple-element.57), channel_id=1, source_target_pairs={{0,1},{1,0},{2,3},{3,2},{4,5},{5,4},{6,7},{7,6},{8,9},{9,8},{10,11... | collective-permute-start | bytes 98312 | tf_op jit(solution)/shard_map/feature_grads_plane/ppermute | solution.py:417
  101.2 5.5 %slope_second.1.dr_ref = f32[1536,384]{1,0:T(8,128)} custom-call(f32[8,1536]{1,0:T(8,128)} %get-tuple-element.51.b_ref, f32[8,1536]{1,0:T(8,128)} %get-tuple-element.63.db_ref, f32[8,1536]{1,0:T(8,128)} %get-tuple-element.52.geo_ref, bf16[64,32]{1,0:T(8,128)(2,1)} %get-tuple-element.118.w1_ref, bf16[64,192]{1,0:T(8,128)(2,1)} %get-tuple-element.136.w2_ref, ...), custom_call_target="tpu_custom_call" | custom-call | flops 2000000000 | bytes 348160 | tf_op jit(solution)/shard_map/slope_second/pallas_call | solution.py:102
  107.3 1.7 %back_middle.1 = (f32[64,128]{1,0:T(8,128)}, f32[32,128]{1,0:T(8,128)}, f32[32,128]{1,0:T(8,128)}) custom-call(f32[128,128]{1,0:T(8,128)} %get-tuple-element.54.gmid_ref, f32[64,128]{1,0:T(8,128)} %copy-done.12, f32[64,128]{1,0:T(8,128)} %copy-done.13, bf16[128,128]{1,0:T(8,128)(2,1)} %get-tuple-element.121.s_ref.pt_ref), custom_call_target="tpu_custom_call" | custom-call | bytes 163840 | tf_op jit(solution)/shard_map/feature_grads_slab/back_middle/pallas_call | solution.py:102
  109.0 5.0 %collective-permute-start.10 = (f32[32,128]{1,0:T(8,128)}, f32[32,128]{1,0:T(8,128)S(1)}, u32[]{:S(2)}, u32[]{:S(2)}) collective-permute-start(f32[32,128]{1,0:T(8,128)} %get-tuple-element.59), channel_id=1, source_target_pairs={{16,32},{48,64},{80,96},{112,128},{144,160},{176,192},{208,224},{2... | collective-permute-start | bytes 49160 | tf_op jit(solution)/shard_map/feature_grads_slab/ppermute | solution.py:401
  114.0 1.9 %collective-permute-start.11 = (f32[32,128]{1,0:T(8,128)}, f32[32,128]{1,0:T(8,128)S(1)}, u32[]{:S(2)}, u32[]{:S(2)}) collective-permute-start(f32[32,128]{1,0:T(8,128)} %get-tuple-element.61), channel_id=1, source_target_pairs={{0,16},{16,0},{32,48},{48,32},{64,80},{80,64},{96,112},{112,96},{1... | collective-permute-start | bytes 49160 | tf_op jit(solution)/shard_map/feature_grads_slab/ppermute | solution.py:406
  115.9 5.4 %early_forces.1.early_ref = f32[8,256]{1,0:T(8,128)} custom-call(f32[1536,384]{1,0:T(8,128)} %get-tuple-element.66.z_ref, f32[1536,384]{1,0:T(8,128)} %slope_second.1.dr_ref, f32[1536,128]{1,0:T(8,128)} %get-tuple-element.67.l_ref, bf16[3,1536,256]{2,1,0:T(8,128)(2,1)} %get-tuple-element.68.m_ref, f32[9,64,128]{2,1,0:T(8,128)} %get-tuple-element.69.ga_ref, ...), custom_call_target="tpu_custom_call" | custom-call | flops 1000000000 | bytes 9093120 | tf_op jit(solution)/shard_map/early_forces/pallas_call | solution.py:102
  121.9 6.5 %late_forces.1 = f32[8,256]{1,0:T(8,128)} custom-call(f32[64,128]{1,0:T(8,128)} %get-tuple-element.58.own_ref, f32[32,128]{1,0:T(8,128)} %copy-done.14, f32[32,128]{1,0:T(8,128)} %copy-done.15, bf16[64,64]{1,0:T(8,128)(2,1)} %get-tuple-element.123.s_ref.st_ref, f32[128,128]{1,0:T(8,128)} %get-tuple-element.81.out_ref, f32[8,128]{1,0:T(8,128)} %get-tuple-element.117.gain_ref, ...), custom_call_target="tpu_custom_call" | custom-call | bytes 8212480 | tf_op jit(solution)/shard_map/late_forces/late_forces/pallas_call | solution.py:102
  129.2 4.5 %collective-permute-start.13 = (f32[8,64]{1,0:T(8,128)S(1)}, f32[8,64]{1,0:T(8,128)S(1)}, u32[]{:S(2)}, u32[]{:S(2)}) collective-permute-start(f32[8,64]{1,0:T(8,128)S(1)} %get-tuple-element.70), channel_id=1, source_target_pairs={{0,1},{1,0},{2,3},{3,2},{4,5},{5,4},{6,7},{7,6},{8,9},{9,8},{10,11... | collective-permute-start | bytes 6152 | tf_op jit(solution)/shard_map/position_grads_plane/ppermute | solution.py:417
  133.7 3.7 %collective-permute-start.12 = (f32[8,64]{1,0:T(8,128)S(1)}, f32[8,64]{1,0:T(8,128)S(1)}, u32[]{:S(2)}, u32[]{:S(2)}) collective-permute-start(f32[8,64]{1,0:T(8,128)S(1)} %get-tuple-element.107), channel_id=1, source_target_pairs={{1,2},{3,4},{5,6},{7,8},{9,10},{11,12},{13,14},{15,0},{2,1},{4,3},... | collective-permute-start | bytes 6152 | tf_op jit(solution)/shard_map/position_grads_plane/ppermute | solution.py:412
  138.7 4.1 %collective-permute-done.12 = f32[8,64]{1,0:T(8,128)S(1)} collective-permute-done((f32[8,64]{1,0:T(8,128)S(1)}, f32[8,64]{1,0:T(8,128)S(1)}, u32[]{:S(2)}, u32[]{:S(2)}) %collective-permute-start.12) | collective-permute-done | bytes 2080 | tf_op jit(solution)/shard_map/position_grads_plane/ppermute | solution.py:412
  143.5 1.5 collect_plane.1
  145.8 2.7 %collective-permute-start.14 = (f32[8,32]{1,0:T(8,128)S(1)}, f32[8,32]{1,0:T(8,128)S(1)}, u32[]{:S(2)}, u32[]{:S(2)}) collective-permute-start(f32[8,32]{1,0:T(8,128)S(1)} %get-tuple-element.114), channel_id=1, source_target_pairs={{16,32},{48,64},{80,96},{112,128},{144,160},{176,192},{208,224},{2... | collective-permute-start | bytes 3080 | tf_op jit(solution)/shard_map/position_grads_slab/ppermute | solution.py:401
  148.5 1.9 %collective-permute-start.15 = (f32[8,32]{1,0:T(8,128)S(1)}, f32[8,32]{1,0:T(8,128)S(1)}, u32[]{:S(2)}, u32[]{:S(2)}) collective-permute-start(f32[8,32]{1,0:T(8,128)S(1)} %get-tuple-element.71), channel_id=1, source_target_pairs={{0,16},{16,0},{32,48},{48,32},{64,80},{80,64},{96,112},{112,96},{1... | collective-permute-start | bytes 3080 | tf_op jit(solution)/shard_map/position_grads_slab/ppermute | solution.py:406
  153.5 1.4 collect_slab.1
  (134 shorter events, 30.2 us)
Async XLA Ops:
  0.6 22.6 %copy-start.18 = (s32[1,1,2,64]{3,2,1,0:T(2,128)S(1)}, s32[1,1,2,64]{3,2,1,0:T(2,128)}, u32[]{:S(2)}) copy-start(s32[1,1,2,64]{3,2,1,0:T(2,128)} %param.22) | copy-start | bytes 1540
  0.6 23.4 %copy-start.2 = (f32[2,128,128]{2,1,0:T(8,128)S(1)}, f32[2,128,128]{2,1,0:T(8,128)}, u32[]{:S(2)}) copy-start(f32[2,128,128]{2,1,0:T(8,128)} %param.32) | copy-start | bytes 393220
  0.7 23.4 %copy-start.3 = (f32[2,128,128]{2,1,0:T(8,128)S(1)}, f32[2,128,128]{2,1,0:T(8,128)}, u32[]{:S(2)}) copy-start(f32[2,128,128]{2,1,0:T(8,128)} %param.31) | copy-start | bytes 393220
  0.7 24.1 %copy-start.9 = (f32[89,128]{1,0:T(8,128)S(1)}, f32[89,128]{1,0:T(8,128)}, u32[]{:S(2)}) copy-start(f32[89,128]{1,0:T(8,128)} %param.25) | copy-start | bytes 136708
  0.7 24.4 %copy-start.16 = (f32[2,8,64]{2,1,0:T(8,128)S(1)}, f32[2,8,64]{2,1,0:T(8,128)}, u32[]{:S(2)}) copy-start(f32[2,8,64]{2,1,0:T(8,128)} %param.27) | copy-start | bytes 12292
  0.7 24.5 %copy-start.6 = (f32[2,64,64]{2,1,0:T(8,128)S(1)}, f32[2,64,64]{2,1,0:T(8,128)}, u32[]{:S(2)}) copy-start(f32[2,64,64]{2,1,0:T(8,128)} %param.28) | copy-start | bytes 98308
  6.4 27.9 %collective-permute-start = (f32[8,32]{1,0:T(8,128)}, f32[8,32]{1,0:T(8,128)S(1)}, u32[]{:S(2)}, u32[]{:S(2)}) collective-permute-start(f32[8,32]{1,0:T(8,128)} %get-tuple-element.37), channel_id=1, source_target_pairs={{16,32},{48,64},{80,96},{112,128},{144,160},{176,192},{208,224},{2... | collective-permute-start | bytes 3080 | tf_op jit(solution)/shard_map/atoms_slab/ppermute | solution.py:401
  16.7 17.6 %collective-permute-start.1 = (f32[8,32]{1,0:T(8,128)}, f32[8,32]{1,0:T(8,128)S(1)}, u32[]{:S(2)}, u32[]{:S(2)}) collective-permute-start(f32[8,32]{1,0:T(8,128)} %get-tuple-element.39), channel_id=1, source_target_pairs={{0,16},{16,0},{32,48},{48,32},{64,80},{80,64},{96,112},{112,96},{1... | collective-permute-start | bytes 3080 | tf_op jit(solution)/shard_map/atoms_slab/ppermute | solution.py:406
  20.8 4.5 %copy-start.7 = (f32[2,64,64]{2,1,0:T(8,128)S(1)}, f32[2,64,64]{2,1,0:T(8,128)}, u32[]{:S(2)}) copy-start(f32[2,64,64]{2,1,0:T(8,128)} %param.29) | copy-start | bytes 98308
  21.0 4.5 %copy-start = (f32[2,64,384]{2,1,0:T(8,128)S(1)}, f32[2,64,384]{2,1,0:T(8,128)}, u32[]{:S(2)}) copy-start(f32[2,64,384]{2,1,0:T(8,128)} %param.30) | copy-start | bytes 589828
  22.2 3.3 %copy-start.17 = (f32[2,4,128]{2,1,0:T(4,128)S(1)}, f32[2,4,128]{2,1,0:T(4,128)}, u32[]{:S(2)}) copy-start(f32[2,4,128]{2,1,0:T(4,128)} %param.34) | copy-start | bytes 12292
  22.2 3.9 %copy-start.1 = (f32[2,128,128]{2,1,0:T(8,128)S(1)}, f32[2,128,128]{2,1,0:T(8,128)}, u32[]{:S(2)}) copy-start(f32[2,128,128]{2,1,0:T(8,128)} %param.33) | copy-start | bytes 393220
  25.5 20.3 %copy-start.21 = (f32[89]{0:T(128)S(1)}, f32[89]{0:T(128)}, u32[]{:S(2)}) copy-start(f32[89]{0:T(128)} %param.26) | copy-start | bytes 1072
  25.5 25.7 %copy-start.8 = (f32[8,64]{1,0:T(8,128)S(1)}, f32[8,64]{1,0:T(8,128)}, u32[]{:S(2)}) copy-start(f32[8,64]{1,0:T(8,128)} %pad_maximum_fusion.8.v_ref.kinds_ref) | copy-start | bytes 6148
  36.6 14.4 %collective-permute-start.2 = (f32[8,64]{1,0:T(8,128)}, f32[8,64]{1,0:T(8,128)S(1)}, u32[]{:S(2)}, u32[]{:S(2)}) collective-permute-start(f32[8,64]{1,0:T(8,128)} %get-tuple-element.40), channel_id=1, source_target_pairs={{1,2},{3,4},{5,6},{7,8},{9,10},{11,12},{13,14},{15,0},{2,1},{4,3},... | collective-permute-start | bytes 6152 | tf_op jit(solution)/shard_map/atoms_plane/ppermute | solution.py:412
  43.8 7.2 %collective-permute-start.3 = (f32[8,64]{1,0:T(8,128)}, f32[8,64]{1,0:T(8,128)S(1)}, u32[]{:S(2)}, u32[]{:S(2)}) collective-permute-start(f32[8,64]{1,0:T(8,128)} %get-tuple-element.42), channel_id=1, source_target_pairs={{0,1},{1,0},{2,3},{3,2},{4,5},{5,4},{6,7},{7,6},{8,9},{9,8},{10,11... | collective-permute-start | bytes 6152 | tf_op jit(solution)/shard_map/atoms_plane/ppermute | solution.py:417
  59.9 9.4 %collective-permute-start.4 = (f32[32,128]{1,0:T(8,128)}, f32[32,128]{1,0:T(8,128)S(1)}, u32[]{:S(2)}, u32[]{:S(2)}) collective-permute-start(f32[32,128]{1,0:T(8,128)} %get-tuple-element.44), channel_id=1, source_target_pairs={{16,32},{48,64},{80,96},{112,128},{144,160},{176,192},{208,224},{2... | collective-permute-start | bytes 49160 | tf_op jit(solution)/shard_map/features_slab/ppermute | solution.py:401
  61.8 7.4 %collective-permute-start.5 = (f32[32,128]{1,0:T(8,128)}, f32[32,128]{1,0:T(8,128)S(1)}, u32[]{:S(2)}, u32[]{:S(2)}) collective-permute-start(f32[32,128]{1,0:T(8,128)} %get-tuple-element.46), channel_id=1, source_target_pairs={{0,16},{16,0},{32,48},{48,32},{64,80},{80,64},{96,112},{112,96},{1... | collective-permute-start | bytes 49160 | tf_op jit(solution)/shard_map/features_slab/ppermute | solution.py:406
  71.5 10.8 %collective-permute-start.6 = (f32[64,128]{1,0:T(8,128)}, f32[64,128]{1,0:T(8,128)S(1)}, u32[]{:S(2)}, u32[]{:S(2)}) collective-permute-start(f32[64,128]{1,0:T(8,128)} %get-tuple-element.47), channel_id=1, source_target_pairs={{1,2},{3,4},{5,6},{7,8},{9,10},{11,12},{13,14},{15,0},{2,1},{4,3},... | collective-permute-start | bytes 98312 | tf_op jit(solution)/shard_map/features_plane/ppermute | solution.py:412
  74.2 8.1 %collective-permute-start.7 = (f32[64,128]{1,0:T(8,128)}, f32[64,128]{1,0:T(8,128)S(1)}, u32[]{:S(2)}, u32[]{:S(2)}) collective-permute-start(f32[64,128]{1,0:T(8,128)} %get-tuple-element.49), channel_id=1, source_target_pairs={{0,1},{1,0},{2,3},{3,2},{4,5},{5,4},{6,7},{7,6},{8,9},{9,8},{10,11... | collective-permute-start | bytes 98312 | tf_op jit(solution)/shard_map/features_plane/ppermute | solution.py:417
  77.0 5.9 %copy-start.19 = (f32[128]{0:T(128)S(1)}, f32[128]{0:T(128)}, u32[]{:S(2)}) copy-start(f32[128]{0:T(128)} %param.35) | copy-start | bytes 1540
  77.0 6.5 %copy-start.20 = (f32[16]{0:T(128)S(1)}, f32[16]{0:T(128)}, u32[]{:S(2)}) copy-start(f32[16]{0:T(128)} %param.37) | copy-start | bytes 196
  82.3 1.9 %copy-start.10 = (f32[64,128]{1,0:T(8,128)}, f32[64,128]{1,0:T(8,128)S(1)}, u32[]{:S(2)}) copy-start(f32[64,128]{1,0:T(8,128)S(1)} %collective-permute-done.6.pl_ref) | copy-start | bytes 98308
  82.3 1.9 %copy-start.11 = (f32[64,128]{1,0:T(8,128)}, f32[64,128]{1,0:T(8,128)S(1)}, u32[]{:S(2)}) copy-start(f32[64,128]{1,0:T(8,128)S(1)} %collective-permute-done.7.ps_ref) | copy-start | bytes 98308
  92.9 13.8 %collective-permute-start.8 = (f32[64,128]{1,0:T(8,128)}, f32[64,128]{1,0:T(8,128)S(1)}, u32[]{:S(2)}, u32[]{:S(2)}) collective-permute-start(f32[64,128]{1,0:T(8,128)} %get-tuple-element.55), channel_id=1, source_target_pairs={{1,2},{3,4},{5,6},{7,8},{9,10},{11,12},{13,14},{15,0},{2,1},{4,3},... | collective-permute-start | bytes 98312 | tf_op jit(solution)/shard_map/feature_grads_plane/ppermute | solution.py:412
  99.0 7.7 %collective-permute-start.9 = (f32[64,128]{1,0:T(8,128)}, f32[64,128]{1,0:T(8,128)S(1)}, u32[]{:S(2)}, u32[]{:S(2)}) collective-permute-start(f32[64,128]{1,0:T(8,128)} %get-tuple-element.57), channel_id=1, source_target_pairs={{0,1},{1,0},{2,3},{3,2},{4,5},{5,4},{6,7},{7,6},{8,9},{9,8},{10,11... | collective-permute-start | bytes 98312 | tf_op jit(solution)/shard_map/feature_grads_plane/ppermute | solution.py:417
  109.0 12.3 %collective-permute-start.10 = (f32[32,128]{1,0:T(8,128)}, f32[32,128]{1,0:T(8,128)S(1)}, u32[]{:S(2)}, u32[]{:S(2)}) collective-permute-start(f32[32,128]{1,0:T(8,128)} %get-tuple-element.59), channel_id=1, source_target_pairs={{16,32},{48,64},{80,96},{112,128},{144,160},{176,192},{208,224},{2... | collective-permute-start | bytes 49160 | tf_op jit(solution)/shard_map/feature_grads_slab/ppermute | solution.py:401
  114.0 7.3 %collective-permute-start.11 = (f32[32,128]{1,0:T(8,128)}, f32[32,128]{1,0:T(8,128)S(1)}, u32[]{:S(2)}, u32[]{:S(2)}) collective-permute-start(f32[32,128]{1,0:T(8,128)} %get-tuple-element.61), channel_id=1, source_target_pairs={{0,16},{16,0},{32,48},{48,32},{64,80},{80,64},{96,112},{112,96},{1... | collective-permute-start | bytes 49160 | tf_op jit(solution)/shard_map/feature_grads_slab/ppermute | solution.py:406
  129.2 9.5 %collective-permute-start.13 = (f32[8,64]{1,0:T(8,128)S(1)}, f32[8,64]{1,0:T(8,128)S(1)}, u32[]{:S(2)}, u32[]{:S(2)}) collective-permute-start(f32[8,64]{1,0:T(8,128)S(1)} %get-tuple-element.70), channel_id=1, source_target_pairs={{0,1},{1,0},{2,3},{3,2},{4,5},{5,4},{6,7},{7,6},{8,9},{9,8},{10,11... | collective-permute-start | bytes 6152 | tf_op jit(solution)/shard_map/position_grads_plane/ppermute | solution.py:417
  133.7 9.1 %collective-permute-start.12 = (f32[8,64]{1,0:T(8,128)S(1)}, f32[8,64]{1,0:T(8,128)S(1)}, u32[]{:S(2)}, u32[]{:S(2)}) collective-permute-start(f32[8,64]{1,0:T(8,128)S(1)} %get-tuple-element.107), channel_id=1, source_target_pairs={{1,2},{3,4},{5,6},{7,8},{9,10},{11,12},{13,14},{15,0},{2,1},{4,3},... | collective-permute-start | bytes 6152 | tf_op jit(solution)/shard_map/position_grads_plane/ppermute | solution.py:412
  145.8 7.0 %collective-permute-start.14 = (f32[8,32]{1,0:T(8,128)S(1)}, f32[8,32]{1,0:T(8,128)S(1)}, u32[]{:S(2)}, u32[]{:S(2)}) collective-permute-start(f32[8,32]{1,0:T(8,128)S(1)} %get-tuple-element.114), channel_id=1, source_target_pairs={{16,32},{48,64},{80,96},{112,128},{144,160},{176,192},{208,224},{2... | collective-permute-start | bytes 3080 | tf_op jit(solution)/shard_map/position_grads_slab/ppermute | solution.py:401
  148.5 3.1 %collective-permute-start.15 = (f32[8,32]{1,0:T(8,128)S(1)}, f32[8,32]{1,0:T(8,128)S(1)}, u32[]{:S(2)}, u32[]{:S(2)}) collective-permute-start(f32[8,32]{1,0:T(8,128)S(1)} %get-tuple-element.71), channel_id=1, source_target_pairs={{0,16},{16,0},{32,48},{48,32},{64,80},{80,64},{96,112},{112,96},{1... | collective-permute-start | bytes 3080 | tf_op jit(solution)/shard_map/position_grads_slab/ppermute | solution.py:406
  (6 other events, 3.6 us)
where the time goes:
time: 158 us; the launch traced here: 156 us
  starting transfers between devices  58.9 us (37%)
  Pallas kernels  54.1 us (34%)
  local copies, waits for them, and re-layouts  15.4 us (10%)
  other arithmetic  15.2 us (10%)
  waiting for transfers between devices  10.6 us (7%)
  between operations  1.86 us (1%)
    pallas_call x13, Pallas kernels, call(): pl.pallas_call(kernel, out_shape=out_shape, in_specs=[spec] * len(args),...  54.1 us
    ppermute x4, starting transfers between devices, swap_slab_far(): return lax.ppermute(value, 'slab', pairs + [(b, a) for a, b in pairs])  19.9 us
    ppermute x4, starting transfers between devices, swap_plane_far(): return lax.ppermute(value, 'plane', pairs + [(b, a) for a, b in pairs])  19.8 us
    ppermute x4, starting transfers between devices, swap_plane_near(): return lax.ppermute(value, 'plane', [(i, i ^ 1) for i in range(count)])  11.4 us
    ppermute x4, starting transfers between devices, swap_slab_near(): return lax.ppermute(value, 'slab', [(i, i ^ 1) for i in range(count)])  7.68 us
    ppermute x4, waiting for transfers between devices, swap_plane_near(): return lax.ppermute(value, 'plane', [(i, i ^ 1) for i in range(count)])  5.26 us
    ppermute x4, waiting for transfers between devices, swap_plane_far(): return lax.ppermute(value, 'plane', pairs + [(b, a) for a, b in pairs])  4.14 us
    unnamed x52, local copies, waits for them, and re-layouts  3.59 us
  transfers between devices with their start and end apart: 16, of which 3 were waited for; matrix products, arithmetic and copies ran while one was open for 11% of the time, Pallas kernels for 14%

commit v1 on v0

v1 whole, which is shorter than its diff:
```python
import functools

import jax
import jax.numpy as jnp
from jax import lax
from jax.experimental import pallas as pl
from jax.experimental.pallas import tpu as pltpu
from jax.sharding import PartitionSpec as P

CELLS_Y = 2
CELLS_Z = 2

cutoff_radius = 5.0
cell_side = 3.0
inverse_neighbours = 0.2
highest = lax.Precision.HIGHEST
f32 = jnp.float32
bf16 = jnp.bfloat16

C = 128
OWN = 64
EXT = 256
EDGES = 1536
BLOCKS = 4
GROUP = 16
SPAN = EDGES // BLOCKS
KINDS = 96
LMS = (1, 3, 5)
FIRST_LM = (0, 1, 4)
STACK_AT = (0, 48, 192)
STACK = 432
R3, R5, R15 = 3.0**0.5, 5.0**0.5, 15.0**0.5

NN = (((1,), (0,)), ((), ()))
TN = (((0,), (0,)), ((), ()))
NT = (((1,), (1,)), ((), ()))


def dot(a, b, dims=NN):
    return lax.dot_general(a, b, dims, preferred_element_type=f32)


def dot3(a, b, dims=NN):
    return lax.dot_general(a, b, dims, precision=lax.Precision.HIGH, preferred_element_type=f32)


def split(x):
    hi = x.astype(bf16)
    return hi, (x - hi.astype(f32)).astype(bf16)


def pair_lanes(x):
    hi, lo = split(x)
    return jnp.concatenate([hi, lo], axis=1)


def halves(o):
    return o[:, :C] + o[:, C:]


def stack_rows(x):
    hi, lo = split(x)
    return jnp.concatenate([hi, lo, hi], axis=0)


def three(x):
    hi = x.astype(bf16).astype(f32)
    rest = x - hi
    mid = rest.astype(bf16).astype(f32)
    return hi, mid, rest - mid


def pick_lanes(values, chooser, dims=NN):
    hi, mid, lo = three(values)
    o = dot(jnp.concatenate([hi, mid, lo, jnp.zeros_like(lo)], axis=0).astype(bf16), chooser, dims)
    return (o[0:8] + o[8:16]) + o[16:24]


def pick_rows(chooser, values, dims=NN):
    hi, mid, lo = three(values)
    o = dot(chooser, jnp.concatenate([hi, mid, lo], axis=1).astype(bf16), dims)
    return (o[:, :C] + o[:, C : 2 * C]) + o[:, 2 * C :]


def silu(x):
    return x * (1.0 / (1.0 + jnp.exp(-x)))


def silu_pair(x):
    s = 1.0 / (1.0 + jnp.exp(-x))
    return x * s, s * (1.0 + x * (1.0 - s))


def span(b):
    return pl.ds(b * SPAN, SPAN)


def fetched(kernel, count):
    def run(*refs):
        given, rest = refs[:count], refs[count:]
        sems, held = rest[-1], rest[-1 - count : -1]
        copies = [pltpu.make_async_copy(src, dst, sems.at[k]) for k, (src, dst) in enumerate(zip(given, held))]
        for copy in copies:
            copy.start()
        for copy in copies:
            copy.wait()
        kernel(*held, *rest[: -1 - count])

    return run


def call(kernel, outs, args, scratch=(), flops=0, name=None, limit=8, raw=False):
    spec = pl.BlockSpec(memory_space=pltpu.VMEM)
    out_shape = tuple(pltpu.VMEM(shape, dtype) for shape, dtype in outs)
    moved = sum(a.size * a.dtype.itemsize for a in args)
    scratch = list(scratch)
    if raw:
        big = [a for a in args if a.size > 1]
        scratch += [pltpu.VMEM(a.shape, a.dtype) for a in big] + [pltpu.SemaphoreType.DMA((len(big),))]
        kernel = fetched(kernel, len(big))
        in_specs = [pl.BlockSpec(memory_space=pltpu.HBM)] * len(big)
        in_specs += [pl.BlockSpec(memory_space=pltpu.SMEM)] * (len(args) - len(big))
        args = [pltpu.with_memory_space_constraint(a, pltpu.HBM) for a in big] + [a for a in args if a.size == 1]
    else:
        in_specs = [spec] * len(args)
        args = [pltpu.with_memory_space_constraint(a, pltpu.VMEM) for a in args]
    return pl.pallas_call(
        kernel,
        out_shape=out_shape,
        in_specs=in_specs,
        out_specs=tuple(spec for _ in out_shape),
        scratch_shapes=scratch,
        compiler_params=pltpu.CompilerParams(vmem_limit_bytes=limit * 1024 * 1024),
        cost_estimate=pl.CostEstimate(flops=flops, bytes_accessed=moved, transcendentals=0),
        name=name,
    )(*args)


def odd(axis):
    return lax.rem(lax.axis_index(axis), 2)


def by_parity(flag, rows):
    swap = jnp.full(rows[0:1].shape, flag) == 1
    return jnp.where(swap, rows[0:1], rows[1:2]), jnp.where(swap, rows[1:2], rows[0:1])


def moved_slab(slot):
    swap = (jnp.full(slot.shape, odd("slab")) == 1) & (slot >= 64) & (slot < 128)
    return jnp.where(swap, slot ^ 32, slot)


def chooser(slots, picked):
    rows = lax.broadcasted_iota(jnp.int32, (slots, picked.shape[1]), 0)
    return (rows == picked).astype(f32).astype(bf16)


def shifted(values, row, step):
    rows = lax.broadcasted_iota(jnp.int32, values.shape, 0)
    return values + jnp.where(rows == row, step, 0.0)


def atoms_slab_kernel(
    pos_ref, kind_ref, list_ref, plane_ref, v_ref, tf_ref, tn_ref, pf_ref, pn_ref, far_ref, near_ref
):
    for k in range(3):
        v_ref[k : k + 1, :] = pos_ref[0, k]
    v_ref[3:4, :] = kind_ref[...].astype(f32)
    v_ref[4:8, :] = jnp.zeros((4, OWN), f32)
    far, near = by_parity(odd("slab"), list_ref[...])
    far, near = chooser(OWN, far), chooser(OWN, near)
    tf_ref[...] = far
    tn_ref[...] = near
    v = v_ref[...]
    far_ref[...] = pick_lanes(v, far)
    near_ref[...] = pick_lanes(v, near)
    for picked, t_ref in zip(by_parity(odd("plane"), plane_ref[...]), (pf_ref, pn_ref)):
        t_ref[...] = chooser(128, moved_slab(picked))


def atoms_plane_kernel(v_ref, far_ref, near_ref, tf_ref, tn_ref, pf_ref, pn_ref, sf_ref, sn_ref):
    step = (2 * odd("slab") - 1).astype(f32) * (CELLS_Z * cell_side)
    far = shifted(far_ref[...], 2, step)
    near = shifted(near_ref[...], 2, -step)
    pf_ref[...] = far
    pn_ref[...] = near
    own = v_ref[...]
    for t_ref, s_ref in ((tf_ref, sf_ref), (tn_ref, sn_ref)):
        s_ref[...] = pick_lanes(own, t_ref[0:64, :]) + (
            pick_lanes(far, t_ref[64:96, :]) + pick_lanes(near, t_ref[96:128, :])
        )


def prepare_kernel(
    edge_ref, one_ref, two_ref, three_ref, four_ref, embed_ref, up_ref, skip_ref, atom_ref, hid_ref, ro_ref,
    out_ref, gain_ref, read_ref, count_ref,
    g_ref, gt_ref, dd_ref, mask_ref, w1_ref, w2_ref, w3_ref, w4_ref, table_ref, skips_ref, refs_ref, hidt_ref, hidro_ref,
    up1_ref, skip1_ref, outs_ref, gains_ref, reads_ref, ros_ref,
):
    per_atom = count_ref[0, 0] // OWN
    senders = jnp.broadcast_to(edge_ref[0:1, :], (8, EDGES))
    swap_plane = jnp.full((1, SPAN), odd("plane")) == 1
    place = lax.broadcasted_iota(jnp.int32, (GROUP, SPAN), 1)
    first_place = lax.broadcasted_iota(jnp.int32, (GROUP, SPAN), 0) * per_atom
    mask = ((place >= first_place) & (place < first_place + per_atom)).astype(f32)
    lanes = lax.broadcasted_iota(jnp.int32, (128, 128), 1).astype(f32)
    for b in range(BLOCKS):
        start = b * GROUP * per_atom
        rows = senders if b == 0 else pltpu.roll(senders, lax.rem(EDGES - start, EDGES), 1)
        row = rows[0:1, :SPAN]
        row = moved_slab(row)
        row = jnp.where(swap_plane & (row >= 128), row ^ 64, row)
        row = jnp.where(place[0:1] < GROUP * per_atom, row, -1)
        t = (lax.broadcasted_iota(jnp.int32, (EXT, SPAN), 0) == row).astype(f32)
        gt_ref[:, span(b)] = t.astype(bf16)
        dd_ref[:, span(b)] = t.astype(bf16)
        mine = pl.ds(b * GROUP, GROUP)
        dd_ref[mine, span(b)] = (t[b * GROUP : (b + 1) * GROUP] - mask).astype(bf16)
        mask_ref[:, span(b)] = mask
        for chunk in range(SPAN // 128):
            part = row[:, chunk * 128 : (chunk + 1) * 128].astype(f32)
            column = jnp.transpose(jnp.broadcast_to(part, (128, 128)))
            here = pl.ds(b * SPAN + chunk * 128, 128)
            g_ref[here, 0:128] = (column == lanes).astype(f32).astype(bf16)
            g_ref[here, 128:256] = (column == lanes + 128.0).astype(f32).astype(bf16)
    for t in range(2):
        hi, mid, lo = three(one_ref[t])
        stacked = jnp.concatenate([hi, hi, mid + lo, jnp.zeros_like(hi)], axis=0)
        w1_ref[t] = jnp.transpose(stacked).astype(bf16)
        for ref, to_ref in ((two_ref, w2_ref), (three_ref, w3_ref)):
            hi, mid, lo = three(ref[t])
            to_ref[t] = jnp.transpose(jnp.concatenate([hi, hi, mid + lo], axis=0)).astype(bf16)
        hi, lo = split(four_ref[t])
        w4_ref[t] = jnp.concatenate([hi, hi, lo], axis=0)
    embed = embed_ref[...]
    kinds = embed.shape[0]
    table_ref[...] = jnp.zeros(table_ref.shape, bf16)
    skips_ref[...] = jnp.zeros(skips_ref.shape, bf16)
    exact = functools.partial(
        lax.dot_general, dimension_numbers=NN, precision=highest, preferred_element_type=f32
    )
    table_ref[0:kinds, :] = pair_lanes(exact(embed, up_ref[0]))
    hi, mid, lo = three(exact(embed, skip_ref[0]))
    skips_ref[0:kinds, :] = jnp.concatenate([hi, mid, lo], axis=1).astype(bf16)
    refs_ref[...] = jnp.zeros(refs_ref.shape, f32)
    refs_ref[0:1, 0:kinds] = atom_ref[...]
    hidt_ref[...] = hid_ref[...]
    hidro_ref[...] = hid_ref[...] * jnp.transpose(jnp.broadcast_to(ro_ref[...], (C, ro_ref.shape[1])))
    up1_ref[...] = up_ref[1]
    skip1_ref[...] = skip_ref[1]
    outs_ref[...] = out_ref[...]
    gains_ref[...] = gain_ref[...]
    reads_ref[...] = read_ref[...]
    ros_ref[...] = jnp.broadcast_to(ro_ref[...], ros_ref.shape)


def geometry(v, valid, b_ref, db_ref, geo_ref):
    vx = jnp.where(valid, v[0:1], 2.0 * cutoff_radius)
    vy = jnp.where(valid, v[1:2], 0.0)
    vz = jnp.where(valid, v[2:3], 0.0)
    d = jnp.sqrt(vx * vx + vy * vy + vz * vz)
    inv = 1.0 / d
    geo_ref[0:1, :] = vx * inv
    geo_ref[1:2, :] = vy * inv
    geo_ref[2:3, :] = vz * inv
    geo_ref[3:4, :] = inv
    s = d / cutoff_radius
    s2 = s * s
    s4 = s2 * s2
    s5 = s4 * s
    s6 = s4 * s2
    s7 = s6 * s
    inside = (s < 1.0) & valid
    u = 1.0 - 28.0 * s6 + 48.0 * s7 - 21.0 * s4 * s4
    du = (-168.0 * s5 + 336.0 * s6 - 168.0 * s7) / cutoff_radius
    geo_ref[4:5, :] = jnp.where(inside, u * inverse_neighbours, 0.0)
    geo_ref[5:6, :] = jnp.where(inside, du * inverse_neighbours, 0.0)
    geo_ref[6:8, :] = jnp.zeros_like(geo_ref[6:8, :])
    t = (jnp.minimum(s, 1.0) - 0.5) * jnp.pi
    z = t * t
    cs = 1.0 - z * (1 / 2 - z * (1 / 24 - z * (1 / 720 - z * (1 / 40320 - z * (1 / 3628800 - z * (1 / 479001600 - z * (1 / 87178291200)))))))
    sn = 1.0 - z * (1 / 6 - z * (1 / 120 - z * (1 / 5040 - z * (1 / 362880 - z * (1 / 39916800 - z * (1 / 6227020800))))))
    s1, c1 = cs, -t * sn

    def plus(a, b):
        return a[0] * b[1] + a[1] * b[0], a[1] * b[1] - a[0] * b[0]

    w1 = (s1, c1)
    w2 = plus(w1, w1)
    w3 = plus(w2, w1)
    w4 = plus(w2, w2)
    waves = (w1, w2, w3, w4, plus(w4, w1), plus(w4, w2), plus(w4, w3), plus(w4, w4))
    gain = (2.0 / cutoff_radius) ** 0.5 * inv
    for n, (sine, cosine) in enumerate(waves):
        b_ref[n : n + 1, :] = gain * sine
        db_ref[n : n + 1, :] = gain * (cosine * ((n + 1) * jnp.pi / cutoff_radius) - sine * inv)


def basis_stack(x):
    hi, mid, _ = three(x)
    lo = x - hi
    return jnp.concatenate([hi, lo, hi, jnp.zeros_like(hi)], axis=0).astype(bf16)


def radial_hidden(b, w1, w2, w3):
    h = silu(dot(w1, basis_stack(b)))
    h = silu(dot(w2, stack_rows(h)))
    return silu(dot(w3, stack_rows(h)))


def radial_hidden_pair(b, db, w1, w2, w3):
    h, g = silu_pair(dot(w1, basis_stack(b)))
    t = g * dot(w1, basis_stack(db))
    h, g = silu_pair(dot(w2, stack_rows(h)))
    t = g * dot(w2, stack_rows(t))
    h, g = silu_pair(dot(w3, stack_rows(h)))
    t = g * dot(w3, stack_rows(t))
    return h, t


def angular_rows(geo):
    x, y, z = geo[0:1], geo[1:2], geo[2:3]
    return (
        jnp.ones_like(x),
        R3 * x,
        R3 * y,
        R3 * z,
        R15 * x * y,
        R15 * y * z,
        0.5 * R5 * (3.0 * z * z - 1.0),
        R15 * x * z,
        0.5 * R15 * (x * x - y * y),
    )


def messages(g_ref, lifted, radial_of, l_ref, m_ref):
    for b in range(BLOCKS):
        lift = halves(dot(g_ref[span(b), :], lifted))
        l_ref[span(b), :] = lift
        radial = radial_of(b)
        for l in range(3):
            m_ref[l, span(b), :] = pair_lanes(radial[:, l * C : (l + 1) * C] * lift)


def amplitudes(ast_ref, m_ref, amp_ref):
    for b in range(BLOCKS):
        for l in range(3):
            n = LMS[l]
            o = dot(ast_ref[pl.ds(b * STACK + STACK_AT[l], 32 * n), :], m_ref[l, span(b), :])
            amp = halves(o[: 16 * n]) + o[16 * n :, :C]
            for k in range(n):
                amp_ref[FIRST_LM[l] + k, pl.ds(b * GROUP, GROUP), :] = amp[16 * k : 16 * (k + 1)]


def invariants(amp_ref, gain):
    b0 = amp_ref[0]
    b1 = sum(amp_ref[k] * amp_ref[k] for k in range(1, 4))
    b2 = sum(amp_ref[k] * amp_ref[k] for k in range(4, 9))
    return gain[0:1] * b0 + gain[1:2] * b1 + gain[2:3] * b2 + gain[3:4] * b0 * b0


def amp_grads(amp_ref, gain, gm, ga_ref):
    ga_ref[0] = gm * (gain[0:1] + 2.0 * gain[3:4] * amp_ref[0])
    one = gm * (2.0 * gain[1:2])
    two = gm * (2.0 * gain[2:3])
    for k in range(1, 4):
        ga_ref[k] = one * amp_ref[k]
    for k in range(4, 9):
        ga_ref[k] = two * amp_ref[k]


def group_grads(ga_ref, b, l):
    return jnp.concatenate(
        [ga_ref[FIRST_LM[l] + k, pl.ds(b * GROUP, GROUP), :] for k in range(LMS[l])], axis=0
    )


def spread(ast_ref, ga_ref, b, l):
    n = LMS[l]
    hi, lo = split(group_grads(ga_ref, b, l))
    return dot(
        ast_ref[pl.ds(b * STACK + STACK_AT[l], 48 * n), :], jnp.concatenate([hi, hi, lo], axis=0), TN
    )


def angular_grads(m_ref, ga_ref, mask_ref, gy_ref):
    for b in range(BLOCKS):
        mask = mask_ref[:, span(b)]
        for l in (1, 2):
            n = LMS[l]
            hi, lo = split(group_grads(ga_ref, b, l))
            left = jnp.concatenate(
                [jnp.concatenate([hi, hi], axis=1), jnp.concatenate([lo, jnp.zeros_like(lo)], axis=1)],
                axis=0,
            )
            w = dot(left, m_ref[l, span(b), :], NT)
            w = w[: 16 * n] + w[16 * n :]
            for k in range(n):
                row = FIRST_LM[l] + k - 1
                gy_ref[row : row + 1, span(b)] = jnp.sum(mask * w[16 * k : 16 * (k + 1)], axis=0, keepdims=True)


def edge_forces(x_ref, gy_ref, geo_ref, gv_ref):
    gd = dot(jnp.ones((16, 2 * C), bf16), x_ref[...], NT)[0:1]
    gy = [None] + [gy_ref[k : k + 1, :] for k in range(8)]
    x, y, z, inv = (geo_ref[k : k + 1, :] for k in range(4))
    gx = R3 * gy[1] + R15 * (y * gy[4] + z * gy[7] + x * gy[8])
    gyy = R3 * gy[2] + R15 * (x * gy[4] + z * gy[5] - y * gy[8])
    gz = R3 * gy[3] + R15 * (y * gy[5] + x * gy[7]) + (3.0 * R5) * z * gy[6]
    along = x * gx + y * gyy + z * gz
    core = gd - along * inv
    gv_ref[0:1, :] = core * x + gx * inv
    gv_ref[1:2, :] = core * y + gyy * inv
    gv_ref[2:3, :] = core * z + gz * inv
    gv_ref[3:8, :] = jnp.zeros((5, EDGES), f32)


def first_kernel(
    v_ref, pf_ref, pn_ref, qf_ref, qn_ref, dd_ref, g_ref, mask_ref, table_ref, skip_ref, w1_ref, w2_ref, w3_ref, w4_ref,
    gain_ref, out_ref, tf_ref, tn_ref,
    f_ref, sf_ref, sn_ref, amp_ref, l_ref, m_ref, ast_ref, b_ref, db_ref, geo_ref,
):
    step = (2 * odd("plane") - 1).astype(f32) * (CELLS_Y * cell_side)
    parts = (v_ref[...], pf_ref[...], pn_ref[...], shifted(qf_ref[...], 1, step), shifted(qn_ref[...], 1, -step))
    valid = jnp.sum(mask_ref[...], axis=0, keepdims=True) > 0.5
    vector, lifted, at = None, [], 0
    for part in parts:
        rows = part.shape[1]
        piece = pick_lanes(part, dd_ref[at : at + rows, :])
        vector = piece if vector is None else vector + piece
        kinds = lax.broadcasted_iota(jnp.int32, (KINDS, rows), 0).astype(f32) == part[3:4]
        kinds = kinds.astype(f32).astype(bf16)
        if at == 0:
            o = dot(kinds, skip_ref[...], TN)
            skipped = (o[:, :C] + o[:, C : 2 * C]) + o[:, 2 * C :]
        lifted.append(dot(kinds, table_ref[...], TN))
        at += rows
    lifted = jnp.concatenate(lifted, axis=0).astype(bf16)
    geometry(vector, valid, b_ref, db_ref, geo_ref)
    h = stack_rows(radial_hidden(b_ref[...], w1_ref[0], w2_ref[0], w3_ref[0]) * geo_ref[4:5, :])
    rows = angular_rows(geo_ref[0:3, :])
    for b in range(BLOCKS):
        mask = mask_ref[:, span(b)]
        for l in range(3):
            a = jnp.concatenate(
                [mask * rows[FIRST_LM[l] + k][:, b * SPAN : (b + 1) * SPAN] for k in range(LMS[l])], axis=0
            )
            ast_ref[pl.ds(b * STACK + STACK_AT[l], 48 * LMS[l]), :] = stack_rows(a)
    messages(g_ref, lifted, lambda b: dot(h[:, b * SPAN : (b + 1) * SPAN], w4_ref[0], TN), l_ref, m_ref)
    amplitudes(ast_ref, m_ref, amp_ref)
    first = skipped + dot3(invariants(amp_ref, gain_ref[0]), out_ref[0])
    f_ref[...] = first
    sf_ref[...] = pick_rows(tf_ref[...], first, TN)
    sn_ref[...] = pick_rows(tn_ref[...], first, TN)


def middle_kernel(f_ref, rf_ref, rn_ref, pf_ref, pn_ref, a_ref, b_ref):
    rows = jnp.concatenate([f_ref[...], rf_ref[...], rn_ref[...]], axis=0)
    a_ref[...] = pick_rows(pf_ref[...], rows, TN)
    b_ref[...] = pick_rows(pn_ref[...], rows, TN)


def slope_kernel(b_ref, db_ref, geo_ref, w1_ref, w2_ref, w3_ref, q_ref, *, layer):
    h, t = radial_hidden_pair(b_ref[...], db_ref[...], w1_ref[layer], w2_ref[layer], w3_ref[layer])
    q_ref[...] = stack_rows(t * geo_ref[4:5, :] + h * geo_ref[5:6, :])


def radial_kernel(b_ref, db_ref, geo_ref, w1_ref, w2_ref, w3_ref, w4_ref, r_ref, q_ref, *, layer):
    h, t = radial_hidden_pair(b_ref[...], db_ref[...], w1_ref[layer], w2_ref[layer], w3_ref[layer])
    q_ref[...] = stack_rows(t * geo_ref[4:5, :] + h * geo_ref[5:6, :])
    h = stack_rows(h * geo_ref[4:5, :])
    for b in range(BLOCKS):
        r_ref[span(b), :] = dot(h[:, b * SPAN : (b + 1) * SPAN], w4_ref[layer], TN)


def expand_kernel(q_ref, w4_ref, r_ref, *, layer):
    for b in range(BLOCKS):
        r_ref[span(b), :] = dot(q_ref[:, span(b)], w4_ref[layer], TN)


def second_kernel(
    f_ref, rf_ref, rn_ref, pf_ref, pn_ref, g_ref, gt_ref, ast_ref, r_ref, up_ref, skip_ref, out_ref, gain_ref,
    v_ref, ref_ref, one_ref, hid_ref, hidro_ref, ro_ref,
    e_ref, gmid_ref, gf_ref, gn_ref, z_ref, l_ref, m_ref, ga_ref,
    amp_ref, glift_ref,
):
    first = f_ref[...]
    ext = jnp.concatenate([first, rf_ref[...], rn_ref[...], pf_ref[...], pn_ref[...]], axis=0)
    up, skip, out, gain = up_ref[...], skip_ref[...], out_ref[1], gain_ref[1]
    lifted = pair_lanes(dot3(ext, up))
    messages(g_ref, lifted, lambda b: r_ref[span(b), :], l_ref, m_ref)
    amplitudes(ast_ref, m_ref, amp_ref)
    second = dot3(first, skip) + dot3(invariants(amp_ref, gain), out)
    hidden = lax.dot_general(hid_ref[...], second, NT, precision=highest, preferred_element_type=f32)
    act, slope = silu_pair(hidden)
    grad_second = dot3(slope, hidro_ref[...], TN)
    gm = dot3(grad_second, out, NT)
    amp_grads(amp_ref, gain, gm, ga_ref)
    for b in range(BLOCKS):
        grad = None
        for l in range(3):
            z = spread(ast_ref, ga_ref, b, l)
            z_ref[span(b), l * C : (l + 1) * C] = z
            term = r_ref[span(b), l * C : (l + 1) * C] * z
            grad = term if grad is None else grad + term
        glift_ref[span(b), :] = pair_lanes(grad)
    glift = halves(dot(gt_ref[...], glift_ref[...]))
    gext = dot3(glift, up, NT)
    gf_ref[...] = gext[128:192]
    gn_ref[...] = gext[192:256]
    gmid_ref[64:128, :] = gext[64:128]
    gmid_ref[0:64, :] = gext[0:64] + dot3(grad_second, skip, NT) + one_ref[...]
    onehot = (lax.broadcasted_iota(jnp.int32, (KINDS, OWN), 0).astype(f32) == v_ref[3:4, :]).astype(f32)

    def exact(a, b, dims=NN):
        return lax.dot_general(a, b, dims, precision=highest, preferred_element_type=f32)

    energy = exact(ref_ref[...], onehot)
    energy = energy + exact(jnp.broadcast_to(one_ref[...], (8, C)), first, NT)
    energy = energy + exact(ro_ref[...], act)
    e_ref[...] = energy[0:1]


def early_kernel(z_ref, q_ref, w4_ref, l_ref, m_ref, ga_ref, geo_ref, mask_ref, gv_ref, x_ref, gy_ref):
    for b in range(BLOCKS):
        slope = dot(q_ref[:, span(b)], w4_ref[1], TN)
        x = sum(z_ref[span(b), l * C : (l + 1) * C] * slope[:, l * C : (l + 1) * C] for l in range(3))
        x_ref[span(b), :] = pair_lanes(x * l_ref[span(b), :])
    angular_grads(m_ref, ga_ref, mask_ref, gy_ref)
    edge_forces(x_ref, gy_ref, geo_ref, gv_ref)


def back_middle_kernel(gmid_ref, rf_ref, rn_ref, pf_ref, pn_ref, own_ref, f_ref, n_ref):
    mid = gmid_ref[...] + (pick_rows(pf_ref[...], rf_ref[...]) + pick_rows(pn_ref[...], rn_ref[...]))
    own_ref[...] = mid[:64]
    f_ref[...] = mid[64:96]
    n_ref[...] = mid[96:128]


def late_kernel(
    own_ref, rf_ref, rn_ref, tf_ref, tn_ref, out_ref, gain_ref, amp_ref, ast_ref, dr_ref, l_ref, m_ref, geo_ref,
    mask_ref, dd_ref, early_ref, of_ref, pf_ref, pn_ref, qf_ref, qn_ref, ga_ref, gv_ref, x_ref, gy_ref,
):
    grad = own_ref[...] + (pick_rows(tf_ref[...], rf_ref[...]) + pick_rows(tn_ref[...], rn_ref[...]))
    amp_grads(amp_ref, gain_ref[0], dot3(grad, out_ref[0], NT), ga_ref)
    for b in range(BLOCKS):
        x = None
        for l in range(3):
            term = spread(ast_ref, ga_ref, b, l) * dr_ref[span(b), l * C : (l + 1) * C]
            x = term if x is None else x + term
        x_ref[span(b), :] = pair_lanes(x * l_ref[span(b), :])
    angular_grads(m_ref, ga_ref, mask_ref, gy_ref)
    edge_forces(x_ref, gy_ref, geo_ref, gv_ref)
    total = gv_ref[...] + early_ref[...]
    at = 0
    for ref in (of_ref, pf_ref, pn_ref, qf_ref, qn_ref):
        rows = ref.shape[1]
        ref[...] = pick_lanes(total, dd_ref[at : at + rows, :], NT)
        at += rows


def collect_plane_kernel(of_ref, pf_ref, pn_ref, rf_ref, rn_ref, tf_ref, tn_ref, o_ref, f_ref, n_ref):
    far, near, at = rf_ref[...], rn_ref[...], 0
    for have_ref, ref in ((of_ref, o_ref), (pf_ref, f_ref), (pn_ref, n_ref)):
        rows = ref.shape[1]
        back = pick_lanes(far, tf_ref[at : at + rows, :], NT) + pick_lanes(near, tn_ref[at : at + rows, :], NT)
        ref[...] = have_ref[...] + back
        at += rows


def collect_slab_kernel(v_ref, rf_ref, rn_ref, tf_ref, tn_ref, o_ref):
    back = pick_lanes(rf_ref[...], tf_ref[...], NT) + pick_lanes(rn_ref[...], tn_ref[...], NT)
    forces = -(v_ref[...] + back)
    for k in range(3):
        o_ref[0, k] = forces[k : k + 1]


def swap_slab_far(value):
    count = lax.axis_size("slab")
    pairs = [(i, i + 1) for i in range(1, count - 1, 2)]
    return lax.ppermute(value, "slab", pairs + [(b, a) for a, b in pairs])


def swap_slab_near(value):
    count = lax.axis_size("slab")
    return lax.ppermute(value, "slab", [(i, i ^ 1) for i in range(count)])


def swap_plane_far(value):
    count = lax.axis_size("plane")
    pairs = [(i, (i + 1) % count) for i in range(1, count, 2)]
    return lax.ppermute(value, "plane", pairs + [(b, a) for a, b in pairs])


def swap_plane_near(value):
    count = lax.axis_size("plane")
    return lax.ppermute(value, "plane", [(i, i ^ 1) for i in range(count)])


def both(swap_far, swap_near, far, near):
    return swap_far(far), swap_near(near)


def body(
    positions,
    species,
    slab_sends,
    plane_sends,
    edges,
    edge_count,
    embed_table,
    atom_ref,
    radial_one,
    radial_two,
    radial_three,
    radial_four,
    up_weight,
    skip_weight,
    out_weight,
    prod_weight,
    read_one,
    read_hidden,
    read_out,
):
    edge_mat = ((EDGES, C), f32)
    message_mat = ((3, EDGES, 2 * C), bf16)
    by_degree = ((EDGES, 3 * C), f32)
    edge_rows = ((8, EDGES), f32)
    amp_mat = ((9, OWN, C), f32)
    slab_rows = ((32, C), f32)
    plane_rows = ((64, C), f32)
    own_lanes = ((8, OWN), f32)
    slab_lanes = ((8, 32), f32)
    plane_lanes = ((8, 64), f32)

    with jax.named_scope("atoms_slab"):
        values, slab_t_far, slab_t_near, plane_t_far, plane_t_near, far, near = call(
            atoms_slab_kernel,
            [own_lanes, ((OWN, 32), bf16), ((OWN, 32), bf16), ((128, 64), bf16), ((128, 64), bf16), slab_lanes, slab_lanes],
            (jnp.transpose(positions, (0, 2, 1, 3)), species[0], slab_sends[0, 0], plane_sends[0, 0]),
            raw=True,
            name="atoms_slab",
        )
        far, near = both(swap_slab_far, swap_slab_near, far, near)
    with jax.named_scope("atoms_plane"):
        slab_far, slab_near, far, near = call(
            atoms_plane_kernel,
            [slab_lanes, slab_lanes, plane_lanes, plane_lanes],
            (values, far, near, plane_t_far, plane_t_near),
            name="atoms_plane",
        )
        edge_list, far, near = lax.optimization_barrier((edges[0, 0], far, near))
        far, near = both(swap_plane_far, swap_plane_near, far, near)
    with jax.named_scope("prepare"):
        square = ((C, C), f32)
        sender_n, sender_t, edge_t, mask, *prepared = call(
            prepare_kernel,
            [((EDGES, EXT), bf16), ((EXT, EDGES), bf16), ((EXT, EDGES), bf16), ((GROUP, EDGES), f32),
             ((2, 64, 32), bf16), ((2, 64, 192), bf16), ((2, 64, 192), bf16), ((2, 192, 3 * C), bf16),
             ((KINDS, 2 * C), bf16), ((KINDS, 3 * C), bf16), ((8, KINDS), f32), ((16, C), f32), ((16, C), f32),
             square, square, ((2, C, C), f32), ((2, 4, C), f32), ((1, C), f32), ((8, 16), f32)],
            (edge_list, radial_one, radial_two, radial_three, radial_four, embed_table, up_weight, skip_weight,
             atom_ref[None, :], jnp.transpose(read_hidden), read_out[None, :], out_weight, prod_weight,
             read_one[None, :], edge_count),
            raw=True,
            flops=1_000_000_000,
            name="prepare",
        )
        weights, (table, skip_table, ref_row, hid, hidro, up_second, skip_second, outs, gains, read_row, read_last) = (
            tuple(prepared[:4]), prepared[4:]
        )

    with jax.named_scope("first_layer"):
        (first, s_far, s_near, amp_first, lift_first, message_first, angular, basis, basis_slope, geo) = call(
            first_kernel,
            [plane_rows, slab_rows, slab_rows, amp_mat, edge_mat, message_mat,
             ((BLOCKS * STACK, SPAN), bf16), edge_rows, edge_rows, edge_rows],
            (values, slab_far, slab_near, far, near, edge_t, sender_n, mask, table, skip_table, *weights,
             gains, outs, slab_t_far, slab_t_near),
            name="first_layer",
        )
    with jax.named_scope("features_slab"):
        slab_far, slab_near = both(swap_slab_far, swap_slab_near, s_far, s_near)
    slope_first, = call(
        functools.partial(slope_kernel, layer=0), [((192, EDGES), bf16)], (basis, basis_slope, geo, *weights[:3]),
        flops=1_000_000_000, name="slope_first",
    )
    with jax.named_scope("features_plane"):
        far, near = call(
            middle_kernel, [plane_rows] * 2, (first, slab_far, slab_near, plane_t_far, plane_t_near), name="middle"
        )
        far, near, basis, geo = lax.optimization_barrier((far, near, basis, geo))
        far, near = both(swap_plane_far, swap_plane_near, far, near)
    radial_second, slope_second = call(
        functools.partial(radial_kernel, layer=1), [by_degree, ((192, EDGES), bf16)],
        (basis, basis_slope, geo, *weights), flops=1_000_000_000, name="radial_second",
    )
    with jax.named_scope("second_layer"):
        energies, gmid, far, near, z, lift_second, message_second, ga = call(
            second_kernel,
            [((1, OWN), f32), ((128, C), f32), plane_rows, plane_rows, by_degree, edge_mat, message_mat, amp_mat],
            (first, slab_far, slab_near, far, near, sender_n, sender_t, angular, radial_second,
             up_second, skip_second, outs, gains, values, ref_row, read_row, hid, hidro, read_last),
            scratch=[pltpu.VMEM((9, OWN, C), f32), pltpu.VMEM((EDGES, 2 * C), bf16)],
            name="second_layer",
        )
    with jax.named_scope("feature_grads_plane"):
        far, near, z, slope_first = lax.optimization_barrier((far, near, z, slope_first))
        far, near = both(swap_plane_far, swap_plane_near, far, near)
    early, = call(
        early_kernel, [edge_rows], (z, slope_second, weights[3], lift_second, message_second, ga, geo, mask),
        scratch=[pltpu.VMEM((EDGES, 2 * C), bf16), pltpu.VMEM((8, EDGES), f32)],
        flops=1_000_000_000, name="early_forces",
    )
    slope_first, = call(
        functools.partial(expand_kernel, layer=0), [by_degree], (slope_first, weights[3]),
        flops=1_000_000_000, name="expand_first",
    )
    with jax.named_scope("feature_grads_slab"):
        own, far, near = call(
            back_middle_kernel, [plane_rows, slab_rows, slab_rows], (gmid, far, near, plane_t_far, plane_t_near),
            name="back_middle",
        )
        far, near = both(swap_slab_far, swap_slab_near, far, near)
    with jax.named_scope("late_forces"):
        own, slab_far, slab_near, far, near = call(
            late_kernel,
            [own_lanes, slab_lanes, slab_lanes, plane_lanes, plane_lanes],
            (own, far, near, slab_t_far, slab_t_near, outs, gains, amp_first, angular, slope_first,
             lift_first, message_first, geo, mask, edge_t, early),
            scratch=[pltpu.VMEM((9, OWN, C), f32), pltpu.VMEM((8, EDGES), f32), pltpu.VMEM((EDGES, 2 * C), bf16),
                     pltpu.VMEM((8, EDGES), f32)],
            name="late_forces",
        )
    with jax.named_scope("position_grads_plane"):
        far, near = both(swap_plane_far, swap_plane_near, far, near)
        own, far, near = call(
            collect_plane_kernel, [own_lanes, slab_lanes, slab_lanes],
            (own, slab_far, slab_near, far, near, plane_t_far, plane_t_near), name="collect_plane",
        )
    with jax.named_scope("position_grads_slab"):
        far, near = both(swap_slab_far, swap_slab_near, far, near)
        forces, = call(
            collect_slab_kernel, [((1, 3, 1, OWN), f32)], (own, far, near, slab_t_far, slab_t_near), name="collect_slab"
        )
    return (energies[None], jnp.transpose(forces, (0, 2, 1, 3)))


def solution(mesh):
    in_specs = (
        P("slab", "plane", None, None),
        P("slab", "plane", None),
        P("slab", "plane", None, None),
        P("slab", "plane", None, None),
        P("slab", "plane", None, None),
        P("slab", "plane"),
    ) + (P(),) * 13
    out_specs = (P("slab", "plane", None), P("slab", "plane", None, None))
    return jax.shard_map(body, mesh=mesh, in_specs=in_specs, out_specs=out_specs, check_vma=False)
```

time: 158 us -> 95.9 us (0.61)
  Pallas kernels: 54.1 us -> 17 us
  other arithmetic: 15.2 us -> 0 us
  local copies, waits for them, and re-layouts: 15.4 us -> 1.09 us
  waiting for transfers between devices: 10.6 us -> 21.8 us
  starting transfers between devices: 58.9 us -> 53.8 us
    pallas_call x13 -> x14, Pallas kernels: 54.1 us -> 17 us  [call(): pl.pallas_call(kernel, out_shape=out_shape, in_specs=in_specs, out_specs=...]
    concatenate x11 -> x0, other arithmetic: 7.33 us -> none  [the longest x2 1.43 us: inner(): return jnp.concatenate([hi, hi, lo], axis=1)]
    convert_element_type x13 -> x0, other arithmetic: 5.16 us -> none  [the longest x1 1.18 us: body(): sender_n = (senders[:, None] == jnp.arange(EXT)[None, :]).astype(bf16)]
    ppermute x4, waiting for transfers between devices: 5.26 us -> 9.26 us  [swap_plane_near(): return lax.ppermute(value, 'plane', [(i, i ^ 1) for i in range(count)])]
    ppermute x4, starting transfers between devices: 11.4 us -> 7.68 us  [swap_plane_near(): return lax.ppermute(value, 'plane', [(i, i ^ 1) for i in range(count)])]
    slice x7 -> x0, local copies, waits for them, and re-layouts: 3.65 us -> none  [the longest x1 1.27 us: body(): grads[:, :128]]
    ppermute x4, waiting for transfers between devices: 1.21 us -> 4.78 us  [swap_slab_far(): return lax.ppermute(value, 'slab', pairs + [(b, a) for a, b in pairs])]
    ppermute x4, waiting for transfers between devices: 4.14 us -> 7.32 us  [swap_plane_far(): return lax.ppermute(value, 'plane', pairs + [(b, a) for a, b in pairs])]
  transfers between devices with their start and end apart: 16 -> 16, of which waited for: 3 -> 11; matrix products, arithmetic and copies ran while one was open for 11% -> 1% of each run, Pallas kernels for 14% -> 7%
where the time goes in v1:
time: 95.9 us; the launch traced here: 95.3 us
  starting transfers between devices  53.8 us (56%)
  waiting for transfers between devices  21.8 us (23%)
  Pallas kernels  17 us (18%)
  between operations  1.5 us (2%)
  local copies, waits for them, and re-layouts  1.09 us (1%)
    ppermute x4, starting transfers between devices, swap_plane_far(): return lax.ppermute(value, 'plane', pairs + [(b, a) for a, b in pairs])  20.1 us
    ppermute x4, starting transfers between devices, swap_slab_far(): return lax.ppermute(value, 'slab', pairs + [(b, a) for a, b in pairs])  18.3 us
    pallas_call x14, Pallas kernels, call(): pl.pallas_call(kernel, out_shape=out_shape, in_specs=in_specs, out_specs=...  17 us
    ppermute x4, waiting for transfers between devices, swap_plane_near(): return lax.ppermute(value, 'plane', [(i, i ^ 1) for i in range(count)])  9.26 us
    ppermute x4, starting transfers between devices, swap_plane_near(): return lax.ppermute(value, 'plane', [(i, i ^ 1) for i in range(count)])  7.68 us
    ppermute x4, starting transfers between devices, swap_slab_near(): return lax.ppermute(value, 'slab', [(i, i ^ 1) for i in range(count)])  7.68 us
    ppermute x4, waiting for transfers between devices, swap_plane_far(): return lax.ppermute(value, 'plane', pairs + [(b, a) for a, b in pairs])  7.32 us
    ppermute x4, waiting for transfers between devices, swap_slab_far(): return lax.ppermute(value, 'slab', pairs + [(b, a) for a, b in pairs])  4.78 us
  transfers between devices with their start and end apart: 16, of which 11 were waited for; matrix products, arithmetic and copies ran while one was open for 1% of the time, Pallas kernels for 7%

profile of v1, /device:TPU:2, one launch (start us, length us, event | category | flops | bytes accessed | tf_op | source)
XLA Modules:
  0.0 95.3 jit_solution(3048373872792220799)
XLA Ops:
  1.6 10.4 %collective-permute-start = (f32[8,32]{1,0:T(8,128)S(1)}, f32[8,32]{1,0:T(8,128)S(1)}, u32[]{:S(2)}, u32[]{:S(2)}) collective-permute-start(f32[8,32]{1,0:T(8,128)S(1)} %get-tuple-element.77), channel_id=1, source_target_pairs={{16,32},{48,64},{80,96},{112,128},{144,160},{176,192},{208,224},{2... | collective-permute-start | bytes 3080 | tf_op jit(solution)/shard_map/atoms_slab/ppermute | solution.py:581
  11.9 1.9 %collective-permute-start.1 = (f32[8,32]{1,0:T(8,128)S(1)}, f32[8,32]{1,0:T(8,128)S(1)}, u32[]{:S(2)}, u32[]{:S(2)}) collective-permute-start(f32[8,32]{1,0:T(8,128)S(1)} %get-tuple-element.78), channel_id=1, source_target_pairs={{0,16},{16,0},{32,48},{48,32},{64,80},{80,64},{96,112},{112,96},{1... | collective-permute-start | bytes 3080 | tf_op jit(solution)/shard_map/atoms_slab/ppermute | solution.py:586
  15.1 7.2 %collective-permute-start.2 = (f32[8,64]{1,0:T(8,128)S(1)}, f32[8,64]{1,0:T(8,128)S(1)}, u32[]{:S(2)}, u32[]{:S(2)}) collective-permute-start(f32[8,64]{1,0:T(8,128)S(1)} %get-tuple-element.85), channel_id=1, source_target_pairs={{1,2},{3,4},{5,6},{7,8},{9,10},{11,12},{13,14},{15,0},{2,1},{4,3},... | collective-permute-start | bytes 6152 | tf_op jit(solution)/shard_map/atoms_plane/ppermute | solution.py:592
  22.4 1.9 %collective-permute-start.3 = (f32[8,64]{1,0:T(8,128)S(1)}, f32[8,64]{1,0:T(8,128)S(1)}, u32[]{:S(2)}, u32[]{:S(2)}) collective-permute-start(f32[8,64]{1,0:T(8,128)S(1)} %get-tuple-element.86), channel_id=1, source_target_pairs={{0,1},{1,0},{2,3},{3,2},{4,5},{5,4},{6,7},{7,6},{8,9},{9,8},{10,11... | collective-permute-start | bytes 6152 | tf_op jit(solution)/shard_map/atoms_plane/ppermute | solution.py:597
  24.3 2.3 %prepare.1 = (bf16[1536,256]{1,0:T(8,128)(2,1)S(1)}, bf16[256,1536]{1,0:T(8,128)(2,1)S(1)}, bf16[256,1536]{1,0:T(8,128)(2,1)S(1)}, f32[16,1536]{1,0:T(8,128)S(1)...) custom-call(s32[2,1536]{1,0:T(2,128)} %bitcast.19, ...), custom_call_target="tpu_custom_call" | custom-call | flops 1000000000 | bytes 730536 | tf_op jit(solution)/shard_map/prepare/prepare/pallas_call | solution.py:127
  26.6 2.8 %collective-permute-done.3.qn_ref = f32[8,64]{1,0:T(8,128)S(1)} collective-permute-done((f32[8,64]{1,0:T(8,128)S(1)}, f32[8,64]{1,0:T(8,128)S(1)}, u32[]{:S(2)}, u32[]{:S(2)}) %collective-permute-start.3) | collective-permute-done | bytes 2080 | tf_op jit(solution)/shard_map/atoms_plane/ppermute | solution.py:597
  29.4 2.9 %first_layer.1 = (f32[64,128]{1,0:T(8,128)S(1)}, f32[32,128]{1,0:T(8,128)S(1)}, f32[32,128]{1,0:T(8,128)S(1)}, f32[9,64,128]{2,1,0:T(8,128)S(1)}, f32[1536,128]{...) custom-call(f32[8,64]{1,0:T(8,128)S(1)} %get-tuple-element.76.v_ref,, ...), custom_call_target="tpu_custom_call" | custom-call | bytes 2347008 | tf_op jit(solution)/shard_map/first_layer/first_layer/pallas_call | solution.py:127
  32.3 3.1 %collective-permute-start.4 = (f32[32,128]{1,0:T(8,128)S(1)}, f32[32,128]{1,0:T(8,128)S(1)}, u32[]{:S(2)}, u32[]{:S(2)}) collective-permute-start(f32[32,128]{1,0:T(8,128)S(1)} %get-tuple-element.102), channel_id=1, source_target_pairs={{16,32},{48,64},{80,96},{112,128},{144,160},{176,192},{208,224},{2... | collective-permute-start | bytes 49160 | tf_op jit(solution)/shard_map/features_slab/ppermute | solution.py:581
  35.4 1.9 %collective-permute-start.5 = (f32[32,128]{1,0:T(8,128)S(1)}, f32[32,128]{1,0:T(8,128)S(1)}, u32[]{:S(2)}, u32[]{:S(2)}) collective-permute-start(f32[32,128]{1,0:T(8,128)S(1)} %get-tuple-element.103), channel_id=1, source_target_pairs={{0,16},{16,0},{32,48},{48,32},{64,80},{80,64},{96,112},{112,96},{1... | collective-permute-start | bytes 49160 | tf_op jit(solution)/shard_map/features_slab/ppermute | solution.py:586
  37.4 1.0 %slope_first.1.q_ref = bf16[192,1536]{1,0:T(8,128)(2,1)S(1)} custom-call(f32[8,1536]{1,0:T(8,128)S(1)} %get-tuple-element.112.b_ref, f32[8,1536]{1,0:T(8,128)S(1)} %get-tuple-element.113.db_ref, f32[8,1536]{1,0:T(8,128)S(1)} %get-tuple-element.114.geo_ref, bf16[2,64,32]{2,1,0:T(8,128)(2,1)S(1)} %get-tuple-element.93.w1_ref, ...), custom_call_target="tpu_custom_call" | custom-call | flops 1000000000 | bytes 253952 | tf_op jit(solution)/shard_map/slope_first/pallas_call | solution.py:127
  38.4 1.1 %collective-permute-done.4.rf_ref = f32[32,128]{1,0:T(8,128)S(1)} collective-permute-done((f32[32,128]{1,0:T(8,128)S(1)}, f32[32,128]{1,0:T(8,128)S(1)}, u32[]{:S(2)}, u32[]{:S(2)}) %collective-permute-start.4) | collective-permute-done | bytes 16416 | tf_op jit(solution)/shard_map/features_slab/ppermute | solution.py:581
  39.7 3.4 %collective-permute-start.6 = (f32[64,128]{1,0:T(8,128)S(1)}, f32[64,128]{1,0:T(8,128)S(1)}, u32[]{:S(2)}, u32[]{:S(2)}) collective-permute-start(f32[64,128]{1,0:T(8,128)S(1)} %get-tuple-element.108), channel_id=1, source_target_pairs={{1,2},{3,4},{5,6},{7,8},{9,10},{11,12},{13,14},{15,0},{2,1},{4,3},... | collective-permute-start | bytes 98312 | tf_op jit(solution)/shard_map/features_plane/ppermute | solution.py:592
  43.1 1.9 %collective-permute-start.7 = (f32[64,128]{1,0:T(8,128)S(1)}, f32[64,128]{1,0:T(8,128)S(1)}, u32[]{:S(2)}, u32[]{:S(2)}) collective-permute-start(f32[64,128]{1,0:T(8,128)S(1)} %get-tuple-element.109), channel_id=1, source_target_pairs={{0,1},{1,0},{2,3},{3,2},{4,5},{5,4},{6,7},{7,6},{8,9},{9,8},{10,11... | collective-permute-start | bytes 98312 | tf_op jit(solution)/shard_map/features_plane/ppermute | solution.py:597
  45.0 1.4 %radial_second.1 = (f32[1536,384]{1,0:T(8,128)S(1)}, bf16[192,1536]{1,0:T(8,128)(2,1)S(1)}) custom-call(f32[8,1536]{1,0:T(8,128)S(1)} %get-tuple-element.112.b_ref, f32[8,1536]{1,0:T(8,128)S(1)} %get-tuple-element.113.db_ref, f32[8,1536]{1,0:T(8,128)S(1)} %get-tuple-element.114.geo_ref, bf16[2,64,32]{2,1,0:T(8,128)(2,1)S(1)} %get-tuple-element.93.w1_ref, ...), custom_call_target="tpu_custom_call" | custom-call | flops 1000000000 | bytes 548864 | tf_op jit(solution)/shard_map/radial_second/pallas_call | solution.py:127
  46.5 2.7 %collective-permute-done.6.pf_ref = f32[64,128]{1,0:T(8,128)S(1)} collective-permute-done((f32[64,128]{1,0:T(8,128)S(1)}, f32[64,128]{1,0:T(8,128)S(1)}, u32[]{:S(2)}, u32[]{:S(2)}) %collective-permute-start.6) | collective-permute-done | bytes 32800 | tf_op jit(solution)/shard_map/features_plane/ppermute | solution.py:592
  49.2 1.2 %collective-permute-done.7.pn_ref = f32[64,128]{1,0:T(8,128)S(1)} collective-permute-done((f32[64,128]{1,0:T(8,128)S(1)}, f32[64,128]{1,0:T(8,128)S(1)}, u32[]{:S(2)}, u32[]{:S(2)}) %collective-permute-start.7) | collective-permute-done | bytes 32800 | tf_op jit(solution)/shard_map/features_plane/ppermute | solution.py:597
  50.4 3.7 %second_layer.1 = (f32[1,64]{1,0:T(1,128)S(1)}, f32[128,128]{1,0:T(8,128)S(1)}, f32[64,128]{1,0:T(8,128)S(1)}, f32[64,128]{1,0:T(8,128)S(1)}, f32[1536,384]{1,0:...) custom-call(f32[64,128]{1,0:T(8,128)S(1)} %get-tuple-element.101.f_ref, ...), custom_call_target="tpu_custom_call" | custom-call | bytes 5679104 | tf_op jit(solution)/shard_map/second_layer/second_layer/pallas_call | solution.py:127
  54.1 6.0 %collective-permute-start.8 = (f32[64,128]{1,0:T(8,128)S(1)}, f32[64,128]{1,0:T(8,128)S(1)}, u32[]{:S(2)}, u32[]{:S(2)}) collective-permute-start(f32[64,128]{1,0:T(8,128)S(1)} %get-tuple-element.128), channel_id=1, source_target_pairs={{1,2},{3,4},{5,6},{7,8},{9,10},{11,12},{13,14},{15,0},{2,1},{4,3},... | collective-permute-start | bytes 98312 | tf_op jit(solution)/shard_map/feature_grads_plane/ppermute | solution.py:592
  60.2 1.9 %collective-permute-start.9 = (f32[64,128]{1,0:T(8,128)S(1)}, f32[64,128]{1,0:T(8,128)S(1)}, u32[]{:S(2)}, u32[]{:S(2)}) collective-permute-start(f32[64,128]{1,0:T(8,128)S(1)} %get-tuple-element.129), channel_id=1, source_target_pairs={{0,1},{1,0},{2,3},{3,2},{4,5},{5,4},{6,7},{7,6},{8,9},{9,8},{10,11... | collective-permute-start | bytes 98312 | tf_op jit(solution)/shard_map/feature_grads_plane/ppermute | solution.py:597
  63.6 3.9 %collective-permute-done.9.rn_ref = f32[64,128]{1,0:T(8,128)S(1)} collective-permute-done((f32[64,128]{1,0:T(8,128)S(1)}, f32[64,128]{1,0:T(8,128)S(1)}, u32[]{:S(2)}, u32[]{:S(2)}) %collective-permute-start.9) | collective-permute-done | bytes 32800 | tf_op jit(solution)/shard_map/feature_grads_plane/ppermute | solution.py:597
  67.7 1.9 %collective-permute-start.10 = (f32[32,128]{1,0:T(8,128)S(1)}, f32[32,128]{1,0:T(8,128)S(1)}, u32[]{:S(2)}, u32[]{:S(2)}) collective-permute-start(f32[32,128]{1,0:T(8,128)S(1)} %get-tuple-element.131), channel_id=1, source_target_pairs={{16,32},{48,64},{80,96},{112,128},{144,160},{176,192},{208,224},{2... | collective-permute-start | bytes 49160 | tf_op jit(solution)/shard_map/feature_grads_slab/ppermute | solution.py:581
  69.6 1.9 %collective-permute-start.11 = (f32[32,128]{1,0:T(8,128)S(1)}, f32[32,128]{1,0:T(8,128)S(1)}, u32[]{:S(2)}, u32[]{:S(2)}) collective-permute-start(f32[32,128]{1,0:T(8,128)S(1)} %get-tuple-element.132), channel_id=1, source_target_pairs={{0,16},{16,0},{32,48},{48,32},{64,80},{80,64},{96,112},{112,96},{1... | collective-permute-start | bytes 49160 | tf_op jit(solution)/shard_map/feature_grads_slab/ppermute | solution.py:586
  71.5 1.3 %early_forces.1.early_ref = f32[8,1536]{1,0:T(8,128)S(1)} custom-call(f32[1536,384]{1,0:T(8,128)S(1)} %get-tuple-element.137.z_ref, bf16[192,1536]{1,0:T(8,128)(2,1)S(1)} %get-tuple-element.138.q_ref, bf16[2,192,384]{2,1,0:T(8,128)(2,1)S(1)} %get-tuple-element.96.w4_ref, f32[1536,128]{1,0:T(8,128)S(1)} %get-tuple-element.139.l_ref, ...), custom_call_target="tpu_custom_call" | custom-call | flops 1000000000 | bytes 6832128 | tf_op jit(solution)/shard_map/early_forces/pallas_call | solution.py:127
  72.8 2.0 %collective-permute-done.10.rf_ref = f32[32,128]{1,0:T(8,128)S(1)} collective-permute-done((f32[32,128]{1,0:T(8,128)S(1)}, f32[32,128]{1,0:T(8,128)S(1)}, u32[]{:S(2)}, u32[]{:S(2)}) %collective-permute-start.10) | collective-permute-done | bytes 16416 | tf_op jit(solution)/shard_map/feature_grads_slab/ppermute | solution.py:581
  74.8 2.1 %late_forces.1 = (f32[8,64]{1,0:T(8,128)S(1)}, f32[8,32]{1,0:T(8,128)S(1)}, f32[8,32]{1,0:T(8,128)S(1)}, f32[8,64]{1,0:T(8,128)S(1)}, f32[8,64]{1,0:T(8,128)S(1)}) custom-call(f32[64,128]{1,0:T(8,128)S(1)} %get-tuple-element.130.own_ref, f32[32,128]{1,0:T(8,128)S(1)} %collective-permute-done.10.rf_ref, f32[32,128]{1,0:T(8,128)S(1)} %collective-permute-done.11.rn_ref, ...), custom_call_target="tpu_custom_call" | custom-call | bytes 8318976 | tf_op jit(solution)/shard_map/late_forces/late_forces/pallas_call | solution.py:127
  76.9 3.4 %collective-permute-start.12 = (f32[8,64]{1,0:T(8,128)S(1)}, f32[8,64]{1,0:T(8,128)S(1)}, u32[]{:S(2)}, u32[]{:S(2)}) collective-permute-start(f32[8,64]{1,0:T(8,128)S(1)} %get-tuple-element.145), channel_id=1, source_target_pairs={{1,2},{3,4},{5,6},{7,8},{9,10},{11,12},{13,14},{15,0},{2,1},{4,3},... | collective-permute-start | bytes 6152 | tf_op jit(solution)/shard_map/position_grads_plane/ppermute | solution.py:592
  80.4 1.9 %collective-permute-start.13 = (f32[8,64]{1,0:T(8,128)S(1)}, f32[8,64]{1,0:T(8,128)S(1)}, u32[]{:S(2)}, u32[]{:S(2)}) collective-permute-start(f32[8,64]{1,0:T(8,128)S(1)} %get-tuple-element.146), channel_id=1, source_target_pairs={{0,1},{1,0},{2,3},{3,2},{4,5},{5,4},{6,7},{7,6},{8,9},{9,8},{10,11... | collective-permute-start | bytes 6152 | tf_op jit(solution)/shard_map/position_grads_plane/ppermute | solution.py:597
  82.3 3.7 %collective-permute-done.12.rf_ref = f32[8,64]{1,0:T(8,128)S(1)} collective-permute-done((f32[8,64]{1,0:T(8,128)S(1)}, f32[8,64]{1,0:T(8,128)S(1)}, u32[]{:S(2)}, u32[]{:S(2)}) %collective-permute-start.12) | collective-permute-done | bytes 2080 | tf_op jit(solution)/shard_map/position_grads_plane/ppermute | solution.py:592
  86.0 1.3 %collective-permute-done.13.rn_ref = f32[8,64]{1,0:T(8,128)S(1)} collective-permute-done((f32[8,64]{1,0:T(8,128)S(1)}, f32[8,64]{1,0:T(8,128)S(1)}, u32[]{:S(2)}, u32[]{:S(2)}) %collective-permute-start.13) | collective-permute-done | bytes 2080 | tf_op jit(solution)/shard_map/position_grads_plane/ppermute | solution.py:597
  87.5 2.9 %collective-permute-start.14 = (f32[8,32]{1,0:T(8,128)S(1)}, f32[8,32]{1,0:T(8,128)S(1)}, u32[]{:S(2)}, u32[]{:S(2)}) collective-permute-start(f32[8,32]{1,0:T(8,128)S(1)} %get-tuple-element.148), channel_id=1, source_target_pairs={{16,32},{48,64},{80,96},{112,128},{144,160},{176,192},{208,224},{2... | collective-permute-start | bytes 3080 | tf_op jit(solution)/shard_map/position_grads_slab/ppermute | solution.py:581
  90.4 1.9 %collective-permute-start.15 = (f32[8,32]{1,0:T(8,128)S(1)}, f32[8,32]{1,0:T(8,128)S(1)}, u32[]{:S(2)}, u32[]{:S(2)}) collective-permute-start(f32[8,32]{1,0:T(8,128)S(1)} %get-tuple-element.149), channel_id=1, source_target_pairs={{0,16},{16,0},{32,48},{48,32},{64,80},{80,64},{96,112},{112,96},{1... | collective-permute-start | bytes 3080 | tf_op jit(solution)/shard_map/position_grads_slab/ppermute | solution.py:586
  92.9 1.7 %collective-permute-done.14.rf_ref = f32[8,32]{1,0:T(8,128)S(1)} collective-permute-done((f32[8,32]{1,0:T(8,128)S(1)}, f32[8,32]{1,0:T(8,128)S(1)}, u32[]{:S(2)}, u32[]{:S(2)}) %collective-permute-start.14) | collective-permute-done | bytes 1056 | tf_op jit(solution)/shard_map/position_grads_slab/ppermute | solution.py:581
  (16 shorter events, 4.8 us)
Async XLA Ops:
  1.6 12.9 %collective-permute-start = (f32[8,32]{1,0:T(8,128)S(1)}, f32[8,32]{1,0:T(8,128)S(1)}, u32[]{:S(2)}, u32[]{:S(2)}) collective-permute-start(f32[8,32]{1,0:T(8,128)S(1)} %get-tuple-element.77), channel_id=1, source_target_pairs={{16,32},{48,64},{80,96},{112,128},{144,160},{176,192},{208,224},{2... | collective-permute-start | bytes 3080 | tf_op jit(solution)/shard_map/atoms_slab/ppermute | solution.py:581
  11.9 3.1 %collective-permute-start.1 = (f32[8,32]{1,0:T(8,128)S(1)}, f32[8,32]{1,0:T(8,128)S(1)}, u32[]{:S(2)}, u32[]{:S(2)}) collective-permute-start(f32[8,32]{1,0:T(8,128)S(1)} %get-tuple-element.78), channel_id=1, source_target_pairs={{0,16},{16,0},{32,48},{48,32},{64,80},{80,64},{96,112},{112,96},{1... | collective-permute-start | bytes 3080 | tf_op jit(solution)/shard_map/atoms_slab/ppermute | solution.py:586
  15.1 11.5 %collective-permute-start.2 = (f32[8,64]{1,0:T(8,128)S(1)}, f32[8,64]{1,0:T(8,128)S(1)}, u32[]{:S(2)}, u32[]{:S(2)}) collective-permute-start(f32[8,64]{1,0:T(8,128)S(1)} %get-tuple-element.85), channel_id=1, source_target_pairs={{1,2},{3,4},{5,6},{7,8},{9,10},{11,12},{13,14},{15,0},{2,1},{4,3},... | collective-permute-start | bytes 6152 | tf_op jit(solution)/shard_map/atoms_plane/ppermute | solution.py:592
  22.4 7.0 %collective-permute-start.3 = (f32[8,64]{1,0:T(8,128)S(1)}, f32[8,64]{1,0:T(8,128)S(1)}, u32[]{:S(2)}, u32[]{:S(2)}) collective-permute-start(f32[8,64]{1,0:T(8,128)S(1)} %get-tuple-element.86), channel_id=1, source_target_pairs={{0,1},{1,0},{2,3},{3,2},{4,5},{5,4},{6,7},{7,6},{8,9},{9,8},{10,11... | collective-permute-start | bytes 6152 | tf_op jit(solution)/shard_map/atoms_plane/ppermute | solution.py:597
  32.3 7.2 %collective-permute-start.4 = (f32[32,128]{1,0:T(8,128)S(1)}, f32[32,128]{1,0:T(8,128)S(1)}, u32[]{:S(2)}, u32[]{:S(2)}) collective-permute-start(f32[32,128]{1,0:T(8,128)S(1)} %get-tuple-element.102), channel_id=1, source_target_pairs={{16,32},{48,64},{80,96},{112,128},{144,160},{176,192},{208,224},{2... | collective-permute-start | bytes 49160 | tf_op jit(solution)/shard_map/features_slab/ppermute | solution.py:581
  35.4 4.0 %collective-permute-start.5 = (f32[32,128]{1,0:T(8,128)S(1)}, f32[32,128]{1,0:T(8,128)S(1)}, u32[]{:S(2)}, u32[]{:S(2)}) collective-permute-start(f32[32,128]{1,0:T(8,128)S(1)} %get-tuple-element.103), channel_id=1, source_target_pairs={{0,16},{16,0},{32,48},{48,32},{64,80},{80,64},{96,112},{112,96},{1... | collective-permute-start | bytes 49160 | tf_op jit(solution)/shard_map/features_slab/ppermute | solution.py:586
  39.7 9.5 %collective-permute-start.6 = (f32[64,128]{1,0:T(8,128)S(1)}, f32[64,128]{1,0:T(8,128)S(1)}, u32[]{:S(2)}, u32[]{:S(2)}) collective-permute-start(f32[64,128]{1,0:T(8,128)S(1)} %get-tuple-element.108), channel_id=1, source_target_pairs={{1,2},{3,4},{5,6},{7,8},{9,10},{11,12},{13,14},{15,0},{2,1},{4,3},... | collective-permute-start | bytes 98312 | tf_op jit(solution)/shard_map/features_plane/ppermute | solution.py:592
  43.1 7.3 %collective-permute-start.7 = (f32[64,128]{1,0:T(8,128)S(1)}, f32[64,128]{1,0:T(8,128)S(1)}, u32[]{:S(2)}, u32[]{:S(2)}) collective-permute-start(f32[64,128]{1,0:T(8,128)S(1)} %get-tuple-element.109), channel_id=1, source_target_pairs={{0,1},{1,0},{2,3},{3,2},{4,5},{5,4},{6,7},{7,6},{8,9},{9,8},{10,11... | collective-permute-start | bytes 98312 | tf_op jit(solution)/shard_map/features_plane/ppermute | solution.py:597
  54.1 9.4 %collective-permute-start.8 = (f32[64,128]{1,0:T(8,128)S(1)}, f32[64,128]{1,0:T(8,128)S(1)}, u32[]{:S(2)}, u32[]{:S(2)}) collective-permute-start(f32[64,128]{1,0:T(8,128)S(1)} %get-tuple-element.128), channel_id=1, source_target_pairs={{1,2},{3,4},{5,6},{7,8},{9,10},{11,12},{13,14},{15,0},{2,1},{4,3},... | collective-permute-start | bytes 98312 | tf_op jit(solution)/shard_map/feature_grads_plane/ppermute | solution.py:592
  60.2 7.3 %collective-permute-start.9 = (f32[64,128]{1,0:T(8,128)S(1)}, f32[64,128]{1,0:T(8,128)S(1)}, u32[]{:S(2)}, u32[]{:S(2)}) collective-permute-start(f32[64,128]{1,0:T(8,128)S(1)} %get-tuple-element.129), channel_id=1, source_target_pairs={{0,1},{1,0},{2,3},{3,2},{4,5},{5,4},{6,7},{7,6},{8,9},{9,8},{10,11... | collective-permute-start | bytes 98312 | tf_op jit(solution)/shard_map/feature_grads_plane/ppermute | solution.py:597
  67.7 7.2 %collective-permute-start.10 = (f32[32,128]{1,0:T(8,128)S(1)}, f32[32,128]{1,0:T(8,128)S(1)}, u32[]{:S(2)}, u32[]{:S(2)}) collective-permute-start(f32[32,128]{1,0:T(8,128)S(1)} %get-tuple-element.131), channel_id=1, source_target_pairs={{16,32},{48,64},{80,96},{112,128},{144,160},{176,192},{208,224},{2... | collective-permute-start | bytes 49160 | tf_op jit(solution)/shard_map/feature_grads_slab/ppermute | solution.py:581
  69.6 5.2 %collective-permute-start.11 = (f32[32,128]{1,0:T(8,128)S(1)}, f32[32,128]{1,0:T(8,128)S(1)}, u32[]{:S(2)}, u32[]{:S(2)}) collective-permute-start(f32[32,128]{1,0:T(8,128)S(1)} %get-tuple-element.132), channel_id=1, source_target_pairs={{0,16},{16,0},{32,48},{48,32},{64,80},{80,64},{96,112},{112,96},{1... | collective-permute-start | bytes 49160 | tf_op jit(solution)/shard_map/feature_grads_slab/ppermute | solution.py:586
  76.9 9.1 %collective-permute-start.12 = (f32[8,64]{1,0:T(8,128)S(1)}, f32[8,64]{1,0:T(8,128)S(1)}, u32[]{:S(2)}, u32[]{:S(2)}) collective-permute-start(f32[8,64]{1,0:T(8,128)S(1)} %get-tuple-element.145), channel_id=1, source_target_pairs={{1,2},{3,4},{5,6},{7,8},{9,10},{11,12},{13,14},{15,0},{2,1},{4,3},... | collective-permute-start | bytes 6152 | tf_op jit(solution)/shard_map/position_grads_plane/ppermute | solution.py:592
  80.4 7.0 %collective-permute-start.13 = (f32[8,64]{1,0:T(8,128)S(1)}, f32[8,64]{1,0:T(8,128)S(1)}, u32[]{:S(2)}, u32[]{:S(2)}) collective-permute-start(f32[8,64]{1,0:T(8,128)S(1)} %get-tuple-element.146), channel_id=1, source_target_pairs={{0,1},{1,0},{2,3},{3,2},{4,5},{5,4},{6,7},{7,6},{8,9},{9,8},{10,11... | collective-permute-start | bytes 6152 | tf_op jit(solution)/shard_map/position_grads_plane/ppermute | solution.py:597
  87.5 7.0 %collective-permute-start.14 = (f32[8,32]{1,0:T(8,128)S(1)}, f32[8,32]{1,0:T(8,128)S(1)}, u32[]{:S(2)}, u32[]{:S(2)}) collective-permute-start(f32[8,32]{1,0:T(8,128)S(1)} %get-tuple-element.148), channel_id=1, source_target_pairs={{16,32},{48,64},{80,96},{112,128},{144,160},{176,192},{208,224},{2... | collective-permute-start | bytes 3080 | tf_op jit(solution)/shard_map/position_grads_slab/ppermute | solution.py:581
  90.4 4.1 %collective-permute-start.15 = (f32[8,32]{1,0:T(8,128)S(1)}, f32[8,32]{1,0:T(8,128)S(1)}, u32[]{:S(2)}, u32[]{:S(2)}) collective-permute-start(f32[8,32]{1,0:T(8,128)S(1)} %get-tuple-element.149), channel_id=1, source_target_pairs={{0,16},{16,0},{32,48},{48,32},{64,80},{80,64},{96,112},{112,96},{1... | collective-permute-start | bytes 3080 | tf_op jit(solution)/shard_map/position_grads_slab/ppermute | solution.py:586

commit v2 on v1

--- a/solution.py
+++ b/solution.py
@@ -29,6 +29,8 @@
 FIRST_LM = (0, 1, 4)
 STACK_AT = (0, 48, 192)
 STACK = 432
+TURNED_AT = (0, 128, 384)
+TURNED = 640
 R3, R5, R15 = 3.0**0.5, 5.0**0.5, 15.0**0.5
 
 NN = (((1,), (0,)), ((), ()))
@@ -42,6 +44,10 @@
 
 def dot3(a, b, dims=NN):
     return lax.dot_general(a, b, dims, precision=lax.Precision.HIGH, preferred_element_type=f32)
+
+
+def exact(a, b, dims=NN):
+    return lax.dot_general(a, b, dims, precision=highest, preferred_element_type=f32)
 
 
 def split(x):
@@ -194,8 +200,8 @@
 def prepare_kernel(
     edge_ref, one_ref, two_ref, three_ref, four_ref, embed_ref, up_ref, skip_ref, atom_ref, hid_ref, ro_ref,
     out_ref, gain_ref, read_ref, count_ref,
-    g_ref, gt_ref, dd_ref, mask_ref, w1_ref, w2_ref, w3_ref, w4_ref, table_ref, skips_ref, refs_ref, hidt_ref, hidro_ref,
-    up1_ref, skip1_ref, outs_ref, gains_ref, reads_ref, ros_ref,
+    g_ref, gt_ref, dd_ref, mask_ref, w1_ref, w2_ref, w3_ref, w4_ref, table_ref, skips_ref, skipups_ref, refs_ref,
+    from_first_ref, from_mix_ref, from_first_ro_ref, from_mix_ro_ref, outup_ref, out0_ref, gains_ref, reads_ref, ros_ref,
 ):
     per_atom = count_ref[0, 0] // OWN
     senders = jnp.broadcast_to(edge_ref[0:1, :], (8, EDGES))
@@ -234,24 +240,43 @@
         w4_ref[t] = jnp.concatenate([hi, hi, lo], axis=0)
     embed = embed_ref[...]
     kinds = embed.shape[0]
-    table_ref[...] = jnp.zeros(table_ref.shape, bf16)
-    skips_ref[...] = jnp.zeros(skips_ref.shape, bf16)
-    exact = functools.partial(
-        lax.dot_general, dimension_numbers=NN, precision=highest, preferred_element_type=f32
-    )
+    for ref in (table_ref, skips_ref, skipups_ref):
+        ref[...] = jnp.zeros(ref.shape, bf16)
     table_ref[0:kinds, :] = pair_lanes(exact(embed, up_ref[0]))
-    hi, mid, lo = three(exact(embed, skip_ref[0]))
-    skips_ref[0:kinds, :] = jnp.concatenate([hi, mid, lo], axis=1).astype(bf16)
+    skipped = exact(embed, skip_ref[0])
+    for ref, values in ((skips_ref, skipped), (skipups_ref, exact(skipped, up_ref[1]))):
+        hi, mid, lo = three(values)
+        ref[0:kinds, :] = jnp.concatenate([hi, mid, lo], axis=1).astype(bf16)
     refs_ref[...] = jnp.zeros(refs_ref.shape, f32)
     refs_ref[0:1, 0:kinds] = atom_ref[...]
-    hidt_ref[...] = hid_ref[...]
-    hidro_ref[...] = hid_ref[...] * jnp.transpose(jnp.broadcast_to(ro_ref[...], (C, ro_ref.shape[1])))
-    up1_ref[...] = up_ref[1]
-    skip1_ref[...] = skip_ref[1]
-    outs_ref[...] = out_ref[...]
+    last = jnp.transpose(jnp.broadcast_to(ro_ref[...], (C, ro_ref.shape[1])))
+    from_first = exact(hid_ref[...], skip_ref[1], NT)
+    from_mix = exact(hid_ref[...], out_ref[1], NT)
+    from_first_ref[...] = from_first
+    from_mix_ref[...] = from_mix
+    from_first_ro_ref[...] = from_first * last
+    from_mix_ro_ref[...] = from_mix * last
+    outup_ref[...] = exact(out_ref[0], up_ref[1])
+    out0_ref[...] = out_ref[0]
     gains_ref[...] = gain_ref[...]
     reads_ref[...] = read_ref[...]
     ros_ref[...] = jnp.broadcast_to(ro_ref[...], ros_ref.shape)
+
+
+def kinds_of(row):
+    kinds = lax.broadcasted_iota(jnp.int32, (KINDS, row.shape[1]), 0).astype(f32) == row
+    return kinds.astype(f32)
+
+
+def near_atoms_kernel(v_ref, pf_ref, pn_ref, dd_ref, table_ref, vector_ref, lifted_ref):
+    vector, at = None, 0
+    for ref in (v_ref, pf_ref, pn_ref):
+        rows = ref.shape[1]
+        piece = pick_lanes(ref[...], dd_ref[at : at + rows, :])
+        vector = piece if vector is None else vector + piece
+        lifted_ref[at : at + rows, :] = dot(kinds_of(ref[3:4, :]).astype(bf16), table_ref[...], TN).astype(bf16)
+        at += rows
+    vector_ref[...] = vector
 
 
 def geometry(v, valid, b_ref, db_ref, geo_ref):
@@ -375,12 +400,10 @@
     )
 
 
-def spread(ast_ref, ga_ref, b, l):
-    n = LMS[l]
+def spread(turned_ref, ga_ref, b, l):
     hi, lo = split(group_grads(ga_ref, b, l))
-    return dot(
-        ast_ref[pl.ds(b * STACK + STACK_AT[l], 48 * n), :], jnp.concatenate([hi, hi, lo], axis=0), TN
-    )
+    angular = turned_ref[span(b), TURNED_AT[l] : TURNED_AT[l] + 48 * LMS[l]]
+    return dot(angular, jnp.concatenate([hi, hi, lo], axis=0))
 
 
 def angular_grads(m_ref, ga_ref, mask_ref, gy_ref):
@@ -416,26 +439,18 @@
 
 
 def first_kernel(
-    v_ref, pf_ref, pn_ref, qf_ref, qn_ref, dd_ref, g_ref, mask_ref, table_ref, skip_ref, w1_ref, w2_ref, w3_ref, w4_ref,
-    gain_ref, out_ref, tf_ref, tn_ref,
-    f_ref, sf_ref, sn_ref, amp_ref, l_ref, m_ref, ast_ref, b_ref, db_ref, geo_ref,
+    v_ref, vector_ref, lifted_ref, qf_ref, qn_ref, dd_ref, g_ref, mask_ref, table_ref, skip_ref, w1_ref, w2_ref, w3_ref, w4_ref,
+    gain_ref, outup_ref, tf_ref, tn_ref,
+    f_ref, sf_ref, sn_ref, mix_ref, amp_ref, l_ref, m_ref, ast_ref, b_ref, db_ref, geo_ref,
 ):
     step = (2 * odd("plane") - 1).astype(f32) * (CELLS_Y * cell_side)
-    parts = (v_ref[...], pf_ref[...], pn_ref[...], shifted(qf_ref[...], 1, step), shifted(qn_ref[...], 1, -step))
+    far, near = shifted(qf_ref[...], 1, step), shifted(qn_ref[...], 1, -step)
     valid = jnp.sum(mask_ref[...], axis=0, keepdims=True) > 0.5
-    vector, lifted, at = None, [], 0
-    for part in parts:
-        rows = part.shape[1]
-        piece = pick_lanes(part, dd_ref[at : at + rows, :])
-        vector = piece if vector is None else vector + piece
-        kinds = lax.broadcasted_iota(jnp.int32, (KINDS, rows), 0).astype(f32) == part[3:4]
-        kinds = kinds.astype(f32).astype(bf16)
-        if at == 0:
-            o = dot(kinds, skip_ref[...], TN)
-            skipped = (o[:, :C] + o[:, C : 2 * C]) + o[:, 2 * C :]
-        lifted.append(dot(kinds, table_ref[...], TN))
-        at += rows
-    lifted = jnp.concatenate(lifted, axis=0).astype(bf16)
+    vector = vector_ref[...] + (pick_lanes(far, dd_ref[128:192, :]) + pick_lanes(near, dd_ref[192:256, :]))
+    lifted = [dot(kinds_of(part[3:4]).astype(bf16), table_ref[...], TN).astype(bf16) for part in (far, near)]
+    lifted = jnp.concatenate([lifted_ref[...]] + lifted, axis=0)
+    o = dot(kinds_of(v_ref[3:4, :]).astype(bf16), skip_ref[...], TN)
+    skipped = (o[:, :C] + o[:, C : 2 * C]) + o[:, 2 * C :]
     geometry(vector, valid, b_ref, db_ref, geo_ref)
     h = stack_rows(radial_hidden(b_ref[...], w1_ref[0], w2_ref[0], w3_ref[0]) * geo_ref[4:5, :])
     rows = angular_rows(geo_ref[0:3, :])
@@ -448,10 +463,20 @@
             ast_ref[pl.ds(b * STACK + STACK_AT[l], 48 * LMS[l]), :] = stack_rows(a)
     messages(g_ref, lifted, lambda b: dot(h[:, b * SPAN : (b + 1) * SPAN], w4_ref[0], TN), l_ref, m_ref)
     amplitudes(ast_ref, m_ref, amp_ref)
-    first = skipped + dot3(invariants(amp_ref, gain_ref[0]), out_ref[0])
-    f_ref[...] = first
-    sf_ref[...] = pick_rows(tf_ref[...], first, TN)
-    sn_ref[...] = pick_rows(tn_ref[...], first, TN)
+    mix = invariants(amp_ref, gain_ref[0])
+    mix_ref[...] = mix
+    lifted = skipped + dot3(mix, outup_ref[...])
+    f_ref[...] = lifted
+    sf_ref[...] = pick_rows(tf_ref[...], lifted, TN)
+    sn_ref[...] = pick_rows(tn_ref[...], lifted, TN)
+
+
+def own_terms_kernel(v_ref, mix_ref, skip_ref, out0_ref, ref_ref, one_ref, from_first_ref, hid_ref, e_ref):
+    kinds = kinds_of(v_ref[3:4, :])
+    o = dot(kinds.astype(bf16), skip_ref[...], TN)
+    first = ((o[:, :C] + o[:, C : 2 * C]) + o[:, 2 * C :]) + exact(mix_ref[...], out0_ref[...])
+    hid_ref[...] = exact(from_first_ref[...], first, NT)
+    e_ref[...] = exact(ref_ref[...], kinds) + exact(jnp.broadcast_to(one_ref[...], (8, C)), first, NT)
 
 
 def middle_kernel(f_ref, rf_ref, rn_ref, pf_ref, pn_ref, a_ref, b_ref):
@@ -478,56 +503,69 @@
         r_ref[span(b), :] = dot(q_ref[:, span(b)], w4_ref[layer], TN)
 
 
+def beside_features_kernel(
+    b_ref, db_ref, geo_ref, w1_ref, w2_ref, w3_ref, w4_ref, v_ref, mix_ref, skip_ref, out0_ref, ref_ref, one_ref, from_first_ref,
+    ast_ref, r_ref, second_q_ref, first_q_ref, hid_ref, e_ref, turned_ref,
+):
+    for b in range(BLOCKS):
+        for l in range(3):
+            rows = ast_ref[pl.ds(b * STACK + STACK_AT[l], 48 * LMS[l]), :]
+            turned_ref[span(b), TURNED_AT[l] : TURNED_AT[l] + 48 * LMS[l]] = jnp.transpose(rows)
+    slope_kernel(b_ref, db_ref, geo_ref, w1_ref, w2_ref, w3_ref, first_q_ref, layer=0)
+    radial_kernel(b_ref, db_ref, geo_ref, w1_ref, w2_ref, w3_ref, w4_ref, r_ref, second_q_ref, layer=1)
+    own_terms_kernel(v_ref, mix_ref, skip_ref, out0_ref, ref_ref, one_ref, from_first_ref, hid_ref, e_ref)
+
+
 def second_kernel(
-    f_ref, rf_ref, rn_ref, pf_ref, pn_ref, g_ref, gt_ref, ast_ref, r_ref, up_ref, skip_ref, out_ref, gain_ref,
-    v_ref, ref_ref, one_ref, hid_ref, hidro_ref, ro_ref,
-    e_ref, gmid_ref, gf_ref, gn_ref, z_ref, l_ref, m_ref, ga_ref,
+    f_ref, rf_ref, rn_ref, pf_ref, pn_ref, g_ref, gt_ref, ast_ref, turned_ref, r_ref, gain_ref, hid_ref, from_mix_ref, from_mix_ro_ref,
+    act_ref, slope_ref, gmid_ref, gf_ref, gn_ref, l_ref, m_ref, ga_ref,
     amp_ref, glift_ref,
 ):
-    first = f_ref[...]
-    ext = jnp.concatenate([first, rf_ref[...], rn_ref[...], pf_ref[...], pn_ref[...]], axis=0)
-    up, skip, out, gain = up_ref[...], skip_ref[...], out_ref[1], gain_ref[1]
-    lifted = pair_lanes(dot3(ext, up))
+    lifted = pair_lanes(
+        jnp.concatenate([f_ref[...], rf_ref[...], rn_ref[...], pf_ref[...], pn_ref[...]], axis=0)
+    )
     messages(g_ref, lifted, lambda b: r_ref[span(b), :], l_ref, m_ref)
     amplitudes(ast_ref, m_ref, amp_ref)
-    second = dot3(first, skip) + dot3(invariants(amp_ref, gain), out)
-    hidden = lax.dot_general(hid_ref[...], second, NT, precision=highest, preferred_element_type=f32)
-    act, slope = silu_pair(hidden)
-    grad_second = dot3(slope, hidro_ref[...], TN)
-    gm = dot3(grad_second, out, NT)
-    amp_grads(amp_ref, gain, gm, ga_ref)
+    gain = gain_ref[1]
+    act, slope = silu_pair(hid_ref[...] + exact(from_mix_ref[...], invariants(amp_ref, gain), NT))
+    act_ref[...] = act
+    slope_ref[...] = slope
+    amp_grads(amp_ref, gain, dot3(slope, from_mix_ro_ref[...], TN), ga_ref)
     for b in range(BLOCKS):
         grad = None
         for l in range(3):
-            z = spread(ast_ref, ga_ref, b, l)
-            z_ref[span(b), l * C : (l + 1) * C] = z
-            term = r_ref[span(b), l * C : (l + 1) * C] * z
+            term = r_ref[span(b), l * C : (l + 1) * C] * spread(turned_ref, ga_ref, b, l)
             grad = term if grad is None else grad + term
         glift_ref[span(b), :] = pair_lanes(grad)
     glift = halves(dot(gt_ref[...], glift_ref[...]))
-    gext = dot3(glift, up, NT)
-    gf_ref[...] = gext[128:192]
-    gn_ref[...] = gext[192:256]
-    gmid_ref[64:128, :] = gext[64:128]
-    gmid_ref[0:64, :] = gext[0:64] + dot3(grad_second, skip, NT) + one_ref[...]
-    onehot = (lax.broadcasted_iota(jnp.int32, (KINDS, OWN), 0).astype(f32) == v_ref[3:4, :]).astype(f32)
-
-    def exact(a, b, dims=NN):
-        return lax.dot_general(a, b, dims, precision=highest, preferred_element_type=f32)
-
-    energy = exact(ref_ref[...], onehot)
-    energy = energy + exact(jnp.broadcast_to(one_ref[...], (8, C)), first, NT)
-    energy = energy + exact(ro_ref[...], act)
-    e_ref[...] = energy[0:1]
-
-
-def early_kernel(z_ref, q_ref, w4_ref, l_ref, m_ref, ga_ref, geo_ref, mask_ref, gv_ref, x_ref, gy_ref):
+    gmid_ref[...] = glift[0:128]
+    gf_ref[...] = glift[128:192]
+    gn_ref[...] = glift[192:256]
+
+
+def own_grads_kernel(act_ref, slope_ref, e0_ref, ro_ref, from_first_ro_ref, one_ref, out0_ref, e_ref, gm_ref):
+    e_ref[...] = (e0_ref[...] + exact(ro_ref[...], act_ref[...]))[0:1]
+    grad = dot3(slope_ref[...], from_first_ro_ref[...], TN) + one_ref[...]
+    gm_ref[...] = dot3(grad, out0_ref[...], NT)
+
+
+def early_kernel(turned_ref, q_ref, w4_ref, l_ref, m_ref, ga_ref, geo_ref, mask_ref, gv_ref, x_ref, gy_ref):
     for b in range(BLOCKS):
         slope = dot(q_ref[:, span(b)], w4_ref[1], TN)
-        x = sum(z_ref[span(b), l * C : (l + 1) * C] * slope[:, l * C : (l + 1) * C] for l in range(3))
+        x = sum(spread(turned_ref, ga_ref, b, l) * slope[:, l * C : (l + 1) * C] for l in range(3))
         x_ref[span(b), :] = pair_lanes(x * l_ref[span(b), :])
     angular_grads(m_ref, ga_ref, mask_ref, gy_ref)
     edge_forces(x_ref, gy_ref, geo_ref, gv_ref)
+
+
+def beside_grads_kernel(
+    turned_ref, second_q_ref, w4_ref, l_ref, m_ref, ga_ref, geo_ref, mask_ref, first_q_ref,
+    act_ref, slope_ref, e0_ref, ro_ref, from_first_ro_ref, one_ref, out0_ref,
+    gv_ref, dr_ref, e_ref, gm_ref, x_ref, gy_ref,
+):
+    early_kernel(turned_ref, second_q_ref, w4_ref, l_ref, m_ref, ga_ref, geo_ref, mask_ref, gv_ref, x_ref, gy_ref)
+    expand_kernel(first_q_ref, w4_ref, dr_ref, layer=0)
+    own_grads_kernel(act_ref, slope_ref, e0_ref, ro_ref, from_first_ro_ref, one_ref, out0_ref, e_ref, gm_ref)
 
 
 def back_middle_kernel(gmid_ref, rf_ref, rn_ref, pf_ref, pn_ref, own_ref, f_ref, n_ref):
@@ -538,15 +576,15 @@
 
 
 def late_kernel(
-    own_ref, rf_ref, rn_ref, tf_ref, tn_ref, out_ref, gain_ref, amp_ref, ast_ref, dr_ref, l_ref, m_ref, geo_ref,
+    own_ref, rf_ref, rn_ref, tf_ref, tn_ref, gm_ref, outup_ref, gain_ref, amp_ref, turned_ref, dr_ref, l_ref, m_ref, geo_ref,
     mask_ref, dd_ref, early_ref, of_ref, pf_ref, pn_ref, qf_ref, qn_ref, ga_ref, gv_ref, x_ref, gy_ref,
 ):
     grad = own_ref[...] + (pick_rows(tf_ref[...], rf_ref[...]) + pick_rows(tn_ref[...], rn_ref[...]))
-    amp_grads(amp_ref, gain_ref[0], dot3(grad, out_ref[0], NT), ga_ref)
+    amp_grads(amp_ref, gain_ref[0], gm_ref[...] + dot3(grad, outup_ref[...], NT), ga_ref)
     for b in range(BLOCKS):
         x = None
         for l in range(3):
-            term = spread(ast_ref, ga_ref, b, l) * dr_ref[span(b), l * C : (l + 1) * C]
+            term = spread(turned_ref, ga_ref, b, l) * dr_ref[span(b), l * C : (l + 1) * C]
             x = term if x is None else x + term
         x_ref[span(b), :] = pair_lanes(x * l_ref[span(b), :])
     angular_grads(m_ref, ga_ref, mask_ref, gy_ref)
@@ -652,13 +690,12 @@
         edge_list, far, near = lax.optimization_barrier((edges[0, 0], far, near))
         far, near = both(swap_plane_far, swap_plane_near, far, near)
     with jax.named_scope("prepare"):
-        square = ((C, C), f32)
         sender_n, sender_t, edge_t, mask, *prepared = call(
             prepare_kernel,
             [((EDGES, EXT), bf16), ((EXT, EDGES), bf16), ((EXT, EDGES), bf16), ((GROUP, EDGES), f32),
              ((2, 64, 32), bf16), ((2, 64, 192), bf16), ((2, 64, 192), bf16), ((2, 192, 3 * C), bf16),
-             ((KINDS, 2 * C), bf16), ((KINDS, 3 * C), bf16), ((8, KINDS), f32), ((16, C), f32), ((16, C), f32),
-             square, square, ((2, C, C), f32), ((2, 4, C), f32), ((1, C), f32), ((8, 16), f32)],
+             ((KINDS, 2 * C), bf16), ((KINDS, 3 * C), bf16), ((KINDS, 3 * C), bf16), ((8, KINDS), f32),
+             *[((16, C), f32)] * 4, ((C, C), f32), ((C, C), f32), ((2, 4, C), f32), ((1, C), f32), ((8, 16), f32)],
             (edge_list, radial_one, radial_two, radial_three, radial_four, embed_table, up_weight, skip_weight,
              atom_ref[None, :], jnp.transpose(read_hidden), read_out[None, :], out_weight, prod_weight,
              read_one[None, :], edge_count),
@@ -666,57 +703,62 @@
             flops=1_000_000_000,
             name="prepare",
         )
-        weights, (table, skip_table, ref_row, hid, hidro, up_second, skip_second, outs, gains, read_row, read_last) = (
-            tuple(prepared[:4]), prepared[4:]
-        )
-
+        weights = tuple(prepared[:4])
+        (table, skip_table, skip_up_table, ref_row, from_first, from_mix, from_first_ro, from_mix_ro, out_up, out_first,
+         gains, read_row, read_last) = prepared[4:]
+        vector, lifted = call(
+            near_atoms_kernel, [edge_rows, ((128, 2 * C), bf16)], (values, slab_far, slab_near, edge_t, table),
+            flops=1_000_000_000, name="near_atoms",
+        )
+
+    hidden_mat = ((16, OWN), f32)
     with jax.named_scope("first_layer"):
-        (first, s_far, s_near, amp_first, lift_first, message_first, angular, basis, basis_slope, geo) = call(
+        far, near, vector, lifted = lax.optimization_barrier((far, near, vector, lifted))
+        (first, s_far, s_near, mix, amp_first, lift_first, message_first, angular, basis, basis_slope, geo) = call(
             first_kernel,
-            [plane_rows, slab_rows, slab_rows, amp_mat, edge_mat, message_mat,
+            [plane_rows, slab_rows, slab_rows, plane_rows, amp_mat, edge_mat, message_mat,
              ((BLOCKS * STACK, SPAN), bf16), edge_rows, edge_rows, edge_rows],
-            (values, slab_far, slab_near, far, near, edge_t, sender_n, mask, table, skip_table, *weights,
-             gains, outs, slab_t_far, slab_t_near),
+            (values, vector, lifted, far, near, edge_t, sender_n, mask, table, skip_up_table, *weights,
+             gains, out_up, slab_t_far, slab_t_near),
             name="first_layer",
         )
     with jax.named_scope("features_slab"):
         slab_far, slab_near = both(swap_slab_far, swap_slab_near, s_far, s_near)
-    slope_first, = call(
-        functools.partial(slope_kernel, layer=0), [((192, EDGES), bf16)], (basis, basis_slope, geo, *weights[:3]),
-        flops=1_000_000_000, name="slope_first",
-    )
     with jax.named_scope("features_plane"):
         far, near = call(
             middle_kernel, [plane_rows] * 2, (first, slab_far, slab_near, plane_t_far, plane_t_near), name="middle"
         )
-        far, near, basis, geo = lax.optimization_barrier((far, near, basis, geo))
+        far, near, basis, geo, mix = lax.optimization_barrier((far, near, basis, geo, mix))
         far, near = both(swap_plane_far, swap_plane_near, far, near)
-    radial_second, slope_second = call(
-        functools.partial(radial_kernel, layer=1), [by_degree, ((192, EDGES), bf16)],
-        (basis, basis_slope, geo, *weights), flops=1_000_000_000, name="radial_second",
+    radial_second, slope_second, slope_first, hidden, energies, turned = call(
+        beside_features_kernel,
+        [by_degree, ((192, EDGES), bf16), ((192, EDGES), bf16), hidden_mat, own_lanes, ((EDGES, TURNED), bf16)],
+        (basis, basis_slope, geo, *weights, values, mix, skip_table, out_first, ref_row, read_row, from_first,
+         angular),
+        flops=1_000_000_000, name="beside_features",
     )
     with jax.named_scope("second_layer"):
-        energies, gmid, far, near, z, lift_second, message_second, ga = call(
+        act, slope, gmid, far, near, lift_second, message_second, ga = call(
             second_kernel,
-            [((1, OWN), f32), ((128, C), f32), plane_rows, plane_rows, by_degree, edge_mat, message_mat, amp_mat],
-            (first, slab_far, slab_near, far, near, sender_n, sender_t, angular, radial_second,
-             up_second, skip_second, outs, gains, values, ref_row, read_row, hid, hidro, read_last),
+            [hidden_mat, hidden_mat, ((128, C), f32), plane_rows, plane_rows, edge_mat, message_mat, amp_mat],
+            (first, slab_far, slab_near, far, near, sender_n, sender_t, angular, turned, radial_second, gains, hidden, from_mix,
+             from_mix_ro),
             scratch=[pltpu.VMEM((9, OWN, C), f32), pltpu.VMEM((EDGES, 2 * C), bf16)],
             name="second_layer",
         )
     with jax.named_scope("feature_grads_plane"):
-        far, near, z, slope_first = lax.optimization_barrier((far, near, z, slope_first))
+        far, near, ga = lax.optimization_barrier((far, near, ga))
         far, near = both(swap_plane_far, swap_plane_near, far, near)
-    early, = call(
-        early_kernel, [edge_rows], (z, slope_second, weights[3], lift_second, message_second, ga, geo, mask),
+    early, slope_first, energies, own_grads = call(
+        beside_grads_kernel,
+        [edge_rows, by_degree, ((1, OWN), f32), plane_rows],
+        (turned, slope_second, weights[3], lift_second, message_second, ga, geo, mask, slope_first,
+         act, slope, energies, read_last, from_first_ro, read_row, out_first),
         scratch=[pltpu.VMEM((EDGES, 2 * C), bf16), pltpu.VMEM((8, EDGES), f32)],
-        flops=1_000_000_000, name="early_forces",
-    )
-    slope_first, = call(
-        functools.partial(expand_kernel, layer=0), [by_degree], (slope_first, weights[3]),
-        flops=1_000_000_000, name="expand_first",
+        flops=1_000_000_000, name="beside_grads",
     )
     with jax.named_scope("feature_grads_slab"):
+        far, near, early = lax.optimization_barrier((far, near, early))
         own, far, near = call(
             back_middle_kernel, [plane_rows, slab_rows, slab_rows], (gmid, far, near, plane_t_far, plane_t_near),
             name="back_middle",
@@ -726,7 +768,7 @@
         own, slab_far, slab_near, far, near = call(
             late_kernel,
             [own_lanes, slab_lanes, slab_lanes, plane_lanes, plane_lanes],
-            (own, far, near, slab_t_far, slab_t_near, outs, gains, amp_first, angular, slope_first,
+            (own, far, near, slab_t_far, slab_t_near, own_grads, out_up, gains, amp_first, turned, slope_first,
              lift_first, message_first, geo, mask, edge_t, early),
             scratch=[pltpu.VMEM((9, OWN, C), f32), pltpu.VMEM((8, EDGES), f32), pltpu.VMEM((EDGES, 2 * C), bf16),
                      pltpu.VMEM((8, EDGES), f32)],

time: 95.9 us -> 95 us (level)
  waiting for transfers between devices: 21.8 us -> 20.5 us
    ppermute x4, waiting for transfers between devices: 7.32 us -> 4.02 us  [swap_plane_far(): return lax.ppermute(value, 'plane', pairs + [(b, a) for a, b in pairs])]
    ppermute x4, waiting for transfers between devices: 4.78 us -> 7.22 us  [swap_slab_far(): return lax.ppermute(value, 'slab', pairs + [(b, a) for a, b in pairs])]
    pallas_call x14 -> x13, Pallas kernels: 17 us -> 17 us  [call(): pl.pallas_call(kernel, out_shape=out_shape, in_specs=in_specs, out_specs=...]
  transfers between devices with their start and end apart: 16 -> 16, of which waited for: 11 -> 10; matrix products, arithmetic and copies ran while one was open for 1% -> 1% of each run, Pallas kernels for 7% -> 8%
where the time goes in v2:
time: 95 us; the launch traced here: 94.4 us
  starting transfers between devices  54.3 us (57%)
  waiting for transfers between devices  20.5 us (22%)
  Pallas kernels  17 us (18%)
  between operations  1.52 us (2%)
  local copies, waits for them, and re-layouts  1.09 us (1%)
    ppermute x4, starting transfers between devices, swap_plane_far(): return lax.ppermute(value, 'plane', pairs + [(b, a) for a, b in pairs])  20.7 us
    ppermute x4, starting transfers between devices, swap_slab_far(): return lax.ppermute(value, 'slab', pairs + [(b, a) for a, b in pairs])  18.2 us
    pallas_call x13, Pallas kernels, call(): pl.pallas_call(kernel, out_shape=out_shape, in_specs=in_specs, out_specs=...  17 us
    ppermute x4, waiting for transfers between devices, swap_plane_near(): return lax.ppermute(value, 'plane', [(i, i ^ 1) for i in range(count)])  8.83 us
    ppermute x4, starting transfers between devices, swap_plane_near(): return lax.ppermute(value, 'plane', [(i, i ^ 1) for i in range(count)])  7.73 us
    ppermute x4, starting transfers between devices, swap_slab_near(): return lax.ppermute(value, 'slab', [(i, i ^ 1) for i in range(count)])  7.68 us
    ppermute x4, waiting for transfers between devices, swap_slab_far(): return lax.ppermute(value, 'slab', pairs + [(b, a) for a, b in pairs])  7.22 us
    ppermute x4, waiting for transfers between devices, swap_plane_far(): return lax.ppermute(value, 'plane', pairs + [(b, a) for a, b in pairs])  4.02 us
  transfers between devices with their start and end apart: 16, of which 10 were waited for; matrix products, arithmetic and copies ran while one was open for 1% of the time, Pallas kernels for 8%

profile of v2, /device:TPU:2, one launch (start us, length us, event | category | flops | bytes accessed | tf_op | source)
XLA Modules:
  0.0 94.4 jit_solution(13839403977020665594)
XLA Ops:
  0.6 0.9 atoms_slab.1
  1.6 10.4 %collective-permute-start = (f32[8,32]{1,0:T(8,128)S(1)}, f32[8,32]{1,0:T(8,128)S(1)}, u32[]{:S(2)}, u32[]{:S(2)}) collective-permute-start(f32[8,32]{1,0:T(8,128)S(1)} %get-tuple-element.97), channel_id=1, source_target_pairs={{16,32},{48,64},{80,96},{112,128},{144,160},{176,192},{208,224},{2... | collective-permute-start | bytes 3080 | tf_op jit(solution)/shard_map/atoms_slab/ppermute | solution.py:619
  11.9 1.9 %collective-permute-start.1 = (f32[8,32]{1,0:T(8,128)S(1)}, f32[8,32]{1,0:T(8,128)S(1)}, u32[]{:S(2)}, u32[]{:S(2)}) collective-permute-start(f32[8,32]{1,0:T(8,128)S(1)} %get-tuple-element.98), channel_id=1, source_target_pairs={{0,16},{16,0},{32,48},{48,32},{64,80},{80,64},{96,112},{112,96},{1... | collective-permute-start | bytes 3080 | tf_op jit(solution)/shard_map/atoms_slab/ppermute | solution.py:624
  15.1 7.2 %collective-permute-start.2 = (f32[8,64]{1,0:T(8,128)S(1)}, f32[8,64]{1,0:T(8,128)S(1)}, u32[]{:S(2)}, u32[]{:S(2)}) collective-permute-start(f32[8,64]{1,0:T(8,128)S(1)} %get-tuple-element.103), channel_id=1, source_target_pairs={{1,2},{3,4},{5,6},{7,8},{9,10},{11,12},{13,14},{15,0},{2,1},{4,3},... | collective-permute-start | bytes 6152 | tf_op jit(solution)/shard_map/atoms_plane/ppermute | solution.py:630
  22.4 1.9 %collective-permute-start.3 = (f32[8,64]{1,0:T(8,128)S(1)}, f32[8,64]{1,0:T(8,128)S(1)}, u32[]{:S(2)}, u32[]{:S(2)}) collective-permute-start(f32[8,64]{1,0:T(8,128)S(1)} %get-tuple-element.104), channel_id=1, source_target_pairs={{0,1},{1,0},{2,3},{3,2},{4,5},{5,4},{6,7},{7,6},{8,9},{9,8},{10,11... | collective-permute-start | bytes 6152 | tf_op jit(solution)/shard_map/atoms_plane/ppermute | solution.py:635
  24.3 2.5 %prepare.1 = (bf16[1536,256]{1,0:T(8,128)(2,1)S(1)}, bf16[256,1536]{1,0:T(8,128)(2,1)S(1)}, bf16[256,1536]{1,0:T(8,128)(2,1)S(1)}, f32[16,1536]{1,0:T(8,128)S(1)...) custom-call(s32[2,1536]{1,0:T(2,128)} %bitcast.19, ...), custom_call_target="tpu_custom_call" | custom-call | flops 1000000000 | bytes 730536 | tf_op jit(solution)/shard_map/prepare/prepare/pallas_call | solution.py:133
  27.1 2.3 %collective-permute-done.3.qn_ref = f32[8,64]{1,0:T(8,128)S(1)} collective-permute-done((f32[8,64]{1,0:T(8,128)S(1)}, f32[8,64]{1,0:T(8,128)S(1)}, u32[]{:S(2)}, u32[]{:S(2)}) %collective-permute-start.3) | collective-permute-done | bytes 2080 | tf_op jit(solution)/shard_map/atoms_plane/ppermute | solution.py:635
  29.4 2.8 %first_layer.1 = (f32[64,128]{1,0:T(8,128)S(1)}, f32[32,128]{1,0:T(8,128)S(1)}, f32[32,128]{1,0:T(8,128)S(1)}, f32[64,128]{1,0:T(8,128)S(1)}, f32[9,64,128]{2,1,...) custom-call(f32[8,64]{1,0:T(8,128)S(1)} %get-tuple-element.96.v_ref,, ...), custom_call_target="tpu_custom_call" | custom-call | bytes 2394112 | tf_op jit(solution)/shard_map/first_layer/first_layer/pallas_call | solution.py:133
  32.2 3.1 %collective-permute-start.4 = (f32[32,128]{1,0:T(8,128)S(1)}, f32[32,128]{1,0:T(8,128)S(1)}, u32[]{:S(2)}, u32[]{:S(2)}) collective-permute-start(f32[32,128]{1,0:T(8,128)S(1)} %get-tuple-element.128), channel_id=1, source_target_pairs={{16,32},{48,64},{80,96},{112,128},{144,160},{176,192},{208,224},{2... | collective-permute-start | bytes 49160 | tf_op jit(solution)/shard_map/features_slab/ppermute | solution.py:619
  35.4 1.9 %collective-permute-start.5 = (f32[32,128]{1,0:T(8,128)S(1)}, f32[32,128]{1,0:T(8,128)S(1)}, u32[]{:S(2)}, u32[]{:S(2)}) collective-permute-start(f32[32,128]{1,0:T(8,128)S(1)} %get-tuple-element.129), channel_id=1, source_target_pairs={{0,16},{16,0},{32,48},{48,32},{64,80},{80,64},{96,112},{112,96},{1... | collective-permute-start | bytes 49160 | tf_op jit(solution)/shard_map/features_slab/ppermute | solution.py:624
  37.3 2.1 %collective-permute-done.4.rf_ref = f32[32,128]{1,0:T(8,128)S(1)} collective-permute-done((f32[32,128]{1,0:T(8,128)S(1)}, f32[32,128]{1,0:T(8,128)S(1)}, u32[]{:S(2)}, u32[]{:S(2)}) %collective-permute-start.4) | collective-permute-done | bytes 16416 | tf_op jit(solution)/shard_map/features_slab/ppermute | solution.py:619
  39.6 4.0 %collective-permute-start.6 = (f32[64,128]{1,0:T(8,128)S(1)}, f32[64,128]{1,0:T(8,128)S(1)}, u32[]{:S(2)}, u32[]{:S(2)}) collective-permute-start(f32[64,128]{1,0:T(8,128)S(1)} %get-tuple-element.147), channel_id=1, source_target_pairs={{1,2},{3,4},{5,6},{7,8},{9,10},{11,12},{13,14},{15,0},{2,1},{4,3},... | collective-permute-start | bytes 98312 | tf_op jit(solution)/shard_map/features_plane/ppermute | solution.py:630
  43.6 1.9 %collective-permute-start.7 = (f32[64,128]{1,0:T(8,128)S(1)}, f32[64,128]{1,0:T(8,128)S(1)}, u32[]{:S(2)}, u32[]{:S(2)}) collective-permute-start(f32[64,128]{1,0:T(8,128)S(1)} %get-tuple-element.148), channel_id=1, source_target_pairs={{0,1},{1,0},{2,3},{3,2},{4,5},{5,4},{6,7},{7,6},{8,9},{9,8},{10,11... | collective-permute-start | bytes 98312 | tf_op jit(solution)/shard_map/features_plane/ppermute | solution.py:635
  45.5 2.7 %beside_features.1 = (f32[1536,384]{1,0:T(8,128)S(1)}, bf16[192,1536]{1,0:T(8,128)(2,1)S(1)}, bf16[192,1536]{1,0:T(8,128)(2,1)S(1)}, f32[16,64]{1,0:T(8,128)S(1)...) custom-call(f32[8,1536]{1,0:T(8,128)S(1)} %get-tuple-element.135.b_ref, f32[8,1536]{1,0:T(8,128)S(1)} %get-tuple-element.136.db_ref, ...), custom_call_target="tpu_custom_call" | custom-call | flops 1000000000 | bytes 2061824 | tf_op jit(solution)/shard_map/beside_features/pallas_call | solution.py:133
  48.2 0.8 collective-permute-done.6.pf_ref
  49.0 1.8 %collective-permute-done.7.pn_ref = f32[64,128]{1,0:T(8,128)S(1)} collective-permute-done((f32[64,128]{1,0:T(8,128)S(1)}, f32[64,128]{1,0:T(8,128)S(1)}, u32[]{:S(2)}, u32[]{:S(2)}) %collective-permute-start.7) | collective-permute-done | bytes 32800 | tf_op jit(solution)/shard_map/features_plane/ppermute | solution.py:635
  50.9 2.4 %second_layer.1 = (f32[16,64]{1,0:T(8,128)S(1)}, f32[16,64]{1,0:T(8,128)S(1)}, f32[128,128]{1,0:T(8,128)S(1)}, f32[64,128]{1,0:T(8,128)S(1)}, f32[64,128]{1,0:T(...) custom-call(f32[64,128]{1,0:T(8,128)S(1)} %get-tuple-element.127.f_ref, ...), custom_call_target="tpu_custom_call" | custom-call | bytes 7380992 | tf_op jit(solution)/shard_map/second_layer/second_layer/pallas_call | solution.py:133
  53.3 5.5 %collective-permute-start.8 = (f32[64,128]{1,0:T(8,128)S(1)}, f32[64,128]{1,0:T(8,128)S(1)}, u32[]{:S(2)}, u32[]{:S(2)}) collective-permute-start(f32[64,128]{1,0:T(8,128)S(1)} %get-tuple-element.168), channel_id=1, source_target_pairs={{1,2},{3,4},{5,6},{7,8},{9,10},{11,12},{13,14},{15,0},{2,1},{4,3},... | collective-permute-start | bytes 98312 | tf_op jit(solution)/shard_map/feature_grads_plane/ppermute | solution.py:630
  58.8 2.0 %collective-permute-start.9 = (f32[64,128]{1,0:T(8,128)S(1)}, f32[64,128]{1,0:T(8,128)S(1)}, u32[]{:S(2)}, u32[]{:S(2)}) collective-permute-start(f32[64,128]{1,0:T(8,128)S(1)} %get-tuple-element.169), channel_id=1, source_target_pairs={{0,1},{1,0},{2,3},{3,2},{4,5},{5,4},{6,7},{7,6},{8,9},{9,8},{10,11... | collective-permute-start | bytes 98312 | tf_op jit(solution)/shard_map/feature_grads_plane/ppermute | solution.py:635
  60.8 2.5 %beside_grads.1 = (f32[8,1536]{1,0:T(8,128)S(1)}, f32[1536,384]{1,0:T(8,128)S(1)}, f32[1,64]{1,0:T(1,128)S(1)}, f32[64,128]{1,0:T(8,128)S(1)}) custom-call(bf16[1536,640]{1,0:T(8,128)(2,1)S(1)} %get-tuple-element.145.turned_ref, bf16[192,1536]{1,0:T(8,128)(2,1)S(1)} %get-tuple-element.146.second_q_ref, bf16[2,192,384]{2,1,0:T(8,128)(2,1)S(1)} %get-tuple-element.122.w4_ref, ...), custom_call_target="tpu_custom_call" | custom-call | flops 1000000000 | bytes 7113728 | tf_op jit(solution)/shard_map/beside_grads/pallas_call | solution.py:133
  63.3 2.9 %collective-permute-done.9.rn_ref = f32[64,128]{1,0:T(8,128)S(1)} collective-permute-done((f32[64,128]{1,0:T(8,128)S(1)}, f32[64,128]{1,0:T(8,128)S(1)}, u32[]{:S(2)}, u32[]{:S(2)}) %collective-permute-start.9) | collective-permute-done | bytes 32800 | tf_op jit(solution)/shard_map/feature_grads_plane/ppermute | solution.py:635
  66.3 1.9 %collective-permute-start.10 = (f32[32,128]{1,0:T(8,128)S(1)}, f32[32,128]{1,0:T(8,128)S(1)}, u32[]{:S(2)}, u32[]{:S(2)}) collective-permute-start(f32[32,128]{1,0:T(8,128)S(1)} %get-tuple-element.174), channel_id=1, source_target_pairs={{16,32},{48,64},{80,96},{112,128},{144,160},{176,192},{208,224},{2... | collective-permute-start | bytes 49160 | tf_op jit(solution)/shard_map/feature_grads_slab/ppermute | solution.py:619
  68.3 1.9 %collective-permute-start.11 = (f32[32,128]{1,0:T(8,128)S(1)}, f32[32,128]{1,0:T(8,128)S(1)}, u32[]{:S(2)}, u32[]{:S(2)}) collective-permute-start(f32[32,128]{1,0:T(8,128)S(1)} %get-tuple-element.175), channel_id=1, source_target_pairs={{0,16},{16,0},{32,48},{48,32},{64,80},{80,64},{96,112},{112,96},{1... | collective-permute-start | bytes 49160 | tf_op jit(solution)/shard_map/feature_grads_slab/ppermute | solution.py:624
  70.2 3.3 %collective-permute-done.10.rf_ref = f32[32,128]{1,0:T(8,128)S(1)} collective-permute-done((f32[32,128]{1,0:T(8,128)S(1)}, f32[32,128]{1,0:T(8,128)S(1)}, u32[]{:S(2)}, u32[]{:S(2)}) %collective-permute-start.10) | collective-permute-done | bytes 16416 | tf_op jit(solution)/shard_map/feature_grads_slab/ppermute | solution.py:619
  73.5 2.0 %late_forces.1 = (f32[8,64]{1,0:T(8,128)S(1)}, f32[8,32]{1,0:T(8,128)S(1)}, f32[8,32]{1,0:T(8,128)S(1)}, f32[8,64]{1,0:T(8,128)S(1)}, f32[8,64]{1,0:T(8,128)S(1)}) custom-call(f32[64,128]{1,0:T(8,128)S(1)} %get-tuple-element.173.own_ref, f32[32,128]{1,0:T(8,128)S(1)} %collective-permute-done.10.rf_ref, f32[32,128]{1,0:T(8,128)S(1)} %collective-permute-done.11.rn_ref, ...), custom_call_target="tpu_custom_call" | custom-call | bytes 8925184 | tf_op jit(solution)/shard_map/late_forces/late_forces/pallas_call | solution.py:133
  75.5 4.0 %collective-permute-start.12 = (f32[8,64]{1,0:T(8,128)S(1)}, f32[8,64]{1,0:T(8,128)S(1)}, u32[]{:S(2)}, u32[]{:S(2)}) collective-permute-start(f32[8,64]{1,0:T(8,128)S(1)} %get-tuple-element.185), channel_id=1, source_target_pairs={{1,2},{3,4},{5,6},{7,8},{9,10},{11,12},{13,14},{15,0},{2,1},{4,3},... | collective-permute-start | bytes 6152 | tf_op jit(solution)/shard_map/position_grads_plane/ppermute | solution.py:630
  79.5 1.9 %collective-permute-start.13 = (f32[8,64]{1,0:T(8,128)S(1)}, f32[8,64]{1,0:T(8,128)S(1)}, u32[]{:S(2)}, u32[]{:S(2)}) collective-permute-start(f32[8,64]{1,0:T(8,128)S(1)} %get-tuple-element.186), channel_id=1, source_target_pairs={{0,1},{1,0},{2,3},{3,2},{4,5},{5,4},{6,7},{7,6},{8,9},{9,8},{10,11... | collective-permute-start | bytes 6152 | tf_op jit(solution)/shard_map/position_grads_plane/ppermute | solution.py:635
  81.4 3.2 %collective-permute-done.12.rf_ref = f32[8,64]{1,0:T(8,128)S(1)} collective-permute-done((f32[8,64]{1,0:T(8,128)S(1)}, f32[8,64]{1,0:T(8,128)S(1)}, u32[]{:S(2)}, u32[]{:S(2)}) %collective-permute-start.12) | collective-permute-done | bytes 2080 | tf_op jit(solution)/shard_map/position_grads_plane/ppermute | solution.py:630
  84.6 1.9 %collective-permute-done.13.rn_ref = f32[8,64]{1,0:T(8,128)S(1)} collective-permute-done((f32[8,64]{1,0:T(8,128)S(1)}, f32[8,64]{1,0:T(8,128)S(1)}, u32[]{:S(2)}, u32[]{:S(2)}) %collective-permute-start.13) | collective-permute-done | bytes 2080 | tf_op jit(solution)/shard_map/position_grads_plane/ppermute | solution.py:635
  86.7 2.8 %collective-permute-start.14 = (f32[8,32]{1,0:T(8,128)S(1)}, f32[8,32]{1,0:T(8,128)S(1)}, u32[]{:S(2)}, u32[]{:S(2)}) collective-permute-start(f32[8,32]{1,0:T(8,128)S(1)} %get-tuple-element.188), channel_id=1, source_target_pairs={{16,32},{48,64},{80,96},{112,128},{144,160},{176,192},{208,224},{2... | collective-permute-start | bytes 3080 | tf_op jit(solution)/shard_map/position_grads_slab/ppermute | solution.py:619
  89.4 1.9 %collective-permute-start.15 = (f32[8,32]{1,0:T(8,128)S(1)}, f32[8,32]{1,0:T(8,128)S(1)}, u32[]{:S(2)}, u32[]{:S(2)}) collective-permute-start(f32[8,32]{1,0:T(8,128)S(1)} %get-tuple-element.189), channel_id=1, source_target_pairs={{0,16},{16,0},{32,48},{48,32},{64,80},{80,64},{96,112},{112,96},{1... | collective-permute-start | bytes 3080 | tf_op jit(solution)/shard_map/position_grads_slab/ppermute | solution.py:624
  91.9 1.8 %collective-permute-done.14.rf_ref = f32[8,32]{1,0:T(8,128)S(1)} collective-permute-done((f32[8,32]{1,0:T(8,128)S(1)}, f32[8,32]{1,0:T(8,128)S(1)}, u32[]{:S(2)}, u32[]{:S(2)}) %collective-permute-start.14) | collective-permute-done | bytes 1056 | tf_op jit(solution)/shard_map/position_grads_slab/ppermute | solution.py:619
  (15 shorter events, 2.7 us)
Async XLA Ops:
  1.6 12.9 %collective-permute-start = (f32[8,32]{1,0:T(8,128)S(1)}, f32[8,32]{1,0:T(8,128)S(1)}, u32[]{:S(2)}, u32[]{:S(2)}) collective-permute-start(f32[8,32]{1,0:T(8,128)S(1)} %get-tuple-element.97), channel_id=1, source_target_pairs={{16,32},{48,64},{80,96},{112,128},{144,160},{176,192},{208,224},{2... | collective-permute-start | bytes 3080 | tf_op jit(solution)/shard_map/atoms_slab/ppermute | solution.py:619
  11.9 3.1 %collective-permute-start.1 = (f32[8,32]{1,0:T(8,128)S(1)}, f32[8,32]{1,0:T(8,128)S(1)}, u32[]{:S(2)}, u32[]{:S(2)}) collective-permute-start(f32[8,32]{1,0:T(8,128)S(1)} %get-tuple-element.98), channel_id=1, source_target_pairs={{0,16},{16,0},{32,48},{48,32},{64,80},{80,64},{96,112},{112,96},{1... | collective-permute-start | bytes 3080 | tf_op jit(solution)/shard_map/atoms_slab/ppermute | solution.py:624
  15.1 12.0 %collective-permute-start.2 = (f32[8,64]{1,0:T(8,128)S(1)}, f32[8,64]{1,0:T(8,128)S(1)}, u32[]{:S(2)}, u32[]{:S(2)}) collective-permute-start(f32[8,64]{1,0:T(8,128)S(1)} %get-tuple-element.103), channel_id=1, source_target_pairs={{1,2},{3,4},{5,6},{7,8},{9,10},{11,12},{13,14},{15,0},{2,1},{4,3},... | collective-permute-start | bytes 6152 | tf_op jit(solution)/shard_map/atoms_plane/ppermute | solution.py:630
  22.4 7.0 %collective-permute-start.3 = (f32[8,64]{1,0:T(8,128)S(1)}, f32[8,64]{1,0:T(8,128)S(1)}, u32[]{:S(2)}, u32[]{:S(2)}) collective-permute-start(f32[8,64]{1,0:T(8,128)S(1)} %get-tuple-element.104), channel_id=1, source_target_pairs={{0,1},{1,0},{2,3},{3,2},{4,5},{5,4},{6,7},{7,6},{8,9},{9,8},{10,11... | collective-permute-start | bytes 6152 | tf_op jit(solution)/shard_map/atoms_plane/ppermute | solution.py:635
  32.2 7.2 %collective-permute-start.4 = (f32[32,128]{1,0:T(8,128)S(1)}, f32[32,128]{1,0:T(8,128)S(1)}, u32[]{:S(2)}, u32[]{:S(2)}) collective-permute-start(f32[32,128]{1,0:T(8,128)S(1)} %get-tuple-element.128), channel_id=1, source_target_pairs={{16,32},{48,64},{80,96},{112,128},{144,160},{176,192},{208,224},{2... | collective-permute-start | bytes 49160 | tf_op jit(solution)/shard_map/features_slab/ppermute | solution.py:619
  35.4 4.0 %collective-permute-start.5 = (f32[32,128]{1,0:T(8,128)S(1)}, f32[32,128]{1,0:T(8,128)S(1)}, u32[]{:S(2)}, u32[]{:S(2)}) collective-permute-start(f32[32,128]{1,0:T(8,128)S(1)} %get-tuple-element.129), channel_id=1, source_target_pairs={{0,16},{16,0},{32,48},{48,32},{64,80},{80,64},{96,112},{112,96},{1... | collective-permute-start | bytes 49160 | tf_op jit(solution)/shard_map/features_slab/ppermute | solution.py:624
  39.6 9.4 %collective-permute-start.6 = (f32[64,128]{1,0:T(8,128)S(1)}, f32[64,128]{1,0:T(8,128)S(1)}, u32[]{:S(2)}, u32[]{:S(2)}) collective-permute-start(f32[64,128]{1,0:T(8,128)S(1)} %get-tuple-element.147), channel_id=1, source_target_pairs={{1,2},{3,4},{5,6},{7,8},{9,10},{11,12},{13,14},{15,0},{2,1},{4,3},... | collective-permute-start | bytes 98312 | tf_op jit(solution)/shard_map/features_plane/ppermute | solution.py:630
  43.6 7.3 %collective-permute-start.7 = (f32[64,128]{1,0:T(8,128)S(1)}, f32[64,128]{1,0:T(8,128)S(1)}, u32[]{:S(2)}, u32[]{:S(2)}) collective-permute-start(f32[64,128]{1,0:T(8,128)S(1)} %get-tuple-element.148), channel_id=1, source_target_pairs={{0,1},{1,0},{2,3},{3,2},{4,5},{5,4},{6,7},{7,6},{8,9},{9,8},{10,11... | collective-permute-start | bytes 98312 | tf_op jit(solution)/shard_map/features_plane/ppermute | solution.py:635
  53.3 9.9 %collective-permute-start.8 = (f32[64,128]{1,0:T(8,128)S(1)}, f32[64,128]{1,0:T(8,128)S(1)}, u32[]{:S(2)}, u32[]{:S(2)}) collective-permute-start(f32[64,128]{1,0:T(8,128)S(1)} %get-tuple-element.168), channel_id=1, source_target_pairs={{1,2},{3,4},{5,6},{7,8},{9,10},{11,12},{13,14},{15,0},{2,1},{4,3},... | collective-permute-start | bytes 98312 | tf_op jit(solution)/shard_map/feature_grads_plane/ppermute | solution.py:630
  58.8 7.3 %collective-permute-start.9 = (f32[64,128]{1,0:T(8,128)S(1)}, f32[64,128]{1,0:T(8,128)S(1)}, u32[]{:S(2)}, u32[]{:S(2)}) collective-permute-start(f32[64,128]{1,0:T(8,128)S(1)} %get-tuple-element.169), channel_id=1, source_target_pairs={{0,1},{1,0},{2,3},{3,2},{4,5},{5,4},{6,7},{7,6},{8,9},{9,8},{10,11... | collective-permute-start | bytes 98312 | tf_op jit(solution)/shard_map/feature_grads_plane/ppermute | solution.py:635
  66.3 7.2 %collective-permute-start.10 = (f32[32,128]{1,0:T(8,128)S(1)}, f32[32,128]{1,0:T(8,128)S(1)}, u32[]{:S(2)}, u32[]{:S(2)}) collective-permute-start(f32[32,128]{1,0:T(8,128)S(1)} %get-tuple-element.174), channel_id=1, source_target_pairs={{16,32},{48,64},{80,96},{112,128},{144,160},{176,192},{208,224},{2... | collective-permute-start | bytes 49160 | tf_op jit(solution)/shard_map/feature_grads_slab/ppermute | solution.py:619
  68.3 5.2 %collective-permute-start.11 = (f32[32,128]{1,0:T(8,128)S(1)}, f32[32,128]{1,0:T(8,128)S(1)}, u32[]{:S(2)}, u32[]{:S(2)}) collective-permute-start(f32[32,128]{1,0:T(8,128)S(1)} %get-tuple-element.175), channel_id=1, source_target_pairs={{0,16},{16,0},{32,48},{48,32},{64,80},{80,64},{96,112},{112,96},{1... | collective-permute-start | bytes 49160 | tf_op jit(solution)/shard_map/feature_grads_slab/ppermute | solution.py:624
  75.5 9.1 %collective-permute-start.12 = (f32[8,64]{1,0:T(8,128)S(1)}, f32[8,64]{1,0:T(8,128)S(1)}, u32[]{:S(2)}, u32[]{:S(2)}) collective-permute-start(f32[8,64]{1,0:T(8,128)S(1)} %get-tuple-element.185), channel_id=1, source_target_pairs={{1,2},{3,4},{5,6},{7,8},{9,10},{11,12},{13,14},{15,0},{2,1},{4,3},... | collective-permute-start | bytes 6152 | tf_op jit(solution)/shard_map/position_grads_plane/ppermute | solution.py:630
  79.5 7.0 %collective-permute-start.13 = (f32[8,64]{1,0:T(8,128)S(1)}, f32[8,64]{1,0:T(8,128)S(1)}, u32[]{:S(2)}, u32[]{:S(2)}) collective-permute-start(f32[8,64]{1,0:T(8,128)S(1)} %get-tuple-element.186), channel_id=1, source_target_pairs={{0,1},{1,0},{2,3},{3,2},{4,5},{5,4},{6,7},{7,6},{8,9},{9,8},{10,11... | collective-permute-start | bytes 6152 | tf_op jit(solution)/shard_map/position_grads_plane/ppermute | solution.py:635
  86.7 7.0 %collective-permute-start.14 = (f32[8,32]{1,0:T(8,128)S(1)}, f32[8,32]{1,0:T(8,128)S(1)}, u32[]{:S(2)}, u32[]{:S(2)}) collective-permute-start(f32[8,32]{1,0:T(8,128)S(1)} %get-tuple-element.188), channel_id=1, source_target_pairs={{16,32},{48,64},{80,96},{112,128},{144,160},{176,192},{208,224},{2... | collective-permute-start | bytes 3080 | tf_op jit(solution)/shard_map/position_grads_slab/ppermute | solution.py:619
  89.4 4.3 %collective-permute-start.15 = (f32[8,32]{1,0:T(8,128)S(1)}, f32[8,32]{1,0:T(8,128)S(1)}, u32[]{:S(2)}, u32[]{:S(2)}) collective-permute-start(f32[8,32]{1,0:T(8,128)S(1)} %get-tuple-element.189), channel_id=1, source_target_pairs={{0,16},{16,0},{32,48},{48,32},{64,80},{80,64},{96,112},{112,96},{1... | collective-permute-start | bytes 3080 | tf_op jit(solution)/shard_map/position_grads_slab/ppermute | solution.py:624

commit v3 on v2

--- a/solution.py
+++ b/solution.py
@@ -101,35 +101,38 @@
     return pl.ds(b * SPAN, SPAN)
 
 
-def fetched(kernel, count):
+def fetched(kernel, count, carried):
     def run(*refs):
-        given, rest = refs[:count], refs[count:]
+        given, rest = refs[: count + carried], refs[count + carried :]
         sems, held = rest[-1], rest[-1 - count : -1]
-        copies = [pltpu.make_async_copy(src, dst, sems.at[k]) for k, (src, dst) in enumerate(zip(given, held))]
+        targets = held + rest[:carried]
+        copies = [pltpu.make_async_copy(src, dst, sems.at[k]) for k, (src, dst) in enumerate(zip(given, targets))]
         for copy in copies:
             copy.start()
-        for copy in copies:
+        for copy in copies[:count]:
             copy.wait()
-        kernel(*held, *rest[: -1 - count])
+        kernel(*held, *rest[carried : -1 - count])
+        for copy in copies[count:]:
+            copy.wait()
 
     return run
 
 
-def call(kernel, outs, args, scratch=(), flops=0, name=None, limit=8, raw=False):
+def call(kernel, outs, args, scratch=(), flops=0, name=None, limit=8, carried=None):
     spec = pl.BlockSpec(memory_space=pltpu.VMEM)
+    scratch = list(scratch)
+    if carried is not None:
+        scratch += [pltpu.VMEM(a.shape, a.dtype) for a in args]
+        scratch.append(pltpu.SemaphoreType.DMA((len(args) + len(carried),)))
+        kernel = fetched(kernel, len(args), len(carried))
+        outs = [(a.shape, a.dtype) for a in carried] + list(outs)
+        args = [pltpu.with_memory_space_constraint(a, pltpu.HBM) for a in [*args, *carried]]
+        in_specs = [pl.BlockSpec(memory_space=pltpu.HBM)] * len(args)
+    else:
+        args = [pltpu.with_memory_space_constraint(a, pltpu.VMEM) for a in args]
+        in_specs = [spec] * len(args)
     out_shape = tuple(pltpu.VMEM(shape, dtype) for shape, dtype in outs)
     moved = sum(a.size * a.dtype.itemsize for a in args)
-    scratch = list(scratch)
-    if raw:
-        big = [a for a in args if a.size > 1]
-        scratch += [pltpu.VMEM(a.shape, a.dtype) for a in big] + [pltpu.SemaphoreType.DMA((len(big),))]
-        kernel = fetched(kernel, len(big))
-        in_specs = [pl.BlockSpec(memory_space=pltpu.HBM)] * len(big)
-        in_specs += [pl.BlockSpec(memory_space=pltpu.SMEM)] * (len(args) - len(big))
-        args = [pltpu.with_memory_space_constraint(a, pltpu.HBM) for a in big] + [a for a in args if a.size == 1]
-    else:
-        in_specs = [spec] * len(args)
-        args = [pltpu.with_memory_space_constraint(a, pltpu.VMEM) for a in args]
     return pl.pallas_call(
         kernel,
         out_shape=out_shape,
@@ -144,6 +147,10 @@
 
 def odd(axis):
     return lax.rem(lax.axis_index(axis), 2)
+
+
+def partner_of(ref):
+    return jnp.where(jnp.full(ref.shape[1:], odd("plane")) == 1, ref[0], ref[1])
 
 
 def by_parity(flag, rows):
@@ -199,11 +206,11 @@
 
 def prepare_kernel(
     edge_ref, one_ref, two_ref, three_ref, four_ref, embed_ref, up_ref, skip_ref, atom_ref, hid_ref, ro_ref,
-    out_ref, gain_ref, read_ref, count_ref,
+    out_ref, gain_ref, read_ref,
     g_ref, gt_ref, dd_ref, mask_ref, w1_ref, w2_ref, w3_ref, w4_ref, table_ref, skips_ref, skipups_ref, refs_ref,
     from_first_ref, from_mix_ref, from_first_ro_ref, from_mix_ro_ref, outup_ref, out0_ref, gains_ref, reads_ref, ros_ref,
 ):
-    per_atom = count_ref[0, 0] // OWN
+    per_atom = jnp.sum((edge_ref[1:2, :] == OWN - 1).astype(f32)).astype(jnp.int32)
     senders = jnp.broadcast_to(edge_ref[0:1, :], (8, EDGES))
     swap_plane = jnp.full((1, SPAN), odd("plane")) == 1
     place = lax.broadcasted_iota(jnp.int32, (GROUP, SPAN), 1)
@@ -444,7 +451,7 @@
     f_ref, sf_ref, sn_ref, mix_ref, amp_ref, l_ref, m_ref, ast_ref, b_ref, db_ref, geo_ref,
 ):
     step = (2 * odd("plane") - 1).astype(f32) * (CELLS_Y * cell_side)
-    far, near = shifted(qf_ref[...], 1, step), shifted(qn_ref[...], 1, -step)
+    far, near = shifted(qf_ref[...], 1, step), shifted(partner_of(qn_ref), 1, -step)
     valid = jnp.sum(mask_ref[...], axis=0, keepdims=True) > 0.5
     vector = vector_ref[...] + (pick_lanes(far, dd_ref[128:192, :]) + pick_lanes(near, dd_ref[192:256, :]))
     lifted = [dot(kinds_of(part[3:4]).astype(bf16), table_ref[...], TN).astype(bf16) for part in (far, near)]
@@ -522,7 +529,7 @@
     amp_ref, glift_ref,
 ):
     lifted = pair_lanes(
-        jnp.concatenate([f_ref[...], rf_ref[...], rn_ref[...], pf_ref[...], pn_ref[...]], axis=0)
+        jnp.concatenate([f_ref[...], rf_ref[...], rn_ref[...], pf_ref[...], partner_of(pn_ref)], axis=0)
     )
     messages(g_ref, lifted, lambda b: r_ref[span(b), :], l_ref, m_ref)
     amplitudes(ast_ref, m_ref, amp_ref)
@@ -569,7 +576,7 @@
 
 
 def back_middle_kernel(gmid_ref, rf_ref, rn_ref, pf_ref, pn_ref, own_ref, f_ref, n_ref):
-    mid = gmid_ref[...] + (pick_rows(pf_ref[...], rf_ref[...]) + pick_rows(pn_ref[...], rn_ref[...]))
+    mid = gmid_ref[...] + (pick_rows(pf_ref[...], rf_ref[...]) + pick_rows(pn_ref[...], partner_of(rn_ref)))
     own_ref[...] = mid[:64]
     f_ref[...] = mid[64:96]
     n_ref[...] = mid[96:128]
@@ -598,7 +605,7 @@
 
 
 def collect_plane_kernel(of_ref, pf_ref, pn_ref, rf_ref, rn_ref, tf_ref, tn_ref, o_ref, f_ref, n_ref):
-    far, near, at = rf_ref[...], rn_ref[...], 0
+    far, near, at = rf_ref[...], partner_of(rn_ref), 0
     for have_ref, ref in ((of_ref, o_ref), (pf_ref, f_ref), (pn_ref, n_ref)):
         rows = ref.shape[1]
         back = pick_lanes(far, tf_ref[at : at + rows, :], NT) + pick_lanes(near, tn_ref[at : at + rows, :], NT)
@@ -632,7 +639,7 @@
 
 def swap_plane_near(value):
     count = lax.axis_size("plane")
-    return lax.ppermute(value, "plane", [(i, i ^ 1) for i in range(count)])
+    return lax.all_gather(value, "plane", axis_index_groups=[[i, i + 1] for i in range(0, count, 2)])
 
 
 def both(swap_far, swap_near, far, near):
@@ -672,23 +679,17 @@
     plane_lanes = ((8, 64), f32)
 
     with jax.named_scope("atoms_slab"):
-        values, slab_t_far, slab_t_near, plane_t_far, plane_t_near, far, near = call(
+        *arguments, values, slab_t_far, slab_t_near, plane_t_far, plane_t_near, far, near = call(
             atoms_slab_kernel,
             [own_lanes, ((OWN, 32), bf16), ((OWN, 32), bf16), ((128, 64), bf16), ((128, 64), bf16), slab_lanes, slab_lanes],
             (jnp.transpose(positions, (0, 2, 1, 3)), species[0], slab_sends[0, 0], plane_sends[0, 0]),
-            raw=True,
+            carried=(
+                edges[0, 0], radial_one, radial_two, radial_three, radial_four, embed_table, up_weight, skip_weight,
+                atom_ref[None, :], jnp.transpose(read_hidden), read_out[None, :], out_weight, prod_weight, read_one[None, :],
+            ),
             name="atoms_slab",
         )
         far, near = both(swap_slab_far, swap_slab_near, far, near)
-    with jax.named_scope("atoms_plane"):
-        slab_far, slab_near, far, near = call(
-            atoms_plane_kernel,
-            [slab_lanes, slab_lanes, plane_lanes, plane_lanes],
-            (values, far, near, plane_t_far, plane_t_near),
-            name="atoms_plane",
-        )
-        edge_list, far, near = lax.optimization_barrier((edges[0, 0], far, near))
-        far, near = both(swap_plane_far, swap_plane_near, far, near)
     with jax.named_scope("prepare"):
         sender_n, sender_t, edge_t, mask, *prepared = call(
             prepare_kernel,
@@ -696,16 +697,22 @@
              ((2, 64, 32), bf16), ((2, 64, 192), bf16), ((2, 64, 192), bf16), ((2, 192, 3 * C), bf16),
              ((KINDS, 2 * C), bf16), ((KINDS, 3 * C), bf16), ((KINDS, 3 * C), bf16), ((8, KINDS), f32),
              *[((16, C), f32)] * 4, ((C, C), f32), ((C, C), f32), ((2, 4, C), f32), ((1, C), f32), ((8, 16), f32)],
-            (edge_list, radial_one, radial_two, radial_three, radial_four, embed_table, up_weight, skip_weight,
-             atom_ref[None, :], jnp.transpose(read_hidden), read_out[None, :], out_weight, prod_weight,
-             read_one[None, :], edge_count),
-            raw=True,
+            arguments,
             flops=1_000_000_000,
             name="prepare",
         )
         weights = tuple(prepared[:4])
         (table, skip_table, skip_up_table, ref_row, from_first, from_mix, from_first_ro, from_mix_ro, out_up, out_first,
          gains, read_row, read_last) = prepared[4:]
+    with jax.named_scope("atoms_plane"):
+        far, near, edge_t = lax.optimization_barrier((far, near, edge_t))
+        slab_far, slab_near, far, near = call(
+            atoms_plane_kernel,
+            [slab_lanes, slab_lanes, plane_lanes, plane_lanes],
+            (values, far, near, plane_t_far, plane_t_near),
+            name="atoms_plane",
+        )
+        far, near = both(swap_plane_far, swap_plane_near, far, near)
         vector, lifted = call(
             near_atoms_kernel, [edge_rows, ((128, 2 * C), bf16)], (values, slab_far, slab_near, edge_t, table),
             flops=1_000_000_000, name="near_atoms",
@@ -724,12 +731,6 @@
         )
     with jax.named_scope("features_slab"):
         slab_far, slab_near = both(swap_slab_far, swap_slab_near, s_far, s_near)
-    with jax.named_scope("features_plane"):
-        far, near = call(
-            middle_kernel, [plane_rows] * 2, (first, slab_far, slab_near, plane_t_far, plane_t_near), name="middle"
-        )
-        far, near, basis, geo, mix = lax.optimization_barrier((far, near, basis, geo, mix))
-        far, near = both(swap_plane_far, swap_plane_near, far, near)
     radial_second, slope_second, slope_first, hidden, energies, turned = call(
         beside_features_kernel,
         [by_degree, ((192, EDGES), bf16), ((192, EDGES), bf16), hidden_mat, own_lanes, ((EDGES, TURNED), bf16)],
@@ -737,6 +738,12 @@
          angular),
         flops=1_000_000_000, name="beside_features",
     )
+    with jax.named_scope("features_plane"):
+        slab_far, slab_near, radial_second = lax.optimization_barrier((slab_far, slab_near, radial_second))
+        far, near = call(
+            middle_kernel, [plane_rows] * 2, (first, slab_far, slab_near, plane_t_far, plane_t_near), name="middle"
+        )
+        far, near = both(swap_plane_far, swap_plane_near, far, near)
     with jax.named_scope("second_layer"):
         act, slope, gmid, far, near, lift_second, message_second, ga = call(
             second_kernel,
@@ -747,8 +754,14 @@
             name="second_layer",
         )
     with jax.named_scope("feature_grads_plane"):
+        far, near = both(swap_plane_far, swap_plane_near, far, near)
+    with jax.named_scope("feature_grads_slab"):
+        own, far, near = call(
+            back_middle_kernel, [plane_rows, slab_rows, slab_rows], (gmid, far, near, plane_t_far, plane_t_near),
+            name="back_middle",
+        )
         far, near, ga = lax.optimization_barrier((far, near, ga))
-        far, near = both(swap_plane_far, swap_plane_near, far, near)
+        far, near = both(swap_slab_far, swap_slab_near, far, near)
     early, slope_first, energies, own_grads = call(
         beside_grads_kernel,
         [edge_rows, by_degree, ((1, OWN), f32), plane_rows],
@@ -757,13 +770,6 @@
         scratch=[pltpu.VMEM((EDGES, 2 * C), bf16), pltpu.VMEM((8, EDGES), f32)],
         flops=1_000_000_000, name="beside_grads",
     )
-    with jax.named_scope("feature_grads_slab"):
-        far, near, early = lax.optimization_barrier((far, near, early))
-        own, far, near = call(
-            back_middle_kernel, [plane_rows, slab_rows, slab_rows], (gmid, far, near, plane_t_far, plane_t_near),
-            name="back_middle",
-        )
-        far, near = both(swap_slab_far, swap_slab_near, far, near)
     with jax.named_scope("late_forces"):
         own, slab_far, slab_near, far, near = call(
             late_kernel,

time: 95 us -> 92.2 us (0.971)
  blocking collectives: 0 us -> 24.6 us
  waiting for transfers between devices: 20.5 us -> 1.1 us
  starting transfers between devices: 54.3 us -> 47.7 us
    all_gather x0 -> x4, blocking collectives: none -> 24.6 us  [swap_plane_near(): lax.all_gather(value, 'plane', axis_index_groups=[[i, i + 1] for i in ran...]
    ppermute x4 -> x0, waiting for transfers between devices: 8.83 us -> none  [swap_plane_near(): return lax.ppermute(value, 'plane', [(i, i ^ 1) for i in range(count)])]
    ppermute x4 -> x0, starting transfers between devices: 7.73 us -> none  [swap_plane_near(): return lax.ppermute(value, 'plane', [(i, i ^ 1) for i in range(count)])]
    ppermute x4, waiting for transfers between devices: 7.22 us -> 0.53 us  [swap_slab_far(): return lax.ppermute(value, 'slab', pairs + [(b, a) for a, b in pairs])]
    ppermute x4, waiting for transfers between devices: 4.02 us -> 0.01 us  [swap_plane_far(): return lax.ppermute(value, 'plane', pairs + [(b, a) for a, b in pairs])]
    ppermute x4, starting transfers between devices: 18.2 us -> 20.2 us  [swap_slab_far(): return lax.ppermute(value, 'slab', pairs + [(b, a) for a, b in pairs])]
    ppermute x4, starting transfers between devices: 20.7 us -> 19.7 us  [swap_plane_far(): return lax.ppermute(value, 'plane', pairs + [(b, a) for a, b in pairs])]
  transfers between devices with their start and end apart: 16 -> 12, of which waited for: 10 -> 3; matrix products, arithmetic and copies ran while one was open for 1% -> 1% of each run, Pallas kernels for 8% -> 7%
where the time goes in v3:
time: 92.2 us; the launch traced here: 91.4 us
  starting transfers between devices  47.7 us (52%)
  blocking collectives  24.6 us (27%)
  Pallas kernels  16.1 us (17%)
  waiting for transfers between devices  1.1 us (1%)
  local copies, waits for them, and re-layouts  1.09 us (1%)
    all_gather x4, blocking collectives, swap_plane_near(): lax.all_gather(value, 'plane', axis_index_groups=[[i, i + 1] for i in ran...  24.6 us
    ppermute x4, starting transfers between devices, swap_slab_far(): return lax.ppermute(value, 'slab', pairs + [(b, a) for a, b in pairs])  20.2 us
    ppermute x4, starting transfers between devices, swap_plane_far(): return lax.ppermute(value, 'plane', pairs + [(b, a) for a, b in pairs])  19.7 us
    pallas_call x13, Pallas kernels, call(): pl.pallas_call(kernel, out_shape=out_shape, in_specs=in_specs, out_specs=...  16.1 us
    ppermute x4, starting transfers between devices, swap_slab_near(): return lax.ppermute(value, 'slab', [(i, i ^ 1) for i in range(count)])  7.86 us
  transfers between devices with their start and end apart: 12, of which 3 were waited for; matrix products, arithmetic and copies ran while one was open for 1% of the time, Pallas kernels for 7%

profile of v3, /device:TPU:2, one launch (start us, length us, event | category | flops | bytes accessed | tf_op | source)
XLA Modules:
  0.0 91.4 jit_solution(12485977627053012274)
XLA Ops:
  0.6 1.5 %atoms_slab.1 = (s32[2,1536]{1,0:T(2,128)S(1)}, f32[2,8,64]{2,1,0:T(8,128)S(1)}, f32[2,64,64]{2,1,0:T(8,128)S(1)}, f32[2,64,64]{2,1,0:T(8,128)S(1)}, f32[2,64,38...) custom-call(f32[1,3,1,64]{3,2,1,0:T(1,128)} %bitcast.25, ...), custom_call_target="tpu_custom_call" | custom-call | bytes 732324 | tf_op jit(solution)/shard_map/atoms_slab/atoms_slab/pallas_call | solution.py:136
  2.1 10.4 %collective-permute-start = (f32[8,32]{1,0:T(8,128)S(1)}, f32[8,32]{1,0:T(8,128)S(1)}, u32[]{:S(2)}, u32[]{:S(2)}) collective-permute-start(f32[8,32]{1,0:T(8,128)S(1)} %get-tuple-element.106), channel_id=1, source_target_pairs={{16,32},{48,64},{80,96},{112,128},{144,160},{176,192},{208,224},{2... | collective-permute-start | bytes 3080 | tf_op jit(solution)/shard_map/atoms_slab/ppermute | solution.py:626
  12.5 1.9 %collective-permute-start.1 = (f32[8,32]{1,0:T(8,128)S(1)}, f32[8,32]{1,0:T(8,128)S(1)}, u32[]{:S(2)}, u32[]{:S(2)}) collective-permute-start(f32[8,32]{1,0:T(8,128)S(1)} %get-tuple-element.107), channel_id=1, source_target_pairs={{0,16},{16,0},{32,48},{48,32},{64,80},{80,64},{96,112},{112,96},{1... | collective-permute-start | bytes 3080 | tf_op jit(solution)/shard_map/atoms_slab/ppermute | solution.py:631
  14.4 1.1 %prepare.1 = (bf16[1536,256]{1,0:T(8,128)(2,1)S(1)}, bf16[256,1536]{1,0:T(8,128)(2,1)S(1)}, bf16[256,1536]{1,0:T(8,128)(2,1)S(1)}, f32[16,1536]{1,0:T(8,128)S(1)...) custom-call(s32[2,1536]{1,0:T(2,128)S(1)} %get-tuple-element.108.edg, ...), custom_call_target="tpu_custom_call" | custom-call | flops 1000000000 | bytes 730532 | tf_op jit(solution)/shard_map/prepare/prepare/pallas_call | solution.py:136
  15.6 0.2 atoms_plane.1
  15.7 7.2 %collective-permute-start.2 = (f32[8,64]{1,0:T(8,128)S(1)}, f32[8,64]{1,0:T(8,128)S(1)}, u32[]{:S(2)}, u32[]{:S(2)}) collective-permute-start(f32[8,64]{1,0:T(8,128)S(1)} %get-tuple-element.127), channel_id=1, source_target_pairs={{1,2},{3,4},{5,6},{7,8},{9,10},{11,12},{13,14},{15,0},{2,1},{4,3},... | collective-permute-start | bytes 6152 | tf_op jit(solution)/shard_map/atoms_plane/ppermute | solution.py:637
  23.0 0.3 near_atoms.1
  23.2 5.8 %all-gather = f32[16,64]{1,0:T(8,128)S(1)} all-gather(f32[8,64]{1,0:T(8,128)S(1)} %get-tuple-element.128), channel_id=2, replica_groups={{0,1},{2,3},{4,5},{6,7},{8,9},{10,11},{12,13},{14,15},{16,17},{18,19},{..., dimensions={0}, use_global_device_ids=true | all-gather | bytes 6144 | tf_op jit(solution)/shard_map/atoms_plane/all_gather | solution.py:642
  29.1 2.8 %first_layer.1 = (f32[64,128]{1,0:T(8,128)S(1)}, f32[32,128]{1,0:T(8,128)S(1)}, f32[32,128]{1,0:T(8,128)S(1)}, f32[64,128]{1,0:T(8,128)S(1)}, f32[9,64,128]{2,1,...) custom-call(f32[8,64]{1,0:T(8,128)S(1)} %get-tuple-element.105.v_ref, ...), custom_call_target="tpu_custom_call" | custom-call | bytes 2396160 | tf_op jit(solution)/shard_map/first_layer/first_layer/pallas_call | solution.py:136
  31.8 3.2 %collective-permute-start.3 = (f32[32,128]{1,0:T(8,128)S(1)}, f32[32,128]{1,0:T(8,128)S(1)}, u32[]{:S(2)}, u32[]{:S(2)}) collective-permute-start(f32[32,128]{1,0:T(8,128)S(1)} %get-tuple-element.163), channel_id=1, source_target_pairs={{16,32},{48,64},{80,96},{112,128},{144,160},{176,192},{208,224},{2... | collective-permute-start | bytes 49160 | tf_op jit(solution)/shard_map/features_slab/ppermute | solution.py:626
  35.0 1.9 %collective-permute-start.4 = (f32[32,128]{1,0:T(8,128)S(1)}, f32[32,128]{1,0:T(8,128)S(1)}, u32[]{:S(2)}, u32[]{:S(2)}) collective-permute-start(f32[32,128]{1,0:T(8,128)S(1)} %get-tuple-element.164), channel_id=1, source_target_pairs={{0,16},{16,0},{32,48},{48,32},{64,80},{80,64},{96,112},{112,96},{1... | collective-permute-start | bytes 49160 | tf_op jit(solution)/shard_map/features_slab/ppermute | solution.py:631
  36.9 2.7 %beside_features.1 = (f32[1536,384]{1,0:T(8,128)S(1)}, bf16[192,1536]{1,0:T(8,128)(2,1)S(1)}, bf16[192,1536]{1,0:T(8,128)(2,1)S(1)}, f32[16,64]{1,0:T(8,128)S(1)...) custom-call(f32[8,1536]{1,0:T(8,128)S(1)} %get-tuple-element.150.b_ref, f32[8,1536]{1,0:T(8,128)S(1)} %get-tuple-element.151.db_ref, ...), custom_call_target="tpu_custom_call" | custom-call | flops 1000000000 | bytes 2061824 | tf_op jit(solution)/shard_map/beside_features/pallas_call | solution.py:136
  39.7 0.2 middle.1
  39.9 2.7 %collective-permute-start.5 = (f32[64,128]{1,0:T(8,128)S(1)}, f32[64,128]{1,0:T(8,128)S(1)}, u32[]{:S(2)}, u32[]{:S(2)}) collective-permute-start(f32[64,128]{1,0:T(8,128)S(1)} %get-tuple-element.168), channel_id=1, source_target_pairs={{1,2},{3,4},{5,6},{7,8},{9,10},{11,12},{13,14},{15,0},{2,1},{4,3},... | collective-permute-start | bytes 98312 | tf_op jit(solution)/shard_map/features_plane/ppermute | solution.py:637
  42.6 6.8 %all-gather.1 = f32[128,128]{1,0:T(8,128)S(1)} all-gather(f32[64,128]{1,0:T(8,128)S(1)} %get-tuple-element.169), channel_id=3, replica_groups={{0,1},{2,3},{4,5},{6,7},{8,9},{10,11},{12,13},{14,15},{16,17},{18,19},{..., dimensions={0}, use_global_device_ids=true | all-gather | bytes 98304 | tf_op jit(solution)/shard_map/features_plane/all_gather | solution.py:642
  49.4 2.4 %second_layer.1 = (f32[16,64]{1,0:T(8,128)S(1)}, f32[16,64]{1,0:T(8,128)S(1)}, f32[128,128]{1,0:T(8,128)S(1)}, f32[64,128]{1,0:T(8,128)S(1)}, f32[64,128]{1,0:T(...) custom-call(f32[64,128]{1,0:T(8,128)S(1)} %get-tuple-element.162.f_ref, ...), custom_call_target="tpu_custom_call" | custom-call | bytes 7413760 | tf_op jit(solution)/shard_map/second_layer/second_layer/pallas_call | solution.py:136
  51.8 6.1 %collective-permute-start.6 = (f32[64,128]{1,0:T(8,128)S(1)}, f32[64,128]{1,0:T(8,128)S(1)}, u32[]{:S(2)}, u32[]{:S(2)}) collective-permute-start(f32[64,128]{1,0:T(8,128)S(1)} %get-tuple-element.178), channel_id=1, source_target_pairs={{1,2},{3,4},{5,6},{7,8},{9,10},{11,12},{13,14},{15,0},{2,1},{4,3},... | collective-permute-start | bytes 98312 | tf_op jit(solution)/shard_map/feature_grads_plane/ppermute | solution.py:637
  57.9 6.1 %all-gather.2 = f32[128,128]{1,0:T(8,128)S(1)} all-gather(f32[64,128]{1,0:T(8,128)S(1)} %get-tuple-element.179), channel_id=4, replica_groups={{0,1},{2,3},{4,5},{6,7},{8,9},{10,11},{12,13},{14,15},{16,17},{18,19},{..., dimensions={0}, use_global_device_ids=true | all-gather | bytes 98304 | tf_op jit(solution)/shard_map/feature_grads_plane/all_gather | solution.py:642
  64.0 0.2 back_middle.1
  64.2 2.2 %collective-permute-start.7 = (f32[32,128]{1,0:T(8,128)S(1)}, f32[32,128]{1,0:T(8,128)S(1)}, u32[]{:S(2)}, u32[]{:S(2)}) collective-permute-start(f32[32,128]{1,0:T(8,128)S(1)} %get-tuple-element.192), channel_id=1, source_target_pairs={{16,32},{48,64},{80,96},{112,128},{144,160},{176,192},{208,224},{2... | collective-permute-start | bytes 49160 | tf_op jit(solution)/shard_map/feature_grads_slab/ppermute | solution.py:626
  66.4 2.1 %collective-permute-start.8 = (f32[32,128]{1,0:T(8,128)S(1)}, f32[32,128]{1,0:T(8,128)S(1)}, u32[]{:S(2)}, u32[]{:S(2)}) collective-permute-start(f32[32,128]{1,0:T(8,128)S(1)} %get-tuple-element.193), channel_id=1, source_target_pairs={{0,16},{16,0},{32,48},{48,32},{64,80},{80,64},{96,112},{112,96},{1... | collective-permute-start | bytes 49160 | tf_op jit(solution)/shard_map/feature_grads_slab/ppermute | solution.py:631
  68.5 2.5 %beside_grads.1 = (f32[8,1536]{1,0:T(8,128)S(1)}, f32[1536,384]{1,0:T(8,128)S(1)}, f32[1,64]{1,0:T(1,128)S(1)}, f32[64,128]{1,0:T(8,128)S(1)}) custom-call(bf16[1536,640]{1,0:T(8,128)(2,1)S(1)} %get-tuple-element.160.turned_ref, bf16[192,1536]{1,0:T(8,128)(2,1)S(1)} %get-tuple-element.161.second_q_ref, bf16[2,192,384]{2,1,0:T(8,128)(2,1)S(1)} %get-tuple-element.145.w4_ref, ...), custom_call_target="tpu_custom_call" | custom-call | flops 1000000000 | bytes 7113728 | tf_op jit(solution)/shard_map/beside_grads/pallas_call | solution.py:136
  71.0 0.4 collective-permute-done.7.rf_ref
  71.4 2.0 %late_forces.1 = (f32[8,64]{1,0:T(8,128)S(1)}, f32[8,32]{1,0:T(8,128)S(1)}, f32[8,32]{1,0:T(8,128)S(1)}, f32[8,64]{1,0:T(8,128)S(1)}, f32[8,64]{1,0:T(8,128)S(1)}) custom-call(f32[64,128]{1,0:T(8,128)S(1)} %get-tuple-element.191.own_ref, f32[32,128]{1,0:T(8,128)S(1)} %collective-permute-done.7.rf_ref, f32[32,128]{1,0:T(8,128)S(1)} %collective-permute-done.8.rn_ref, ...), custom_call_target="tpu_custom_call" | custom-call | bytes 8925184 | tf_op jit(solution)/shard_map/late_forces/late_forces/pallas_call | solution.py:136
  73.4 3.7 %collective-permute-start.9 = (f32[8,64]{1,0:T(8,128)S(1)}, f32[8,64]{1,0:T(8,128)S(1)}, u32[]{:S(2)}, u32[]{:S(2)}) collective-permute-start(f32[8,64]{1,0:T(8,128)S(1)} %get-tuple-element.203), channel_id=1, source_target_pairs={{1,2},{3,4},{5,6},{7,8},{9,10},{11,12},{13,14},{15,0},{2,1},{4,3},... | collective-permute-start | bytes 6152 | tf_op jit(solution)/shard_map/position_grads_plane/ppermute | solution.py:637
  77.1 5.8 %all-gather.3 = f32[16,64]{1,0:T(8,128)S(1)} all-gather(f32[8,64]{1,0:T(8,128)S(1)} %get-tuple-element.204), channel_id=5, replica_groups={{0,1},{2,3},{4,5},{6,7},{8,9},{10,11},{12,13},{14,15},{16,17},{18,19},{..., dimensions={0}, use_global_device_ids=true | all-gather | bytes 6144 | tf_op jit(solution)/shard_map/position_grads_plane/all_gather | solution.py:642
  82.9 0.1 collect_plane.1
  83.1 4.5 %collective-permute-start.10 = (f32[8,32]{1,0:T(8,128)S(1)}, f32[8,32]{1,0:T(8,128)S(1)}, u32[]{:S(2)}, u32[]{:S(2)}) collective-permute-start(f32[8,32]{1,0:T(8,128)S(1)} %get-tuple-element.206), channel_id=1, source_target_pairs={{16,32},{48,64},{80,96},{112,128},{144,160},{176,192},{208,224},{2... | collective-permute-start | bytes 3080 | tf_op jit(solution)/shard_map/position_grads_slab/ppermute | solution.py:626
  87.6 1.9 %collective-permute-start.11 = (f32[8,32]{1,0:T(8,128)S(1)}, f32[8,32]{1,0:T(8,128)S(1)}, u32[]{:S(2)}, u32[]{:S(2)}) collective-permute-start(f32[8,32]{1,0:T(8,128)S(1)} %get-tuple-element.207), channel_id=1, source_target_pairs={{0,16},{16,0},{32,48},{48,32},{64,80},{80,64},{96,112},{112,96},{1... | collective-permute-start | bytes 3080 | tf_op jit(solution)/shard_map/position_grads_slab/ppermute | solution.py:631
  89.5 0.5 copy.21
  90.1 0.5 collective-permute-done.11.rn_ref
  90.8 0.6 copy.22
  (11 shorter events, 0.3 us)
Async XLA Ops:
  2.1 13.4 %collective-permute-start = (f32[8,32]{1,0:T(8,128)S(1)}, f32[8,32]{1,0:T(8,128)S(1)}, u32[]{:S(2)}, u32[]{:S(2)}) collective-permute-start(f32[8,32]{1,0:T(8,128)S(1)} %get-tuple-element.106), channel_id=1, source_target_pairs={{16,32},{48,64},{80,96},{112,128},{144,160},{176,192},{208,224},{2... | collective-permute-start | bytes 3080 | tf_op jit(solution)/shard_map/atoms_slab/ppermute | solution.py:626
  12.5 3.1 %collective-permute-start.1 = (f32[8,32]{1,0:T(8,128)S(1)}, f32[8,32]{1,0:T(8,128)S(1)}, u32[]{:S(2)}, u32[]{:S(2)}) collective-permute-start(f32[8,32]{1,0:T(8,128)S(1)} %get-tuple-element.107), channel_id=1, source_target_pairs={{0,16},{16,0},{32,48},{48,32},{64,80},{80,64},{96,112},{112,96},{1... | collective-permute-start | bytes 3080 | tf_op jit(solution)/shard_map/atoms_slab/ppermute | solution.py:631
  15.7 13.4 %collective-permute-start.2 = (f32[8,64]{1,0:T(8,128)S(1)}, f32[8,64]{1,0:T(8,128)S(1)}, u32[]{:S(2)}, u32[]{:S(2)}) collective-permute-start(f32[8,64]{1,0:T(8,128)S(1)} %get-tuple-element.127), channel_id=1, source_target_pairs={{1,2},{3,4},{5,6},{7,8},{9,10},{11,12},{13,14},{15,0},{2,1},{4,3},... | collective-permute-start | bytes 6152 | tf_op jit(solution)/shard_map/atoms_plane/ppermute | solution.py:637
  31.8 7.8 %collective-permute-start.3 = (f32[32,128]{1,0:T(8,128)S(1)}, f32[32,128]{1,0:T(8,128)S(1)}, u32[]{:S(2)}, u32[]{:S(2)}) collective-permute-start(f32[32,128]{1,0:T(8,128)S(1)} %get-tuple-element.163), channel_id=1, source_target_pairs={{16,32},{48,64},{80,96},{112,128},{144,160},{176,192},{208,224},{2... | collective-permute-start | bytes 49160 | tf_op jit(solution)/shard_map/features_slab/ppermute | solution.py:626
  35.0 4.7 %collective-permute-start.4 = (f32[32,128]{1,0:T(8,128)S(1)}, f32[32,128]{1,0:T(8,128)S(1)}, u32[]{:S(2)}, u32[]{:S(2)}) collective-permute-start(f32[32,128]{1,0:T(8,128)S(1)} %get-tuple-element.164), channel_id=1, source_target_pairs={{0,16},{16,0},{32,48},{48,32},{64,80},{80,64},{96,112},{112,96},{1... | collective-permute-start | bytes 49160 | tf_op jit(solution)/shard_map/features_slab/ppermute | solution.py:631
  39.9 9.5 %collective-permute-start.5 = (f32[64,128]{1,0:T(8,128)S(1)}, f32[64,128]{1,0:T(8,128)S(1)}, u32[]{:S(2)}, u32[]{:S(2)}) collective-permute-start(f32[64,128]{1,0:T(8,128)S(1)} %get-tuple-element.168), channel_id=1, source_target_pairs={{1,2},{3,4},{5,6},{7,8},{9,10},{11,12},{13,14},{15,0},{2,1},{4,3},... | collective-permute-start | bytes 98312 | tf_op jit(solution)/shard_map/features_plane/ppermute | solution.py:637
  51.8 12.2 %collective-permute-start.6 = (f32[64,128]{1,0:T(8,128)S(1)}, f32[64,128]{1,0:T(8,128)S(1)}, u32[]{:S(2)}, u32[]{:S(2)}) collective-permute-start(f32[64,128]{1,0:T(8,128)S(1)} %get-tuple-element.178), channel_id=1, source_target_pairs={{1,2},{3,4},{5,6},{7,8},{9,10},{11,12},{13,14},{15,0},{2,1},{4,3},... | collective-permute-start | bytes 98312 | tf_op jit(solution)/shard_map/feature_grads_plane/ppermute | solution.py:637
  64.2 7.2 %collective-permute-start.7 = (f32[32,128]{1,0:T(8,128)S(1)}, f32[32,128]{1,0:T(8,128)S(1)}, u32[]{:S(2)}, u32[]{:S(2)}) collective-permute-start(f32[32,128]{1,0:T(8,128)S(1)} %get-tuple-element.192), channel_id=1, source_target_pairs={{16,32},{48,64},{80,96},{112,128},{144,160},{176,192},{208,224},{2... | collective-permute-start | bytes 49160 | tf_op jit(solution)/shard_map/feature_grads_slab/ppermute | solution.py:626
  66.4 5.0 %collective-permute-start.8 = (f32[32,128]{1,0:T(8,128)S(1)}, f32[32,128]{1,0:T(8,128)S(1)}, u32[]{:S(2)}, u32[]{:S(2)}) collective-permute-start(f32[32,128]{1,0:T(8,128)S(1)} %get-tuple-element.193), channel_id=1, source_target_pairs={{0,16},{16,0},{32,48},{48,32},{64,80},{80,64},{96,112},{112,96},{1... | collective-permute-start | bytes 49160 | tf_op jit(solution)/shard_map/feature_grads_slab/ppermute | solution.py:631
  73.4 9.5 %collective-permute-start.9 = (f32[8,64]{1,0:T(8,128)S(1)}, f32[8,64]{1,0:T(8,128)S(1)}, u32[]{:S(2)}, u32[]{:S(2)}) collective-permute-start(f32[8,64]{1,0:T(8,128)S(1)} %get-tuple-element.203), channel_id=1, source_target_pairs={{1,2},{3,4},{5,6},{7,8},{9,10},{11,12},{13,14},{15,0},{2,1},{4,3},... | collective-permute-start | bytes 6152 | tf_op jit(solution)/shard_map/position_grads_plane/ppermute | solution.py:637
  83.1 7.0 %collective-permute-start.10 = (f32[8,32]{1,0:T(8,128)S(1)}, f32[8,32]{1,0:T(8,128)S(1)}, u32[]{:S(2)}, u32[]{:S(2)}) collective-permute-start(f32[8,32]{1,0:T(8,128)S(1)} %get-tuple-element.206), channel_id=1, source_target_pairs={{16,32},{48,64},{80,96},{112,128},{144,160},{176,192},{208,224},{2... | collective-permute-start | bytes 3080 | tf_op jit(solution)/shard_map/position_grads_slab/ppermute | solution.py:626
  87.6 3.1 %collective-permute-start.11 = (f32[8,32]{1,0:T(8,128)S(1)}, f32[8,32]{1,0:T(8,128)S(1)}, u32[]{:S(2)}, u32[]{:S(2)}) collective-permute-start(f32[8,32]{1,0:T(8,128)S(1)} %get-tuple-element.207), channel_id=1, source_target_pairs={{0,16},{16,0},{32,48},{48,32},{64,80},{80,64},{96,112},{112,96},{1... | collective-permute-start | bytes 3080 | tf_op jit(solution)/shard_map/position_grads_slab/ppermute | solution.py:631

commit v4 on v3

--- a/solution.py
+++ b/solution.py
@@ -29,8 +29,9 @@
 FIRST_LM = (0, 1, 4)
 STACK_AT = (0, 48, 192)
 STACK = 432
-TURNED_AT = (0, 128, 384)
-TURNED = 640
+PAIR_ROWS = 192
+TURNED_AT = 256
+TURNED = 512
 R3, R5, R15 = 3.0**0.5, 5.0**0.5, 15.0**0.5
 
 NN = (((1,), (0,)), ((), ()))
@@ -88,12 +89,16 @@
     return (o[:, :C] + o[:, C : 2 * C]) + o[:, 2 * C :]
 
 
+def sigmoid(x):
+    return 0.5 + 0.5 * jnp.tanh(0.5 * x)
+
+
 def silu(x):
-    return x * (1.0 / (1.0 + jnp.exp(-x)))
+    return x * sigmoid(x)
 
 
 def silu_pair(x):
-    s = 1.0 / (1.0 + jnp.exp(-x))
+    s = sigmoid(x)
     return x * s, s * (1.0 + x * (1.0 - s))
 
 
@@ -275,17 +280,6 @@
     return kinds.astype(f32)
 
 
-def near_atoms_kernel(v_ref, pf_ref, pn_ref, dd_ref, table_ref, vector_ref, lifted_ref):
-    vector, at = None, 0
-    for ref in (v_ref, pf_ref, pn_ref):
-        rows = ref.shape[1]
-        piece = pick_lanes(ref[...], dd_ref[at : at + rows, :])
-        vector = piece if vector is None else vector + piece
-        lifted_ref[at : at + rows, :] = dot(kinds_of(ref[3:4, :]).astype(bf16), table_ref[...], TN).astype(bf16)
-        at += rows
-    vector_ref[...] = vector
-
-
 def geometry(v, valid, b_ref, db_ref, geo_ref):
     vx = jnp.where(valid, v[0:1], 2.0 * cutoff_radius)
     vy = jnp.where(valid, v[1:2], 0.0)
@@ -407,10 +401,18 @@
     )
 
 
-def spread(turned_ref, ga_ref, b, l):
-    hi, lo = split(group_grads(ga_ref, b, l))
-    angular = turned_ref[span(b), TURNED_AT[l] : TURNED_AT[l] + 48 * LMS[l]]
-    return dot(angular, jnp.concatenate([hi, hi, lo], axis=0))
+def spread(turned_ref, ga_ref, b):
+    pieces = [split(group_grads(ga_ref, b, l)) for l in range(3)]
+    rows = []
+    for l in range(2):
+        hi, lo = pieces[l]
+        none = jnp.zeros_like(hi)
+        for part in (hi, hi, lo):
+            rows.append(jnp.concatenate([part, none] if l == 0 else [none, part], axis=1))
+    first = dot(turned_ref[span(b), 0:PAIR_ROWS], jnp.concatenate(rows, axis=0))
+    hi, lo = pieces[2]
+    last = turned_ref[span(b), TURNED_AT : TURNED_AT + STACK - PAIR_ROWS]
+    return first[:, :C], first[:, C:], dot(last, jnp.concatenate([hi, hi, lo], axis=0))
 
 
 def angular_grads(m_ref, ga_ref, mask_ref, gy_ref):
@@ -446,16 +448,21 @@
 
 
 def first_kernel(
-    v_ref, vector_ref, lifted_ref, qf_ref, qn_ref, dd_ref, g_ref, mask_ref, table_ref, skip_ref, w1_ref, w2_ref, w3_ref, w4_ref,
+    v_ref, pf_ref, pn_ref, qf_ref, qn_ref, dd_ref, g_ref, mask_ref, table_ref, skip_ref, w1_ref, w2_ref, w3_ref, w4_ref,
     gain_ref, outup_ref, tf_ref, tn_ref,
     f_ref, sf_ref, sn_ref, mix_ref, amp_ref, l_ref, m_ref, ast_ref, b_ref, db_ref, geo_ref,
 ):
     step = (2 * odd("plane") - 1).astype(f32) * (CELLS_Y * cell_side)
     far, near = shifted(qf_ref[...], 1, step), shifted(partner_of(qn_ref), 1, -step)
     valid = jnp.sum(mask_ref[...], axis=0, keepdims=True) > 0.5
-    vector = vector_ref[...] + (pick_lanes(far, dd_ref[128:192, :]) + pick_lanes(near, dd_ref[192:256, :]))
-    lifted = [dot(kinds_of(part[3:4]).astype(bf16), table_ref[...], TN).astype(bf16) for part in (far, near)]
-    lifted = jnp.concatenate([lifted_ref[...]] + lifted, axis=0)
+    vector, lifted, at = None, [], 0
+    for part in (v_ref[...], pf_ref[...], pn_ref[...], far, near):
+        rows = part.shape[1]
+        piece = pick_lanes(part, dd_ref[at : at + rows, :])
+        vector = piece if vector is None else vector + piece
+        lifted.append(dot(kinds_of(part[3:4]).astype(bf16), table_ref[...], TN).astype(bf16))
+        at += rows
+    lifted = jnp.concatenate(lifted, axis=0)
     o = dot(kinds_of(v_ref[3:4, :]).astype(bf16), skip_ref[...], TN)
     skipped = (o[:, :C] + o[:, C : 2 * C]) + o[:, 2 * C :]
     geometry(vector, valid, b_ref, db_ref, geo_ref)
@@ -515,9 +522,9 @@
     ast_ref, r_ref, second_q_ref, first_q_ref, hid_ref, e_ref, turned_ref,
 ):
     for b in range(BLOCKS):
-        for l in range(3):
-            rows = ast_ref[pl.ds(b * STACK + STACK_AT[l], 48 * LMS[l]), :]
-            turned_ref[span(b), TURNED_AT[l] : TURNED_AT[l] + 48 * LMS[l]] = jnp.transpose(rows)
+        turned_ref[span(b), 0:PAIR_ROWS] = jnp.transpose(ast_ref[pl.ds(b * STACK, PAIR_ROWS), :])
+        rest = ast_ref[pl.ds(b * STACK + PAIR_ROWS, STACK - PAIR_ROWS), :]
+        turned_ref[span(b), TURNED_AT : TURNED_AT + STACK - PAIR_ROWS] = jnp.transpose(rest)
     slope_kernel(b_ref, db_ref, geo_ref, w1_ref, w2_ref, w3_ref, first_q_ref, layer=0)
     radial_kernel(b_ref, db_ref, geo_ref, w1_ref, w2_ref, w3_ref, w4_ref, r_ref, second_q_ref, layer=1)
     own_terms_kernel(v_ref, mix_ref, skip_ref, out0_ref, ref_ref, one_ref, from_first_ref, hid_ref, e_ref)
@@ -540,8 +547,8 @@
     amp_grads(amp_ref, gain, dot3(slope, from_mix_ro_ref[...], TN), ga_ref)
     for b in range(BLOCKS):
         grad = None
-        for l in range(3):
-            term = r_ref[span(b), l * C : (l + 1) * C] * spread(turned_ref, ga_ref, b, l)
+        for l, z in enumerate(spread(turned_ref, ga_ref, b)):
+            term = r_ref[span(b), l * C : (l + 1) * C] * z
             grad = term if grad is None else grad + term
         glift_ref[span(b), :] = pair_lanes(grad)
     glift = halves(dot(gt_ref[...], glift_ref[...]))
@@ -559,7 +566,7 @@
 def early_kernel(turned_ref, q_ref, w4_ref, l_ref, m_ref, ga_ref, geo_ref, mask_ref, gv_ref, x_ref, gy_ref):
     for b in range(BLOCKS):
         slope = dot(q_ref[:, span(b)], w4_ref[1], TN)
-        x = sum(spread(turned_ref, ga_ref, b, l) * slope[:, l * C : (l + 1) * C] for l in range(3))
+        x = sum(z * slope[:, l * C : (l + 1) * C] for l, z in enumerate(spread(turned_ref, ga_ref, b)))
         x_ref[span(b), :] = pair_lanes(x * l_ref[span(b), :])
     angular_grads(m_ref, ga_ref, mask_ref, gy_ref)
     edge_forces(x_ref, gy_ref, geo_ref, gv_ref)
@@ -590,8 +597,8 @@
     amp_grads(amp_ref, gain_ref[0], gm_ref[...] + dot3(grad, outup_ref[...], NT), ga_ref)
     for b in range(BLOCKS):
         x = None
-        for l in range(3):
-            term = spread(turned_ref, ga_ref, b, l) * dr_ref[span(b), l * C : (l + 1) * C]
+        for l, z in enumerate(spread(turned_ref, ga_ref, b)):
+            term = z * dr_ref[span(b), l * C : (l + 1) * C]
             x = term if x is None else x + term
         x_ref[span(b), :] = pair_lanes(x * l_ref[span(b), :])
     angular_grads(m_ref, ga_ref, mask_ref, gy_ref)
@@ -713,19 +720,14 @@
             name="atoms_plane",
         )
         far, near = both(swap_plane_far, swap_plane_near, far, near)
-        vector, lifted = call(
-            near_atoms_kernel, [edge_rows, ((128, 2 * C), bf16)], (values, slab_far, slab_near, edge_t, table),
-            flops=1_000_000_000, name="near_atoms",
-        )
 
     hidden_mat = ((16, OWN), f32)
     with jax.named_scope("first_layer"):
-        far, near, vector, lifted = lax.optimization_barrier((far, near, vector, lifted))
         (first, s_far, s_near, mix, amp_first, lift_first, message_first, angular, basis, basis_slope, geo) = call(
             first_kernel,
             [plane_rows, slab_rows, slab_rows, plane_rows, amp_mat, edge_mat, message_mat,
              ((BLOCKS * STACK, SPAN), bf16), edge_rows, edge_rows, edge_rows],
-            (values, vector, lifted, far, near, edge_t, sender_n, mask, table, skip_up_table, *weights,
+            (values, slab_far, slab_near, far, near, edge_t, sender_n, mask, table, skip_up_table, *weights,
              gains, out_up, slab_t_far, slab_t_near),
             name="first_layer",
         )
@@ -789,7 +791,7 @@
     with jax.named_scope("position_grads_slab"):
         far, near = both(swap_slab_far, swap_slab_near, far, near)
         forces, = call(
-            collect_slab_kernel, [((1, 3, 1, OWN), f32)], (own, far, near, slab_t_far, slab_t_near), name="collect_slab"
+            collect_slab_kernel, [((1, 3, 1, OWN), f32)], (own, far, near, slab_t_far, slab_t_near), name="collect_slab",
         )
     return (energies[None], jnp.transpose(forces, (0, 2, 1, 3)))
 

time: 92.2 us -> 91.3 us (level)
    pallas_call x13 -> x12, Pallas kernels: 16.1 us -> 15.4 us  [call(): pl.pallas_call(kernel, out_shape=out_shape, in_specs=in_specs, out_specs=...]
where the time goes in v4:
time: 91.3 us; the launch traced here: 90.5 us
  starting transfers between devices  47.1 us (52%)
  blocking collectives  24.5 us (27%)
  Pallas kernels  15.4 us (17%)
  waiting for transfers between devices  1.59 us (2%)
  local copies, waits for them, and re-layouts  1.09 us (1%)
    all_gather x4, blocking collectives, swap_plane_near(): lax.all_gather(value, 'plane', axis_index_groups=[[i, i + 1] for i in ran...  24.5 us
    ppermute x4, starting transfers between devices, swap_plane_far(): return lax.ppermute(value, 'plane', pairs + [(b, a) for a, b in pairs])  19.8 us
    ppermute x4, starting transfers between devices, swap_slab_far(): return lax.ppermute(value, 'slab', pairs + [(b, a) for a, b in pairs])  19.7 us
    pallas_call x12, Pallas kernels, call(): pl.pallas_call(kernel, out_shape=out_shape, in_specs=in_specs, out_specs=...  15.4 us
    ppermute x4, starting transfers between devices, swap_slab_near(): return lax.ppermute(value, 'slab', [(i, i ^ 1) for i in range(count)])  7.68 us
  transfers between devices with their start and end apart: 12, of which 3 were waited for; matrix products, arithmetic and copies ran while one was open for 1% of the time, Pallas kernels for 7%

profile of v4, /device:TPU:2, one launch (start us, length us, event | category | flops | bytes accessed | tf_op | source)
XLA Modules:
  0.0 90.5 jit_solution(1713965694902790086)
XLA Ops:
  0.6 1.5 %atoms_slab.1 = (s32[2,1536]{1,0:T(2,128)S(1)}, f32[2,8,64]{2,1,0:T(8,128)S(1)}, f32[2,64,64]{2,1,0:T(8,128)S(1)}, f32[2,64,64]{2,1,0:T(8,128)S(1)}, f32[2,64,38...) custom-call(f32[1,3,1,64]{3,2,1,0:T(1,128)} %bitcast.25, ...), custom_call_target="tpu_custom_call" | custom-call | bytes 732324 | tf_op jit(solution)/shard_map/atoms_slab/atoms_slab/pallas_call | solution.py:141
  2.1 10.4 %collective-permute-start = (f32[8,32]{1,0:T(8,128)S(1)}, f32[8,32]{1,0:T(8,128)S(1)}, u32[]{:S(2)}, u32[]{:S(2)}) collective-permute-start(f32[8,32]{1,0:T(8,128)S(1)} %get-tuple-element.100), channel_id=1, source_target_pairs={{16,32},{48,64},{80,96},{112,128},{144,160},{176,192},{208,224},{2... | collective-permute-start | bytes 3080 | tf_op jit(solution)/shard_map/atoms_slab/ppermute | solution.py:633
  12.5 1.9 %collective-permute-start.1 = (f32[8,32]{1,0:T(8,128)S(1)}, f32[8,32]{1,0:T(8,128)S(1)}, u32[]{:S(2)}, u32[]{:S(2)}) collective-permute-start(f32[8,32]{1,0:T(8,128)S(1)} %get-tuple-element.101), channel_id=1, source_target_pairs={{0,16},{16,0},{32,48},{48,32},{64,80},{80,64},{96,112},{112,96},{1... | collective-permute-start | bytes 3080 | tf_op jit(solution)/shard_map/atoms_slab/ppermute | solution.py:638
  14.4 1.1 %prepare.1 = (bf16[1536,256]{1,0:T(8,128)(2,1)S(1)}, bf16[256,1536]{1,0:T(8,128)(2,1)S(1)}, bf16[256,1536]{1,0:T(8,128)(2,1)S(1)}, f32[16,1536]{1,0:T(8,128)S(1)...) custom-call(s32[2,1536]{1,0:T(2,128)S(1)} %get-tuple-element.102.edg, ...), custom_call_target="tpu_custom_call" | custom-call | flops 1000000000 | bytes 730532 | tf_op jit(solution)/shard_map/prepare/prepare/pallas_call | solution.py:141
  15.6 0.2 atoms_plane.1
  15.7 7.2 %collective-permute-start.2 = (f32[8,64]{1,0:T(8,128)S(1)}, f32[8,64]{1,0:T(8,128)S(1)}, u32[]{:S(2)}, u32[]{:S(2)}) collective-permute-start(f32[8,64]{1,0:T(8,128)S(1)} %get-tuple-element.123), channel_id=1, source_target_pairs={{1,2},{3,4},{5,6},{7,8},{9,10},{11,12},{13,14},{15,0},{2,1},{4,3},... | collective-permute-start | bytes 6152 | tf_op jit(solution)/shard_map/atoms_plane/ppermute | solution.py:644
  23.0 5.8 %all-gather = f32[16,64]{1,0:T(8,128)S(1)} all-gather(f32[8,64]{1,0:T(8,128)S(1)} %get-tuple-element.124), channel_id=2, replica_groups={{0,1},{2,3},{4,5},{6,7},{8,9},{10,11},{12,13},{14,15},{16,17},{18,19},{..., dimensions={0}, use_global_device_ids=true | all-gather | bytes 6144 | tf_op jit(solution)/shard_map/atoms_plane/all_gather | solution.py:649
  28.8 2.8 %first_layer.1 = (f32[64,128]{1,0:T(8,128)S(1)}, f32[32,128]{1,0:T(8,128)S(1)}, f32[32,128]{1,0:T(8,128)S(1)}, f32[64,128]{1,0:T(8,128)S(1)}, f32[9,64,128]{2,1,...) custom-call(f32[8,64]{1,0:T(8,128)S(1)} %get-tuple-element.99.v_ref,, ...), custom_call_target="tpu_custom_call" | custom-call | bytes 2283520 | tf_op jit(solution)/shard_map/first_layer/first_layer/pallas_call | solution.py:141
  31.6 3.1 %collective-permute-start.3 = (f32[32,128]{1,0:T(8,128)S(1)}, f32[32,128]{1,0:T(8,128)S(1)}, u32[]{:S(2)}, u32[]{:S(2)}) collective-permute-start(f32[32,128]{1,0:T(8,128)S(1)} %get-tuple-element.151), channel_id=1, source_target_pairs={{16,32},{48,64},{80,96},{112,128},{144,160},{176,192},{208,224},{2... | collective-permute-start | bytes 49160 | tf_op jit(solution)/shard_map/features_slab/ppermute | solution.py:633
  34.8 1.9 %collective-permute-start.4 = (f32[32,128]{1,0:T(8,128)S(1)}, f32[32,128]{1,0:T(8,128)S(1)}, u32[]{:S(2)}, u32[]{:S(2)}) collective-permute-start(f32[32,128]{1,0:T(8,128)S(1)} %get-tuple-element.152), channel_id=1, source_target_pairs={{0,16},{16,0},{32,48},{48,32},{64,80},{80,64},{96,112},{112,96},{1... | collective-permute-start | bytes 49160 | tf_op jit(solution)/shard_map/features_slab/ppermute | solution.py:638
  36.7 2.6 %beside_features.1 = (f32[1536,384]{1,0:T(8,128)S(1)}, bf16[192,1536]{1,0:T(8,128)(2,1)S(1)}, bf16[192,1536]{1,0:T(8,128)(2,1)S(1)}, f32[16,64]{1,0:T(8,128)S(1)...) custom-call(f32[8,1536]{1,0:T(8,128)S(1)} %get-tuple-element.138.b_ref, f32[8,1536]{1,0:T(8,128)S(1)} %get-tuple-element.139.db_ref, ...), custom_call_target="tpu_custom_call" | custom-call | flops 1000000000 | bytes 2061824 | tf_op jit(solution)/shard_map/beside_features/pallas_call | solution.py:141
  39.3 0.2 middle.1
  39.6 2.9 %collective-permute-start.5 = (f32[64,128]{1,0:T(8,128)S(1)}, f32[64,128]{1,0:T(8,128)S(1)}, u32[]{:S(2)}, u32[]{:S(2)}) collective-permute-start(f32[64,128]{1,0:T(8,128)S(1)} %get-tuple-element.156), channel_id=1, source_target_pairs={{1,2},{3,4},{5,6},{7,8},{9,10},{11,12},{13,14},{15,0},{2,1},{4,3},... | collective-permute-start | bytes 98312 | tf_op jit(solution)/shard_map/features_plane/ppermute | solution.py:644
  42.5 6.7 %all-gather.1 = f32[128,128]{1,0:T(8,128)S(1)} all-gather(f32[64,128]{1,0:T(8,128)S(1)} %get-tuple-element.157), channel_id=3, replica_groups={{0,1},{2,3},{4,5},{6,7},{8,9},{10,11},{12,13},{14,15},{16,17},{18,19},{..., dimensions={0}, use_global_device_ids=true | all-gather | bytes 98304 | tf_op jit(solution)/shard_map/features_plane/all_gather | solution.py:649
  49.2 2.3 %second_layer.1 = (f32[16,64]{1,0:T(8,128)S(1)}, f32[16,64]{1,0:T(8,128)S(1)}, f32[128,128]{1,0:T(8,128)S(1)}, f32[64,128]{1,0:T(8,128)S(1)}, f32[64,128]{1,0:T(...) custom-call(f32[64,128]{1,0:T(8,128)S(1)} %get-tuple-element.150.f_ref, ...), custom_call_target="tpu_custom_call" | custom-call | bytes 7020544 | tf_op jit(solution)/shard_map/second_layer/second_layer/pallas_call | solution.py:141
  51.5 5.9 %collective-permute-start.6 = (f32[64,128]{1,0:T(8,128)S(1)}, f32[64,128]{1,0:T(8,128)S(1)}, u32[]{:S(2)}, u32[]{:S(2)}) collective-permute-start(f32[64,128]{1,0:T(8,128)S(1)} %get-tuple-element.166), channel_id=1, source_target_pairs={{1,2},{3,4},{5,6},{7,8},{9,10},{11,12},{13,14},{15,0},{2,1},{4,3},... | collective-permute-start | bytes 98312 | tf_op jit(solution)/shard_map/feature_grads_plane/ppermute | solution.py:644
  57.4 6.1 %all-gather.2 = f32[128,128]{1,0:T(8,128)S(1)} all-gather(f32[64,128]{1,0:T(8,128)S(1)} %get-tuple-element.167), channel_id=4, replica_groups={{0,1},{2,3},{4,5},{6,7},{8,9},{10,11},{12,13},{14,15},{16,17},{18,19},{..., dimensions={0}, use_global_device_ids=true | all-gather | bytes 98304 | tf_op jit(solution)/shard_map/feature_grads_plane/all_gather | solution.py:649
  63.5 0.2 back_middle.1
  63.7 2.0 %collective-permute-start.7 = (f32[32,128]{1,0:T(8,128)S(1)}, f32[32,128]{1,0:T(8,128)S(1)}, u32[]{:S(2)}, u32[]{:S(2)}) collective-permute-start(f32[32,128]{1,0:T(8,128)S(1)} %get-tuple-element.180), channel_id=1, source_target_pairs={{16,32},{48,64},{80,96},{112,128},{144,160},{176,192},{208,224},{2... | collective-permute-start | bytes 49160 | tf_op jit(solution)/shard_map/feature_grads_slab/ppermute | solution.py:633
  65.7 1.9 %collective-permute-start.8 = (f32[32,128]{1,0:T(8,128)S(1)}, f32[32,128]{1,0:T(8,128)S(1)}, u32[]{:S(2)}, u32[]{:S(2)}) collective-permute-start(f32[32,128]{1,0:T(8,128)S(1)} %get-tuple-element.181), channel_id=1, source_target_pairs={{0,16},{16,0},{32,48},{48,32},{64,80},{80,64},{96,112},{112,96},{1... | collective-permute-start | bytes 49160 | tf_op jit(solution)/shard_map/feature_grads_slab/ppermute | solution.py:638
  67.6 2.3 %beside_grads.1 = (f32[8,1536]{1,0:T(8,128)S(1)}, f32[1536,384]{1,0:T(8,128)S(1)}, f32[1,64]{1,0:T(1,128)S(1)}, f32[64,128]{1,0:T(8,128)S(1)}) custom-call(bf16[1536,512]{1,0:T(8,128)(2,1)S(1)} %get-tuple-element.148.turned_ref, bf16[192,1536]{1,0:T(8,128)(2,1)S(1)} %get-tuple-element.149.second_q_ref, bf16[2,192,384]{2,1,0:T(8,128)(2,1)S(1)} %get-tuple-element.133.w4_ref, ...), custom_call_target="tpu_custom_call" | custom-call | flops 1000000000 | bytes 6720512 | tf_op jit(solution)/shard_map/beside_grads/pallas_call | solution.py:141
  70.0 0.9 %collective-permute-done.7.rf_ref = f32[32,128]{1,0:T(8,128)S(1)} collective-permute-done((f32[32,128]{1,0:T(8,128)S(1)}, f32[32,128]{1,0:T(8,128)S(1)}, u32[]{:S(2)}, u32[]{:S(2)}) %collective-permute-start.7) | collective-permute-done | bytes 16416 | tf_op jit(solution)/shard_map/feature_grads_slab/ppermute | solution.py:633
  70.9 1.9 %late_forces.1 = (f32[8,64]{1,0:T(8,128)S(1)}, f32[8,32]{1,0:T(8,128)S(1)}, f32[8,32]{1,0:T(8,128)S(1)}, f32[8,64]{1,0:T(8,128)S(1)}, f32[8,64]{1,0:T(8,128)S(1)}) custom-call(f32[64,128]{1,0:T(8,128)S(1)} %get-tuple-element.179.own_ref, f32[32,128]{1,0:T(8,128)S(1)} %collective-permute-done.7.rf_ref, f32[32,128]{1,0:T(8,128)S(1)} %collective-permute-done.8.rn_ref, ...), custom_call_target="tpu_custom_call" | custom-call | bytes 8531968 | tf_op jit(solution)/shard_map/late_forces/late_forces/pallas_call | solution.py:141
  72.8 3.7 %collective-permute-start.9 = (f32[8,64]{1,0:T(8,128)S(1)}, f32[8,64]{1,0:T(8,128)S(1)}, u32[]{:S(2)}, u32[]{:S(2)}) collective-permute-start(f32[8,64]{1,0:T(8,128)S(1)} %get-tuple-element.191), channel_id=1, source_target_pairs={{1,2},{3,4},{5,6},{7,8},{9,10},{11,12},{13,14},{15,0},{2,1},{4,3},... | collective-permute-start | bytes 6152 | tf_op jit(solution)/shard_map/position_grads_plane/ppermute | solution.py:644
  76.5 5.8 %all-gather.3 = f32[16,64]{1,0:T(8,128)S(1)} all-gather(f32[8,64]{1,0:T(8,128)S(1)} %get-tuple-element.192), channel_id=5, replica_groups={{0,1},{2,3},{4,5},{6,7},{8,9},{10,11},{12,13},{14,15},{16,17},{18,19},{..., dimensions={0}, use_global_device_ids=true | all-gather | bytes 6144 | tf_op jit(solution)/shard_map/position_grads_plane/all_gather | solution.py:649
  82.3 0.2 collect_plane.1
  82.5 4.2 %collective-permute-start.10 = (f32[8,32]{1,0:T(8,128)S(1)}, f32[8,32]{1,0:T(8,128)S(1)}, u32[]{:S(2)}, u32[]{:S(2)}) collective-permute-start(f32[8,32]{1,0:T(8,128)S(1)} %get-tuple-element.194), channel_id=1, source_target_pairs={{16,32},{48,64},{80,96},{112,128},{144,160},{176,192},{208,224},{2... | collective-permute-start | bytes 3080 | tf_op jit(solution)/shard_map/position_grads_slab/ppermute | solution.py:633
  86.7 1.9 %collective-permute-start.11 = (f32[8,32]{1,0:T(8,128)S(1)}, f32[8,32]{1,0:T(8,128)S(1)}, u32[]{:S(2)}, u32[]{:S(2)}) collective-permute-start(f32[8,32]{1,0:T(8,128)S(1)} %get-tuple-element.195), channel_id=1, source_target_pairs={{0,16},{16,0},{32,48},{48,32},{64,80},{80,64},{96,112},{112,96},{1... | collective-permute-start | bytes 3080 | tf_op jit(solution)/shard_map/position_grads_slab/ppermute | solution.py:638
  88.6 0.5 copy.21
  89.1 0.4 collective-permute-done.10.rf_ref
  89.5 0.2 collective-permute-done.11.rn_ref
  89.9 0.6 copy.22
  (10 shorter events, 0.2 us)
Async XLA Ops:
  2.1 13.4 %collective-permute-start = (f32[8,32]{1,0:T(8,128)S(1)}, f32[8,32]{1,0:T(8,128)S(1)}, u32[]{:S(2)}, u32[]{:S(2)}) collective-permute-start(f32[8,32]{1,0:T(8,128)S(1)} %get-tuple-element.100), channel_id=1, source_target_pairs={{16,32},{48,64},{80,96},{112,128},{144,160},{176,192},{208,224},{2... | collective-permute-start | bytes 3080 | tf_op jit(solution)/shard_map/atoms_slab/ppermute | solution.py:633
  12.5 3.1 %collective-permute-start.1 = (f32[8,32]{1,0:T(8,128)S(1)}, f32[8,32]{1,0:T(8,128)S(1)}, u32[]{:S(2)}, u32[]{:S(2)}) collective-permute-start(f32[8,32]{1,0:T(8,128)S(1)} %get-tuple-element.101), channel_id=1, source_target_pairs={{0,16},{16,0},{32,48},{48,32},{64,80},{80,64},{96,112},{112,96},{1... | collective-permute-start | bytes 3080 | tf_op jit(solution)/shard_map/atoms_slab/ppermute | solution.py:638
  15.7 13.1 %collective-permute-start.2 = (f32[8,64]{1,0:T(8,128)S(1)}, f32[8,64]{1,0:T(8,128)S(1)}, u32[]{:S(2)}, u32[]{:S(2)}) collective-permute-start(f32[8,64]{1,0:T(8,128)S(1)} %get-tuple-element.123), channel_id=1, source_target_pairs={{1,2},{3,4},{5,6},{7,8},{9,10},{11,12},{13,14},{15,0},{2,1},{4,3},... | collective-permute-start | bytes 6152 | tf_op jit(solution)/shard_map/atoms_plane/ppermute | solution.py:644
  31.6 7.7 %collective-permute-start.3 = (f32[32,128]{1,0:T(8,128)S(1)}, f32[32,128]{1,0:T(8,128)S(1)}, u32[]{:S(2)}, u32[]{:S(2)}) collective-permute-start(f32[32,128]{1,0:T(8,128)S(1)} %get-tuple-element.151), channel_id=1, source_target_pairs={{16,32},{48,64},{80,96},{112,128},{144,160},{176,192},{208,224},{2... | collective-permute-start | bytes 49160 | tf_op jit(solution)/shard_map/features_slab/ppermute | solution.py:633
  34.8 4.6 %collective-permute-start.4 = (f32[32,128]{1,0:T(8,128)S(1)}, f32[32,128]{1,0:T(8,128)S(1)}, u32[]{:S(2)}, u32[]{:S(2)}) collective-permute-start(f32[32,128]{1,0:T(8,128)S(1)} %get-tuple-element.152), channel_id=1, source_target_pairs={{0,16},{16,0},{32,48},{48,32},{64,80},{80,64},{96,112},{112,96},{1... | collective-permute-start | bytes 49160 | tf_op jit(solution)/shard_map/features_slab/ppermute | solution.py:638
  39.6 9.7 %collective-permute-start.5 = (f32[64,128]{1,0:T(8,128)S(1)}, f32[64,128]{1,0:T(8,128)S(1)}, u32[]{:S(2)}, u32[]{:S(2)}) collective-permute-start(f32[64,128]{1,0:T(8,128)S(1)} %get-tuple-element.156), channel_id=1, source_target_pairs={{1,2},{3,4},{5,6},{7,8},{9,10},{11,12},{13,14},{15,0},{2,1},{4,3},... | collective-permute-start | bytes 98312 | tf_op jit(solution)/shard_map/features_plane/ppermute | solution.py:644
  51.5 12.0 %collective-permute-start.6 = (f32[64,128]{1,0:T(8,128)S(1)}, f32[64,128]{1,0:T(8,128)S(1)}, u32[]{:S(2)}, u32[]{:S(2)}) collective-permute-start(f32[64,128]{1,0:T(8,128)S(1)} %get-tuple-element.166), channel_id=1, source_target_pairs={{1,2},{3,4},{5,6},{7,8},{9,10},{11,12},{13,14},{15,0},{2,1},{4,3},... | collective-permute-start | bytes 98312 | tf_op jit(solution)/shard_map/feature_grads_plane/ppermute | solution.py:644
  63.7 7.2 %collective-permute-start.7 = (f32[32,128]{1,0:T(8,128)S(1)}, f32[32,128]{1,0:T(8,128)S(1)}, u32[]{:S(2)}, u32[]{:S(2)}) collective-permute-start(f32[32,128]{1,0:T(8,128)S(1)} %get-tuple-element.180), channel_id=1, source_target_pairs={{16,32},{48,64},{80,96},{112,128},{144,160},{176,192},{208,224},{2... | collective-permute-start | bytes 49160 | tf_op jit(solution)/shard_map/feature_grads_slab/ppermute | solution.py:633
  65.7 5.2 %collective-permute-start.8 = (f32[32,128]{1,0:T(8,128)S(1)}, f32[32,128]{1,0:T(8,128)S(1)}, u32[]{:S(2)}, u32[]{:S(2)}) collective-permute-start(f32[32,128]{1,0:T(8,128)S(1)} %get-tuple-element.181), channel_id=1, source_target_pairs={{0,16},{16,0},{32,48},{48,32},{64,80},{80,64},{96,112},{112,96},{1... | collective-permute-start | bytes 49160 | tf_op jit(solution)/shard_map/feature_grads_slab/ppermute | solution.py:638
  72.8 9.5 %collective-permute-start.9 = (f32[8,64]{1,0:T(8,128)S(1)}, f32[8,64]{1,0:T(8,128)S(1)}, u32[]{:S(2)}, u32[]{:S(2)}) collective-permute-start(f32[8,64]{1,0:T(8,128)S(1)} %get-tuple-element.191), channel_id=1, source_target_pairs={{1,2},{3,4},{5,6},{7,8},{9,10},{11,12},{13,14},{15,0},{2,1},{4,3},... | collective-permute-start | bytes 6152 | tf_op jit(solution)/shard_map/position_grads_plane/ppermute | solution.py:644
  82.5 7.0 %collective-permute-start.10 = (f32[8,32]{1,0:T(8,128)S(1)}, f32[8,32]{1,0:T(8,128)S(1)}, u32[]{:S(2)}, u32[]{:S(2)}) collective-permute-start(f32[8,32]{1,0:T(8,128)S(1)} %get-tuple-element.194), channel_id=1, source_target_pairs={{16,32},{48,64},{80,96},{112,128},{144,160},{176,192},{208,224},{2... | collective-permute-start | bytes 3080 | tf_op jit(solution)/shard_map/position_grads_slab/ppermute | solution.py:633
  86.7 3.1 %collective-permute-start.11 = (f32[8,32]{1,0:T(8,128)S(1)}, f32[8,32]{1,0:T(8,128)S(1)}, u32[]{:S(2)}, u32[]{:S(2)}) collective-permute-start(f32[8,32]{1,0:T(8,128)S(1)} %get-tuple-element.195), channel_id=1, source_target_pairs={{0,16},{16,0},{32,48},{48,32},{64,80},{80,64},{96,112},{112,96},{1... | collective-permute-start | bytes 3080 | tf_op jit(solution)/shard_map/position_grads_slab/ppermute | solution.py:638

commit v5 on v4

--- a/solution.py
+++ b/solution.py
@@ -488,8 +488,8 @@
 def own_terms_kernel(v_ref, mix_ref, skip_ref, out0_ref, ref_ref, one_ref, from_first_ref, hid_ref, e_ref):
     kinds = kinds_of(v_ref[3:4, :])
     o = dot(kinds.astype(bf16), skip_ref[...], TN)
-    first = ((o[:, :C] + o[:, C : 2 * C]) + o[:, 2 * C :]) + exact(mix_ref[...], out0_ref[...])
-    hid_ref[...] = exact(from_first_ref[...], first, NT)
+    first = ((o[:, :C] + o[:, C : 2 * C]) + o[:, 2 * C :]) + dot3(mix_ref[...], out0_ref[...])
+    hid_ref[...] = dot3(from_first_ref[...], first, NT)
     e_ref[...] = exact(ref_ref[...], kinds) + exact(jnp.broadcast_to(one_ref[...], (8, C)), first, NT)
 
 
@@ -541,7 +541,7 @@
     messages(g_ref, lifted, lambda b: r_ref[span(b), :], l_ref, m_ref)
     amplitudes(ast_ref, m_ref, amp_ref)
     gain = gain_ref[1]
-    act, slope = silu_pair(hid_ref[...] + exact(from_mix_ref[...], invariants(amp_ref, gain), NT))
+    act, slope = silu_pair(hid_ref[...] + dot3(from_mix_ref[...], invariants(amp_ref, gain), NT))
     act_ref[...] = act
     slope_ref[...] = slope
     amp_grads(amp_ref, gain, dot3(slope, from_mix_ro_ref[...], TN), ga_ref)

time: 91.3 us -> 91.3 us (level)
  no operation moved by 1% of the time
where the time goes in v5:
time: 91.3 us; the launch traced here: 90.4 us
  starting transfers between devices  47.1 us (52%)
  blocking collectives  24.5 us (27%)
  Pallas kernels  15.4 us (17%)
  waiting for transfers between devices  1.59 us (2%)
  local copies, waits for them, and re-layouts  1.09 us (1%)
    all_gather x4, blocking collectives, swap_plane_near(): lax.all_gather(value, 'plane', axis_index_groups=[[i, i + 1] for i in ran...  24.5 us
    ppermute x4, starting transfers between devices, swap_plane_far(): return lax.ppermute(value, 'plane', pairs + [(b, a) for a, b in pairs])  19.8 us
    ppermute x4, starting transfers between devices, swap_slab_far(): return lax.ppermute(value, 'slab', pairs + [(b, a) for a, b in pairs])  19.7 us
    pallas_call x12, Pallas kernels, call(): pl.pallas_call(kernel, out_shape=out_shape, in_specs=in_specs, out_specs=...  15.4 us
    ppermute x4, starting transfers between devices, swap_slab_near(): return lax.ppermute(value, 'slab', [(i, i ^ 1) for i in range(count)])  7.68 us
  transfers between devices with their start and end apart: 12, of which 3 were waited for; matrix products, arithmetic and copies ran while one was open for 1% of the time, Pallas kernels for 7%

profile of v5, /device:TPU:2, one launch (start us, length us, event | category | flops | bytes accessed | tf_op | source)
XLA Modules:
  0.0 90.4 jit_solution(15919625321401238319)
XLA Ops:
  0.6 1.5 %atoms_slab.1 = (s32[2,1536]{1,0:T(2,128)S(1)}, f32[2,8,64]{2,1,0:T(8,128)S(1)}, f32[2,64,64]{2,1,0:T(8,128)S(1)}, f32[2,64,64]{2,1,0:T(8,128)S(1)}, f32[2,64,38...) custom-call(f32[1,3,1,64]{3,2,1,0:T(1,128)} %bitcast.25, ...), custom_call_target="tpu_custom_call" | custom-call | bytes 732324 | tf_op jit(solution)/shard_map/atoms_slab/atoms_slab/pallas_call | solution.py:141
  2.1 10.4 %collective-permute-start = (f32[8,32]{1,0:T(8,128)S(1)}, f32[8,32]{1,0:T(8,128)S(1)}, u32[]{:S(2)}, u32[]{:S(2)}) collective-permute-start(f32[8,32]{1,0:T(8,128)S(1)} %get-tuple-element.100), channel_id=1, source_target_pairs={{16,32},{48,64},{80,96},{112,128},{144,160},{176,192},{208,224},{2... | collective-permute-start | bytes 3080 | tf_op jit(solution)/shard_map/atoms_slab/ppermute | solution.py:633
  12.5 1.9 %collective-permute-start.1 = (f32[8,32]{1,0:T(8,128)S(1)}, f32[8,32]{1,0:T(8,128)S(1)}, u32[]{:S(2)}, u32[]{:S(2)}) collective-permute-start(f32[8,32]{1,0:T(8,128)S(1)} %get-tuple-element.101), channel_id=1, source_target_pairs={{0,16},{16,0},{32,48},{48,32},{64,80},{80,64},{96,112},{112,96},{1... | collective-permute-start | bytes 3080 | tf_op jit(solution)/shard_map/atoms_slab/ppermute | solution.py:638
  14.4 1.1 %prepare.1 = (bf16[1536,256]{1,0:T(8,128)(2,1)S(1)}, bf16[256,1536]{1,0:T(8,128)(2,1)S(1)}, bf16[256,1536]{1,0:T(8,128)(2,1)S(1)}, f32[16,1536]{1,0:T(8,128)S(1)...) custom-call(s32[2,1536]{1,0:T(2,128)S(1)} %get-tuple-element.102.edg, ...), custom_call_target="tpu_custom_call" | custom-call | flops 1000000000 | bytes 730532 | tf_op jit(solution)/shard_map/prepare/prepare/pallas_call | solution.py:141
  15.6 0.2 atoms_plane.1
  15.7 7.2 %collective-permute-start.2 = (f32[8,64]{1,0:T(8,128)S(1)}, f32[8,64]{1,0:T(8,128)S(1)}, u32[]{:S(2)}, u32[]{:S(2)}) collective-permute-start(f32[8,64]{1,0:T(8,128)S(1)} %get-tuple-element.123), channel_id=1, source_target_pairs={{1,2},{3,4},{5,6},{7,8},{9,10},{11,12},{13,14},{15,0},{2,1},{4,3},... | collective-permute-start | bytes 6152 | tf_op jit(solution)/shard_map/atoms_plane/ppermute | solution.py:644
  23.0 5.8 %all-gather = f32[16,64]{1,0:T(8,128)S(1)} all-gather(f32[8,64]{1,0:T(8,128)S(1)} %get-tuple-element.124), channel_id=2, replica_groups={{0,1},{2,3},{4,5},{6,7},{8,9},{10,11},{12,13},{14,15},{16,17},{18,19},{..., dimensions={0}, use_global_device_ids=true | all-gather | bytes 6144 | tf_op jit(solution)/shard_map/atoms_plane/all_gather | solution.py:649
  28.8 2.8 %first_layer.1 = (f32[64,128]{1,0:T(8,128)S(1)}, f32[32,128]{1,0:T(8,128)S(1)}, f32[32,128]{1,0:T(8,128)S(1)}, f32[64,128]{1,0:T(8,128)S(1)}, f32[9,64,128]{2,1,...) custom-call(f32[8,64]{1,0:T(8,128)S(1)} %get-tuple-element.99.v_ref,, ...), custom_call_target="tpu_custom_call" | custom-call | bytes 2283520 | tf_op jit(solution)/shard_map/first_layer/first_layer/pallas_call | solution.py:141
  31.6 3.1 %collective-permute-start.3 = (f32[32,128]{1,0:T(8,128)S(1)}, f32[32,128]{1,0:T(8,128)S(1)}, u32[]{:S(2)}, u32[]{:S(2)}) collective-permute-start(f32[32,128]{1,0:T(8,128)S(1)} %get-tuple-element.151), channel_id=1, source_target_pairs={{16,32},{48,64},{80,96},{112,128},{144,160},{176,192},{208,224},{2... | collective-permute-start | bytes 49160 | tf_op jit(solution)/shard_map/features_slab/ppermute | solution.py:633
  34.8 1.9 %collective-permute-start.4 = (f32[32,128]{1,0:T(8,128)S(1)}, f32[32,128]{1,0:T(8,128)S(1)}, u32[]{:S(2)}, u32[]{:S(2)}) collective-permute-start(f32[32,128]{1,0:T(8,128)S(1)} %get-tuple-element.152), channel_id=1, source_target_pairs={{0,16},{16,0},{32,48},{48,32},{64,80},{80,64},{96,112},{112,96},{1... | collective-permute-start | bytes 49160 | tf_op jit(solution)/shard_map/features_slab/ppermute | solution.py:638
  36.7 2.6 %beside_features.1 = (f32[1536,384]{1,0:T(8,128)S(1)}, bf16[192,1536]{1,0:T(8,128)(2,1)S(1)}, bf16[192,1536]{1,0:T(8,128)(2,1)S(1)}, f32[16,64]{1,0:T(8,128)S(1)...) custom-call(f32[8,1536]{1,0:T(8,128)S(1)} %get-tuple-element.138.b_ref, f32[8,1536]{1,0:T(8,128)S(1)} %get-tuple-element.139.db_ref, ...), custom_call_target="tpu_custom_call" | custom-call | flops 1000000000 | bytes 2061824 | tf_op jit(solution)/shard_map/beside_features/pallas_call | solution.py:141
  39.3 0.2 middle.1
  39.6 2.9 %collective-permute-start.5 = (f32[64,128]{1,0:T(8,128)S(1)}, f32[64,128]{1,0:T(8,128)S(1)}, u32[]{:S(2)}, u32[]{:S(2)}) collective-permute-start(f32[64,128]{1,0:T(8,128)S(1)} %get-tuple-element.156), channel_id=1, source_target_pairs={{1,2},{3,4},{5,6},{7,8},{9,10},{11,12},{13,14},{15,0},{2,1},{4,3},... | collective-permute-start | bytes 98312 | tf_op jit(solution)/shard_map/features_plane/ppermute | solution.py:644
  42.5 6.7 %all-gather.1 = f32[128,128]{1,0:T(8,128)S(1)} all-gather(f32[64,128]{1,0:T(8,128)S(1)} %get-tuple-element.157), channel_id=3, replica_groups={{0,1},{2,3},{4,5},{6,7},{8,9},{10,11},{12,13},{14,15},{16,17},{18,19},{..., dimensions={0}, use_global_device_ids=true | all-gather | bytes 98304 | tf_op jit(solution)/shard_map/features_plane/all_gather | solution.py:649
  49.2 2.2 %second_layer.1 = (f32[16,64]{1,0:T(8,128)S(1)}, f32[16,64]{1,0:T(8,128)S(1)}, f32[128,128]{1,0:T(8,128)S(1)}, f32[64,128]{1,0:T(8,128)S(1)}, f32[64,128]{1,0:T(...) custom-call(f32[64,128]{1,0:T(8,128)S(1)} %get-tuple-element.150.f_ref, ...), custom_call_target="tpu_custom_call" | custom-call | bytes 7020544 | tf_op jit(solution)/shard_map/second_layer/second_layer/pallas_call | solution.py:141
  51.5 5.9 %collective-permute-start.6 = (f32[64,128]{1,0:T(8,128)S(1)}, f32[64,128]{1,0:T(8,128)S(1)}, u32[]{:S(2)}, u32[]{:S(2)}) collective-permute-start(f32[64,128]{1,0:T(8,128)S(1)} %get-tuple-element.166), channel_id=1, source_target_pairs={{1,2},{3,4},{5,6},{7,8},{9,10},{11,12},{13,14},{15,0},{2,1},{4,3},... | collective-permute-start | bytes 98312 | tf_op jit(solution)/shard_map/feature_grads_plane/ppermute | solution.py:644
  57.4 6.1 %all-gather.2 = f32[128,128]{1,0:T(8,128)S(1)} all-gather(f32[64,128]{1,0:T(8,128)S(1)} %get-tuple-element.167), channel_id=4, replica_groups={{0,1},{2,3},{4,5},{6,7},{8,9},{10,11},{12,13},{14,15},{16,17},{18,19},{..., dimensions={0}, use_global_device_ids=true | all-gather | bytes 98304 | tf_op jit(solution)/shard_map/feature_grads_plane/all_gather | solution.py:649
  63.5 0.2 back_middle.1
  63.7 2.0 %collective-permute-start.7 = (f32[32,128]{1,0:T(8,128)S(1)}, f32[32,128]{1,0:T(8,128)S(1)}, u32[]{:S(2)}, u32[]{:S(2)}) collective-permute-start(f32[32,128]{1,0:T(8,128)S(1)} %get-tuple-element.180), channel_id=1, source_target_pairs={{16,32},{48,64},{80,96},{112,128},{144,160},{176,192},{208,224},{2... | collective-permute-start | bytes 49160 | tf_op jit(solution)/shard_map/feature_grads_slab/ppermute | solution.py:633
  65.7 1.9 %collective-permute-start.8 = (f32[32,128]{1,0:T(8,128)S(1)}, f32[32,128]{1,0:T(8,128)S(1)}, u32[]{:S(2)}, u32[]{:S(2)}) collective-permute-start(f32[32,128]{1,0:T(8,128)S(1)} %get-tuple-element.181), channel_id=1, source_target_pairs={{0,16},{16,0},{32,48},{48,32},{64,80},{80,64},{96,112},{112,96},{1... | collective-permute-start | bytes 49160 | tf_op jit(solution)/shard_map/feature_grads_slab/ppermute | solution.py:638
  67.6 2.3 %beside_grads.1 = (f32[8,1536]{1,0:T(8,128)S(1)}, f32[1536,384]{1,0:T(8,128)S(1)}, f32[1,64]{1,0:T(1,128)S(1)}, f32[64,128]{1,0:T(8,128)S(1)}) custom-call(bf16[1536,512]{1,0:T(8,128)(2,1)S(1)} %get-tuple-element.148.turned_ref, bf16[192,1536]{1,0:T(8,128)(2,1)S(1)} %get-tuple-element.149.second_q_ref, bf16[2,192,384]{2,1,0:T(8,128)(2,1)S(1)} %get-tuple-element.133.w4_ref, ...), custom_call_target="tpu_custom_call" | custom-call | flops 1000000000 | bytes 6720512 | tf_op jit(solution)/shard_map/beside_grads/pallas_call | solution.py:141
  69.9 0.9 %collective-permute-done.7.rf_ref = f32[32,128]{1,0:T(8,128)S(1)} collective-permute-done((f32[32,128]{1,0:T(8,128)S(1)}, f32[32,128]{1,0:T(8,128)S(1)}, u32[]{:S(2)}, u32[]{:S(2)}) %collective-permute-start.7) | collective-permute-done | bytes 16416 | tf_op jit(solution)/shard_map/feature_grads_slab/ppermute | solution.py:633
  70.9 1.9 %late_forces.1 = (f32[8,64]{1,0:T(8,128)S(1)}, f32[8,32]{1,0:T(8,128)S(1)}, f32[8,32]{1,0:T(8,128)S(1)}, f32[8,64]{1,0:T(8,128)S(1)}, f32[8,64]{1,0:T(8,128)S(1)}) custom-call(f32[64,128]{1,0:T(8,128)S(1)} %get-tuple-element.179.own_ref, f32[32,128]{1,0:T(8,128)S(1)} %collective-permute-done.7.rf_ref, f32[32,128]{1,0:T(8,128)S(1)} %collective-permute-done.8.rn_ref, ...), custom_call_target="tpu_custom_call" | custom-call | bytes 8531968 | tf_op jit(solution)/shard_map/late_forces/late_forces/pallas_call | solution.py:141
  72.8 3.7 %collective-permute-start.9 = (f32[8,64]{1,0:T(8,128)S(1)}, f32[8,64]{1,0:T(8,128)S(1)}, u32[]{:S(2)}, u32[]{:S(2)}) collective-permute-start(f32[8,64]{1,0:T(8,128)S(1)} %get-tuple-element.191), channel_id=1, source_target_pairs={{1,2},{3,4},{5,6},{7,8},{9,10},{11,12},{13,14},{15,0},{2,1},{4,3},... | collective-permute-start | bytes 6152 | tf_op jit(solution)/shard_map/position_grads_plane/ppermute | solution.py:644
  76.5 5.8 %all-gather.3 = f32[16,64]{1,0:T(8,128)S(1)} all-gather(f32[8,64]{1,0:T(8,128)S(1)} %get-tuple-element.192), channel_id=5, replica_groups={{0,1},{2,3},{4,5},{6,7},{8,9},{10,11},{12,13},{14,15},{16,17},{18,19},{..., dimensions={0}, use_global_device_ids=true | all-gather | bytes 6144 | tf_op jit(solution)/shard_map/position_grads_plane/all_gather | solution.py:649
  82.3 0.2 collect_plane.1
  82.5 4.2 %collective-permute-start.10 = (f32[8,32]{1,0:T(8,128)S(1)}, f32[8,32]{1,0:T(8,128)S(1)}, u32[]{:S(2)}, u32[]{:S(2)}) collective-permute-start(f32[8,32]{1,0:T(8,128)S(1)} %get-tuple-element.194), channel_id=1, source_target_pairs={{16,32},{48,64},{80,96},{112,128},{144,160},{176,192},{208,224},{2... | collective-permute-start | bytes 3080 | tf_op jit(solution)/shard_map/position_grads_slab/ppermute | solution.py:633
  86.7 1.9 %collective-permute-start.11 = (f32[8,32]{1,0:T(8,128)S(1)}, f32[8,32]{1,0:T(8,128)S(1)}, u32[]{:S(2)}, u32[]{:S(2)}) collective-permute-start(f32[8,32]{1,0:T(8,128)S(1)} %get-tuple-element.195), channel_id=1, source_target_pairs={{0,16},{16,0},{32,48},{48,32},{64,80},{80,64},{96,112},{112,96},{1... | collective-permute-start | bytes 3080 | tf_op jit(solution)/shard_map/position_grads_slab/ppermute | solution.py:638
  88.6 0.5 copy.21
  89.1 0.4 collective-permute-done.10.rf_ref
  89.5 0.2 collective-permute-done.11.rn_ref
  89.9 0.6 copy.22
  (10 shorter events, 0.2 us)
Async XLA Ops:
  2.1 13.4 %collective-permute-start = (f32[8,32]{1,0:T(8,128)S(1)}, f32[8,32]{1,0:T(8,128)S(1)}, u32[]{:S(2)}, u32[]{:S(2)}) collective-permute-start(f32[8,32]{1,0:T(8,128)S(1)} %get-tuple-element.100), channel_id=1, source_target_pairs={{16,32},{48,64},{80,96},{112,128},{144,160},{176,192},{208,224},{2... | collective-permute-start | bytes 3080 | tf_op jit(solution)/shard_map/atoms_slab/ppermute | solution.py:633
  12.5 3.1 %collective-permute-start.1 = (f32[8,32]{1,0:T(8,128)S(1)}, f32[8,32]{1,0:T(8,128)S(1)}, u32[]{:S(2)}, u32[]{:S(2)}) collective-permute-start(f32[8,32]{1,0:T(8,128)S(1)} %get-tuple-element.101), channel_id=1, source_target_pairs={{0,16},{16,0},{32,48},{48,32},{64,80},{80,64},{96,112},{112,96},{1... | collective-permute-start | bytes 3080 | tf_op jit(solution)/shard_map/atoms_slab/ppermute | solution.py:638
  15.7 13.1 %collective-permute-start.2 = (f32[8,64]{1,0:T(8,128)S(1)}, f32[8,64]{1,0:T(8,128)S(1)}, u32[]{:S(2)}, u32[]{:S(2)}) collective-permute-start(f32[8,64]{1,0:T(8,128)S(1)} %get-tuple-element.123), channel_id=1, source_target_pairs={{1,2},{3,4},{5,6},{7,8},{9,10},{11,12},{13,14},{15,0},{2,1},{4,3},... | collective-permute-start | bytes 6152 | tf_op jit(solution)/shard_map/atoms_plane/ppermute | solution.py:644
  31.6 7.7 %collective-permute-start.3 = (f32[32,128]{1,0:T(8,128)S(1)}, f32[32,128]{1,0:T(8,128)S(1)}, u32[]{:S(2)}, u32[]{:S(2)}) collective-permute-start(f32[32,128]{1,0:T(8,128)S(1)} %get-tuple-element.151), channel_id=1, source_target_pairs={{16,32},{48,64},{80,96},{112,128},{144,160},{176,192},{208,224},{2... | collective-permute-start | bytes 49160 | tf_op jit(solution)/shard_map/features_slab/ppermute | solution.py:633
  34.8 4.6 %collective-permute-start.4 = (f32[32,128]{1,0:T(8,128)S(1)}, f32[32,128]{1,0:T(8,128)S(1)}, u32[]{:S(2)}, u32[]{:S(2)}) collective-permute-start(f32[32,128]{1,0:T(8,128)S(1)} %get-tuple-element.152), channel_id=1, source_target_pairs={{0,16},{16,0},{32,48},{48,32},{64,80},{80,64},{96,112},{112,96},{1... | collective-permute-start | bytes 49160 | tf_op jit(solution)/shard_map/features_slab/ppermute | solution.py:638
  39.6 9.7 %collective-permute-start.5 = (f32[64,128]{1,0:T(8,128)S(1)}, f32[64,128]{1,0:T(8,128)S(1)}, u32[]{:S(2)}, u32[]{:S(2)}) collective-permute-start(f32[64,128]{1,0:T(8,128)S(1)} %get-tuple-element.156), channel_id=1, source_target_pairs={{1,2},{3,4},{5,6},{7,8},{9,10},{11,12},{13,14},{15,0},{2,1},{4,3},... | collective-permute-start | bytes 98312 | tf_op jit(solution)/shard_map/features_plane/ppermute | solution.py:644
  51.5 12.0 %collective-permute-start.6 = (f32[64,128]{1,0:T(8,128)S(1)}, f32[64,128]{1,0:T(8,128)S(1)}, u32[]{:S(2)}, u32[]{:S(2)}) collective-permute-start(f32[64,128]{1,0:T(8,128)S(1)} %get-tuple-element.166), channel_id=1, source_target_pairs={{1,2},{3,4},{5,6},{7,8},{9,10},{11,12},{13,14},{15,0},{2,1},{4,3},... | collective-permute-start | bytes 98312 | tf_op jit(solution)/shard_map/feature_grads_plane/ppermute | solution.py:644
  63.7 7.2 %collective-permute-start.7 = (f32[32,128]{1,0:T(8,128)S(1)}, f32[32,128]{1,0:T(8,128)S(1)}, u32[]{:S(2)}, u32[]{:S(2)}) collective-permute-start(f32[32,128]{1,0:T(8,128)S(1)} %get-tuple-element.180), channel_id=1, source_target_pairs={{16,32},{48,64},{80,96},{112,128},{144,160},{176,192},{208,224},{2... | collective-permute-start | bytes 49160 | tf_op jit(solution)/shard_map/feature_grads_slab/ppermute | solution.py:633
  65.7 5.2 %collective-permute-start.8 = (f32[32,128]{1,0:T(8,128)S(1)}, f32[32,128]{1,0:T(8,128)S(1)}, u32[]{:S(2)}, u32[]{:S(2)}) collective-permute-start(f32[32,128]{1,0:T(8,128)S(1)} %get-tuple-element.181), channel_id=1, source_target_pairs={{0,16},{16,0},{32,48},{48,32},{64,80},{80,64},{96,112},{112,96},{1... | collective-permute-start | bytes 49160 | tf_op jit(solution)/shard_map/feature_grads_slab/ppermute | solution.py:638
  72.8 9.5 %collective-permute-start.9 = (f32[8,64]{1,0:T(8,128)S(1)}, f32[8,64]{1,0:T(8,128)S(1)}, u32[]{:S(2)}, u32[]{:S(2)}) collective-permute-start(f32[8,64]{1,0:T(8,128)S(1)} %get-tuple-element.191), channel_id=1, source_target_pairs={{1,2},{3,4},{5,6},{7,8},{9,10},{11,12},{13,14},{15,0},{2,1},{4,3},... | collective-permute-start | bytes 6152 | tf_op jit(solution)/shard_map/position_grads_plane/ppermute | solution.py:644
  82.5 7.0 %collective-permute-start.10 = (f32[8,32]{1,0:T(8,128)S(1)}, f32[8,32]{1,0:T(8,128)S(1)}, u32[]{:S(2)}, u32[]{:S(2)}) collective-permute-start(f32[8,32]{1,0:T(8,128)S(1)} %get-tuple-element.194), channel_id=1, source_target_pairs={{16,32},{48,64},{80,96},{112,128},{144,160},{176,192},{208,224},{2... | collective-permute-start | bytes 3080 | tf_op jit(solution)/shard_map/position_grads_slab/ppermute | solution.py:633
  86.7 3.1 %collective-permute-start.11 = (f32[8,32]{1,0:T(8,128)S(1)}, f32[8,32]{1,0:T(8,128)S(1)}, u32[]{:S(2)}, u32[]{:S(2)}) collective-permute-start(f32[8,32]{1,0:T(8,128)S(1)} %get-tuple-element.195), channel_id=1, source_target_pairs={{0,16},{16,0},{32,48},{48,32},{64,80},{80,64},{96,112},{112,96},{1... | collective-permute-start | bytes 3080 | tf_op jit(solution)/shard_map/position_grads_slab/ppermute | solution.py:638
